TPU v7x, 32 devices: a whole 2x2x4 slice. The times are simulated.
32 devices in a mesh: group: 4 (over x, core), resp: 8 (over z, y).
Axes of the slice: x: 2, y: 2, z: 4, core: 2. Of those that a mesh axis runs over, the one named last changes fastest.
Arguments:
- prompt_in: bfloat16 [4, 1024, 10240], P('group', 'resp'), may hold values from -6 to 6
- prompt_dt: bfloat16 [4, 1024, 128], P('group', 'resp'), may hold values from -3 to 9
- doc_starts: int32 [4, 4], P('group'), may hold values from 0 to 127, as said below
- resp_in: bfloat16 [4, 8, 256, 10240], P('group', 'resp'), may hold values from -6 to 6
- resp_dt: bfloat16 [4, 8, 256, 128], P('group', 'resp'), may hold values from -3 to 9
- resp_len: int32 [4, 8], P('group', 'resp'), may hold values from 64 to 256, as said below
- upstream: bfloat16 [4, 8, 256, 8192], P('group', 'resp'), may hold values from -6 to 6
- reward: float32 [4, 8], P('group', 'resp'), may hold values from -4 to 4
- conv_w: float32 [4, 10240], replicated, may hold values from -3 to 3
- conv_b: float32 [10240], replicated, may hold values from -0.5 to 0.5
- head_params: float32 [3, 128], replicated, may hold values from -5.5 to 1.5
Outputs:
- grad_conv_w: float32 [4, 10240], replicated
- grad_conv_b: float32 [10240], replicated
- grad_heads: float32 [3, 128], replicated
Inputs may be any that keep to these rules, and one draw needn't show every extreme that they name: doc_starts begins with 0 and rises strictly; all documents but the last start within the first 128 positions. `resp_len`: each group has a response of 256 tokens.
All inputs are finite; a program needn't handle non-finite values.
Results may differ from a plain program's by a relative error of at most 0.01.
Values may be sent and summed in bfloat16 or wider, within the bound.
No kernel may reach another device: no remote copies, remote signals or barrier semaphores. Data moves between devices by JAX's collectives and lax.ppermute only.
A program may use at most 448 MiB of HBM per device.

v0:
```python
import functools

import jax
import jax.numpy as jnp
from jax import lax
from jax.experimental import pallas as pl
from jax.experimental.pallas import tpu as pltpu
from jax.sharding import PartitionSpec as P

H = 128
PS = 64
N = 256
G = 4
K = 4
HG = H // G
XC = H * PS
GX = HG * PS
LANES = 128
PAD = 8
VMEM_MIB = 63

f32 = jnp.float32
bf16 = jnp.bfloat16

NN = (((1,), (0,)), ((), ()))
NT = (((1,), (1,)), ((), ()))


def dot(a, b, dims=NN, precision=None):
    return lax.dot_general(a, b, dims, precision=precision, preferred_element_type=f32)


def halves(v):
    hi = v.astype(bf16)
    return hi, (v - hi.astype(f32)).astype(bf16)


def indicator(first, width):
    row = lax.broadcasted_iota(jnp.int32, (LANES, width), 0)
    head = lax.shift_right_logical(lax.broadcasted_iota(jnp.int32, (LANES, width), 1), 6)
    return jnp.where(row - first == head, 1.0, 0.0).astype(bf16)


def expand(v, ind):
    hi, lo = halves(v)
    return dot(hi, ind) + dot(lo, ind)


def head_sums(z_hi, z_lo, ind):
    return dot(z_hi, ind, NT) + dot(z_lo, ind, NT)


def triangle(n, keep):
    i = lax.broadcasted_iota(jnp.int32, (n, n), 0)
    j = lax.broadcasted_iota(jnp.int32, (n, n), 1)
    return jnp.where(keep(i, j), 1.0, 0.0).astype(f32)


def tri_sum(tri, v):
    return dot(tri, v, precision=lax.Precision.HIGHEST)


def softplus(z):
    return jnp.maximum(z, 0.0) + jnp.log1p(jnp.exp(-jnp.abs(z)))


def sigmoid(z):
    return 0.5 * jnp.tanh(0.5 * z) + 0.5


def taps_of(ext, lanes, row, rows):
    return [ext[pl.ds(PAD - K + 1 + k + row, rows), lanes] for k in range(K)]


def conv_pre(taps, wb, masks=None):
    total = wb[K : K + 1] + wb[K - 1 : K] * taps[K - 1]
    for k in range(K - 1):
        term = wb[k : k + 1] * taps[k]
        if masks is not None:
            term = term * masks[k]
        total = total + term
    return total


def act_and_slope(pre):
    sig = sigmoid(pre)
    act = pre * sig
    return act, sig + act * (1.0 - sig)


def fold8(v):
    return jnp.sum(v.reshape(v.shape[0] // 8, 8, v.shape[1]), axis=0)


def as_rows(parts):
    row = lax.broadcasted_iota(jnp.int32, (PAD, LANES), 0)
    total = jnp.zeros((PAD, LANES), f32)
    for k, part in enumerate(parts):
        total = total + jnp.where(row == k, jnp.sum(part, axis=0, keepdims=True), 0.0)
    return total


def lane_loop(width, body, step=LANES):
    def one(i, _):
        body(pl.ds(pl.multiple_of(i * step, step), step))
        return 0

    lax.fori_loop(0, width // step, one, 0)


RC = 64


def conv_forward(u, tail, wb, ext, act, slope, rows, width):
    def body(lanes):
        ext[0:PAD, lanes] = tail[:, lanes]
        ext[PAD : PAD + rows, lanes] = u[:, lanes].astype(f32)
        w = wb[:, lanes]
        for r in range(0, rows, RC):
            a, s = act_and_slope(conv_pre(taps_of(ext, lanes, r, RC), w))
            act[r : r + RC, lanes] = a.astype(bf16)
            if slope is not None:
                slope[r : r + RC, lanes] = s

    lane_loop(width, body)


def conv_backward(ext, slope, lanes, cotangent, grad, rows):
    sums = [jnp.zeros((8, LANES), f32) for _ in range(K + 1)]
    for r in range(0, rows, RC):
        d = cotangent(r) * slope[r : r + RC, lanes]
        taps = taps_of(ext, lanes, r, RC)
        for k in range(K):
            sums[k] = sums[k] + fold8(d * taps[k])
        sums[K] = sums[K] + fold8(d)
    grad[:, lanes] = as_rows(sums)


def steps_kernel(len_ref, dt, hp, step, cum, cum_t, decay_in):
    rows = dt.shape[0]
    s = softplus(dt[...].astype(f32) + hp[1:2])
    logd = -jnp.exp(hp[0:1]) * s
    c = tri_sum(triangle(rows, lambda i, j: i >= j), logd)
    step[...] = s
    cum[...] = c
    cum_t[...] = c.T
    t = lax.broadcasted_iota(jnp.int32, c.shape, 0)
    decay_in[...] = jnp.where(t < len_ref[0, 0], jnp.exp(c), 0.0)


def resp_state_kernel(adv, u_c, tail_c, wb_c, dy, decay_in, state, weighted, c_out, ext):
    g = pl.program_id(0)
    rows, width = dy.shape
    conv_forward(u_c, tail_c, wb_c, ext, c_out, None, rows, N)
    c_t = c_out[...].astype(f32).T.astype(bf16)
    a = (dy[...].astype(f32) * expand(decay_in[...], indicator(g * HG, width))).astype(bf16)
    weighted[...] = a
    state[0] = (dot(c_t, a) * adv[0, 0]).astype(bf16)


def resp_mid_kernel(
    g, len_ref, u_x, u_b, tail_x, tail_b, wb_x, wb_b, c_act, dy, step, cum, cum4, cum_t4, skip,
    earlier_out, *refs,
):
    if g:
        sums_in, refs = refs[3], refs[4:]
    (
    grad_x, grad_b, dc, sums_out,
    ext, ext_b, x_s, xs_s, b_s, dym, slope, slope_b, step_e, y_s, t_s,
    a1, bm, sw_e, u_off, y_off, z_hi, z_lo, d_skip,
    ) = refs
    rows = u_x.shape[0]
    half = rows // 2
    conv_forward(u_x, tail_x, wb_x, ext, x_s, slope, rows, GX)
    conv_forward(u_b, tail_b, wb_b, ext_b, b_s, slope_b, rows, N)
    ind = indicator(g * HG, GX)
    step_e[...] = expand(step[...], ind)
    cum_v = cum[...]
    mid = cum_v[half - 1 : half]
    sw_e[...] = expand(jnp.exp(mid - cum_v[:half]) * step[:half], ind)
    y_off[...] = expand(jnp.exp(cum_v[half:] - mid), ind)
    live = jnp.where(lax.broadcasted_iota(jnp.int32, (rows, LANES), 0) < len_ref[0, 0], 1.0, 0.0)

    def prepare(lanes):
        d = dy[:, lanes].astype(f32) * live
        dym[:, lanes] = d.astype(bf16)
        x = x_s[:, lanes].astype(f32)
        xs_s[:, lanes] = (x * step_e[:, lanes]).astype(bf16)
        bm[:, lanes] = (x[:half] * sw_e[:, lanes]).astype(bf16)
        a1[:, lanes] = (d[half:] * y_off[:, lanes]).astype(bf16)

    lane_loop(GX, prepare)

    c_v, b_v = c_act[...], b_s[...]
    c0, c1, b0, b1 = c_v[:half], c_v[half:], b_v[:half], b_v[half:]
    i = lax.broadcasted_iota(jnp.int32, (half, half), 0)
    j = lax.broadcasted_iota(jnp.int32, (half, half), 1)
    lane = lax.broadcasted_iota(jnp.int32, (half, LANES), 1)
    first = jnp.where(lane < PS, 1.0, 0.0).astype(bf16)
    second = jnp.where(lane >= PS, 1.0, 0.0).astype(bf16)

    y_off[...] = dot(dot(c1, b0, NT).astype(bf16), bm[...])
    u_off[...] = dot(dot(b0, c1, NT).astype(bf16), a1[...])
    d10 = dot(a1[...], bm[...], NT)

    d_diag = []
    for q, (c_q, b_q) in enumerate(((c0, b0), (c1, b1))):
        r = slice(q * half, (q + 1) * half)
        lower = jnp.where(i >= j, dot(c_q, b_q, NT), 0.0)
        upper = jnp.where(j >= i, dot(b_q, c_q, NT), 0.0)
        d_sc = jnp.zeros((half, half), f32)
        for p in range(HG // 2):
            lanes = slice(p * LANES, (p + 1) * LANES)
            xs_p, dy_p = xs_s[r, lanes], dym[r, lanes]
            xb = jnp.concatenate([xs_p * first, xs_p * second], axis=0)
            dyb = jnp.concatenate([dy_p * first, dy_p * second], axis=0)
            d_m = dot(dy_p, xb, NT)
            mats, mats_t = [], []
            for a in range(2):
                h = 2 * p + a
                gap = jnp.exp(-jnp.abs(cum4[0, r, h : h + 1] - cum_t4[0, h : h + 1, r]))
                d_sc = d_sc + d_m[:, a * half : (a + 1) * half] * gap
                mats.append((gap * lower).astype(bf16))
                mats_t.append((gap * upper).astype(bf16))
            y_s[r, lanes] = dot(jnp.concatenate(mats, axis=1), xb)
            t_s[r, lanes] = dot(jnp.concatenate(mats_t, axis=1), dyb)
        d_diag.append(jnp.where(i >= j, d_sc, 0.0))

    d00, d11 = d_diag
    dc[:half] = dot(d00.astype(bf16), b0)
    dc[half:] = dot(d11.astype(bf16), b1) + dot(d10.astype(bf16), b0)
    db0 = dot(d00.T.astype(bf16), c0) + dot(d10.T.astype(bf16), c1)
    db1 = dot(d11.T.astype(bf16), c1)
    db = jnp.concatenate([db0, db1], axis=0)
    for k in range(N // LANES):
        lanes = slice(k * LANES, (k + 1) * LANES)
        conv_backward(ext_b, slope_b, lanes, lambda r: db[r : r + RC, lanes], grad_b, rows)

    def put(z, r, lanes):
        hi, lo = halves(z)
        z_hi[r : r + RC, lanes] = hi
        z_lo[r : r + RC, lanes] = lo

    def row_products(lanes):
        for r in range(0, rows, RC):
            z = dym[r : r + RC, lanes].astype(f32) * y_s[r : r + RC, lanes]
            if r >= half:
                o = r - half
                z = z + a1[o : o + RC, lanes].astype(f32) * y_off[o : o + RC, lanes]
            put(z, r, lanes)

    lane_loop(GX, row_products)
    row_sum = head_sums(z_hi[...], z_lo[...], ind)

    def finish(lanes):
        d_skips = jnp.zeros((8, LANES), f32)
        for r in range(0, rows, RC):
            t = t_s[r : r + RC, lanes]
            z = xs_s[r : r + RC, lanes].astype(f32) * t
            if r < half:
                z = z + bm[r : r + RC, lanes].astype(f32) * u_off[r : r + RC, lanes]
            put(z, r, lanes)
            d_skips = d_skips + fold8(
                dym[r : r + RC, lanes].astype(f32) * x_s[r : r + RC, lanes].astype(f32)
            )

        def cotangent(r):
            d = step_e[r : r + RC, lanes] * t_s[r : r + RC, lanes]
            d = d + skip[:, lanes] * dym[r : r + RC, lanes].astype(f32)
            if r < half:
                d = d + sw_e[r : r + RC, lanes] * u_off[r : r + RC, lanes]
            return d

        conv_backward(ext, slope, lanes, cotangent, grad_x, rows)
        d_skip[:, lanes] = d_skips

    lane_loop(GX, finish)
    col_sum = head_sums(z_hi[...], z_lo[...], ind)

    skip_sum = head_sums(*halves(d_skip[...]), ind)
    for at, part in ((0, row_sum), (rows, col_sum), (2 * rows, skip_sum)):
        span = slice(at, at + part.shape[0])
        sums_out[span] = sums_in[span] + part if g else part


X_TILES = XC // LANES
B_TILES = G * N // LANES
C_TILES = X_TILES + 2 * B_TILES
HEAD_TILE = (K + 1) * C_TILES // PAD


def tile(k):
    return slice(k * LANES, (k + 1) * LANES)


def resp_end_kernel(
    place, scale, u_c, tail_c, wb_c, c_act, weighted, start, dc, sums, step, dt, hp,
    grad_x, grad_b, p_grad, p_heads,
    packed, ext, c_s, slope, total, grad_c, tiles,
):
    g = pl.program_id(0)
    rows, width = weighted.shape
    conv_forward(u_c, tail_c, wb_c, ext, c_s, slope, rows, N)

    @pl.when(g == 0)
    def _():
        total[...] = sums[0:rows] - sums[rows : 2 * rows]

    a = weighted[...]
    z_hi, z_lo = halves(a.astype(f32) * dot(c_act[...], start[0]))
    total[...] += head_sums(z_hi, z_lo, indicator(g * HG, width))
    d = dc[...] + dot(a, start[0], NT)
    for k in range(N // LANES):
        conv_backward(ext, slope, tile(k), lambda r: d[r : r + RC, tile(k)], grad_c, rows)
        tiles[X_TILES + B_TILES + g * (N // LANES) + k] = grad_c[:, tile(k)] * scale[0, 0]

    @pl.when(g == pl.num_programs(0) - 1)
    def _():
        d_log = tri_sum(triangle(rows, lambda i, j: j >= i), total[...])
        rate = -jnp.exp(hp[0:1])
        s = step[...]
        d_step = sums[rows : 2 * rows] / s + rate * d_log
        sig = sigmoid(dt[...].astype(f32) + hp[1:2])
        heads = as_rows([d_log * rate * s, d_step * sig, sums[2 * rows :]])
        for k in range(X_TILES):
            tiles[k] = grad_x[:, tile(k)] * scale[0, 0]
        for k in range(B_TILES):
            tiles[X_TILES + k] = grad_b[:, tile(k)] * scale[0, 0]
        for k in range(width // LANES):
            tiles[place[0, 0] * (width // LANES) + k] += p_grad[:, tile(k)]
        for k in range(N // LANES):
            tiles[X_TILES + place[0, 0] * (N // LANES) + k] += p_grad[:, tile(width // LANES + k)]
        for k in range(K + 1):
            for at in range(C_TILES):
                row = k * C_TILES + at
                packed[row // PAD, row % PAD : row % PAD + 1] = tiles[at, k : k + 1]
        packed[HEAD_TILE] = heads * scale[0, 0] + p_heads[...]
        for k in range(HEAD_TILE + 1, packed.shape[0]):
            packed[k] = jnp.zeros((PAD, LANES), f32)


def unpack_kernel(packed, conv_w, conv_b, heads):
    for k in range(K + 1):
        for at in range(C_TILES):
            row = k * C_TILES + at
            part = packed[row // PAD, row % PAD : row % PAD + 1]
            if k < K:
                conv_w[k : k + 1, tile(at)] = part
            else:
                conv_b[:, tile(at)] = part
    heads[...] = packed[HEAD_TILE, 0:3]


RB = 256


def prompt_conv(v, masks, wb, ext, act, slope, row, width):
    def body(lanes):
        ext[PAD : PAD + RB, lanes] = v[pl.ds(row, RB), lanes].astype(f32)
        w = wb[:, lanes]
        for r in range(0, RB, RC):
            m = [masks[pl.ds(row + r, RC), k : k + 1] for k in range(K - 1)]
            a, s = act_and_slope(conv_pre(taps_of(ext, lanes, r, RC), w, m))
            act[r : r + RC, lanes] = a.astype(bf16)
            if slope is not None:
                slope[r : r + RC, lanes] = s

    lane_loop(width, body)


def rows_before(v, halo, row, width):
    if row:
        return v[row - 16 : row, :width].astype(f32)[16 - PAD :]
    return halo[...]


def prompt_state_kernel(
    place, v, halo, dt_all, masks, wb, hp, start, weight, step, beyond, ext, act, acc
):
    rows = v.shape[0]
    width = start.shape[1]
    first = place[0, 1]
    ind = indicator(place[0, 0] * HG, width)
    later = triangle(RB, lambda i, j: j > i)
    rate = -jnp.exp(hp[0:1])
    ahead = jnp.zeros((1, LANES), f32)
    slopes = jnp.zeros((1, LANES), f32)
    for row in range(0, dt_all.shape[0], RB):
        s = softplus(dt_all[row : row + RB].astype(f32) + hp[1:2])
        position = row + lax.broadcasted_iota(jnp.int32, s.shape, 0)
        past = position >= first + rows
        sig = sigmoid(dt_all[row : row + RB].astype(f32) + hp[1:2])
        ahead = ahead + rate * jnp.sum(jnp.where(past, s, 0.0), axis=0, keepdims=True)
        slopes = slopes + rate * jnp.sum(jnp.where(past, sig, 0.0), axis=0, keepdims=True)
    beyond[...] = jnp.zeros_like(beyond)
    beyond[0:1] = ahead
    beyond[1:2] = slopes
    acc[...] = jnp.zeros_like(acc)
    for row in range(rows - RB, -1, -RB):
        at = pl.ds(pl.multiple_of(first + row, RB), RB)
        s = softplus(dt_all[at, :].astype(f32) + hp[1:2])
        logd = rate * s
        after = tri_sum(later, logd) + ahead
        ahead = ahead + jnp.sum(logd, axis=0, keepdims=True)
        w = masks[row : row + RB, K - 1 : K] * jnp.exp(after) * s
        step[row : row + RB] = s
        weight[row : row + RB] = w
        ext[0:PAD] = rows_before(v, halo, row, width + N)
        prompt_conv(v, masks, wb, ext, act, None, row, width + N)
        wx = (act[:, :width].astype(f32) * expand(w, ind)).astype(bf16)
        acc[...] += dot(act[:, width:].astype(f32).T.astype(bf16), wx)
    start[...] = acc[...].astype(bf16)


def prompt_grad_kernel(
    count, place, v, halo, dt_mine, masks, wb, hp, weight, step, beyond, *refs
):
    states = refs[:count]
    grad, grad_h, ext, act, slope, g_s, d_s, sums = refs[count:]
    rows = v.shape[0]
    width = g_s.shape[1]
    ind = indicator(place[0, 0] * HG, width)
    earlier = triangle(RB, lambda i, j: j < i)
    total = states[0][...].astype(f32)
    for k in range(1, count):
        total = total + states[k][...].astype(f32)
    g_s[...] = total.astype(bf16)
    behind = jnp.zeros((1, LANES), f32)
    rate = -jnp.exp(hp[0:1])
    d_rate = jnp.zeros((1, LANES), f32)
    d_bias = jnp.zeros((1, LANES), f32)
    sums[...] = jnp.zeros_like(sums)
    for row in range(0, rows, RB):
        ext[0:PAD] = rows_before(v, halo, row, width + N)
        prompt_conv(v, masks, wb, ext, act, slope, row, width + N)
        w_e = expand(weight[row : row + RB], ind)
        t = dot(act[:, width:], g_s[...])
        wx = (act[:, :width].astype(f32) * w_e).astype(bf16)
        d_s[:, :width] = t * w_e
        d_s[:, width:] = dot(wx, g_s[...], NT)
        z_hi, z_lo = halves(wx.astype(f32) * t)
        q = head_sums(z_hi, z_lo, ind)
        d_log = tri_sum(earlier, q) + behind
        behind = behind + jnp.sum(q, axis=0, keepdims=True)
        s = step[row : row + RB]
        d_step = q / s + rate * d_log
        sig = sigmoid(dt_mine[row : row + RB].astype(f32) + hp[1:2])
        d_rate = d_rate + jnp.sum(d_log * rate * s, axis=0, keepdims=True)
        d_bias = d_bias + jnp.sum(d_step * sig, axis=0, keepdims=True)

        def back(lanes):
            acc = [jnp.zeros((8, LANES), f32) for _ in range(K + 1)]
            for r in range(0, RB, RC):
                d = d_s[r : r + RC, lanes] * slope[r : r + RC, lanes]
                taps = taps_of(ext, lanes, r, RC)
                for k in range(K):
                    part = d * taps[k]
                    if k < K - 1:
                        part = part * masks[pl.ds(row + r, RC), k : k + 1]
                    acc[k] = acc[k] + fold8(part)
                acc[K] = acc[K] + fold8(d)
            for k in range(K + 1):
                sums[k : k + 1, lanes] += jnp.sum(acc[k], axis=0, keepdims=True)

        lane_loop(width + N, back)
    grad[...] = sums[...]
    grad_h[...] = jnp.zeros_like(grad_h)
    grad_h[0:1] = d_rate + behind * beyond[0:1]
    grad_h[1:2] = d_bias + behind * beyond[1:2]


def add_kernel(count, grads, *refs):
    starts, (grad_sum, start) = refs[:count], refs[count + 1 :]
    grad_sum[...] = jnp.sum(grads[...].astype(f32), axis=0).astype(bf16)
    total = starts[0][...].astype(f32)
    for k in range(1, count):
        total = total + starts[k][...].astype(f32)
    total = total.astype(bf16)
    for k in range(start.shape[0]):
        start[k] = total


def params(*semantics):
    return pltpu.CompilerParams(
        vmem_limit_bytes=VMEM_MIB * 2**20, dimension_semantics=semantics or None
    )


SMEM = pl.BlockSpec(memory_space=pltpu.SMEM)


def whole(shape):
    return pl.BlockSpec(shape, lambda *_: (0,) * len(shape))


def sds(shape, dtype):
    return jax.ShapeDtypeStruct(shape, dtype)


def response_steps(length, dt, hp):
    rows = dt.shape[0]
    square = sds((rows, H), f32)
    return pl.pallas_call(
        steps_kernel,
        out_shape=(square, square, sds((H, rows), f32), square),
        in_specs=[SMEM, pl.BlockSpec(), pl.BlockSpec()],
        compiler_params=params(),
        name="resp_steps",
    )(length, dt, hp)


def response_state(scale, u, tail, wb, dy, decay_in):
    rows = u.shape[0]
    c_at = lambda g: (0, XC // N + G + g)
    g_at = lambda g: (0, g)
    return pl.pallas_call(
        resp_state_kernel,
        grid=(G,),
        in_specs=[
            SMEM,
            pl.BlockSpec((rows, N), c_at),
            pl.BlockSpec((PAD, N), c_at),
            pl.BlockSpec((PAD, N), c_at),
            pl.BlockSpec((rows, GX), g_at),
            whole((rows, H)),
        ],
        out_specs=[
            pl.BlockSpec((1, N, GX), lambda g: (g, 0, 0)),
            pl.BlockSpec((rows, GX), g_at),
            pl.BlockSpec((rows, N), g_at),
        ],
        out_shape=(sds((G, N, GX), bf16), sds((rows, XC), bf16), sds((rows, G * N), bf16)),
        scratch_shapes=[pltpu.VMEM((PAD + rows, N), f32)],
        compiler_params=params("arbitrary"),
        cost_estimate=pl.CostEstimate(
            flops=2 * rows * N * XC, bytes_accessed=14 * 2**20, transcendentals=rows * G * N
        ),
        name="resp_state",
    )(scale, u, tail, wb, dy, decay_in)


def response_mid(
    g, length, u, tail, wb, c_act, dy, step, cum, cum4, cum_t4, skip, earlier_out, so_far
):
    rows = u.shape[0]
    half = rows // 2
    x_at = lambda i: (0, g)
    b_at = lambda i: (0, XC // N + g)
    sums = (2 * rows + PAD, H)
    v = pltpu.VMEM
    anywhere = pl.BlockSpec(memory_space=pl.ANY)
    return pl.pallas_call(
        functools.partial(resp_mid_kernel, g),
        grid=(1,),
        in_specs=[
            SMEM,
            pl.BlockSpec((rows, GX), x_at),
            pl.BlockSpec((rows, N), b_at),
            pl.BlockSpec((PAD, GX), x_at),
            pl.BlockSpec((PAD, N), b_at),
            pl.BlockSpec((PAD, GX), x_at),
            pl.BlockSpec((PAD, N), b_at),
            pl.BlockSpec((rows, N), x_at),
            pl.BlockSpec((rows, GX), x_at),
            whole((rows, H)),
            whole((rows, H)),
            pl.BlockSpec((1, rows, HG), lambda i: (g, 0, 0)),
            pl.BlockSpec((1, HG, rows), lambda i: (g, 0, 0)),
            pl.BlockSpec((1, GX), x_at),
            anywhere,
        ]
        + ([anywhere] * 3 + [whole(sums)] if so_far else []),
        out_specs=[
            pl.BlockSpec((PAD, GX), x_at),
            pl.BlockSpec((PAD, N), x_at),
            pl.BlockSpec((rows, N), x_at),
            whole(sums),
        ],
        out_shape=(
            sds((PAD, XC), f32),
            sds((PAD, G * N), f32),
            sds((rows, G * N), f32),
            sds(sums, f32),
        ),
        input_output_aliases={15 + k: k for k in range(3)} if so_far else {},
        scratch_shapes=[
            v((PAD + rows, GX), f32),
            v((PAD + rows, N), f32),
            v((rows, GX), bf16),
            v((rows, GX), bf16),
            v((rows, N), bf16),
            v((rows, GX), bf16),
            v((rows, GX), f32),
            v((rows, N), f32),
            v((rows, GX), f32),
            v((rows, GX), f32),
            v((rows, GX), f32),
            v((half, GX), bf16),
            v((half, GX), bf16),
            v((half, GX), f32),
            v((half, GX), f32),
            v((half, GX), f32),
            v((rows, GX), bf16),
            v((rows, GX), bf16),
            v((PAD, GX), f32),
        ],
        compiler_params=params("arbitrary"),
        cost_estimate=pl.CostEstimate(
            flops=8 * 2**30, bytes_accessed=3 * 2**20, transcendentals=rows * half * HG
        ),
        name="resp_mid",
    )(
        length, u, u, tail, tail, wb, wb, c_act, dy, step, cum, cum4, cum_t4, skip, earlier_out,
        *so_far,
    )


def response_end(
    tiles, place, scale, u, tail, wb, c_act, weighted, start, dc, sums, step, dt, hp, grads
):
    rows = u.shape[0]
    c_at = lambda g: (0, XC // N + G + g)
    g_at = lambda g: (0, g)
    v = pltpu.VMEM
    return pl.pallas_call(
        resp_end_kernel,
        grid=(G,),
        in_specs=[
            SMEM,
            SMEM,
            pl.BlockSpec((rows, N), c_at),
            pl.BlockSpec((PAD, N), c_at),
            pl.BlockSpec((PAD, N), c_at),
            pl.BlockSpec((rows, N), g_at),
            pl.BlockSpec((rows, GX), g_at),
            pl.BlockSpec((1, N, GX), lambda g: (g, 0, 0)),
            pl.BlockSpec((rows, N), g_at),
        ]
        + [whole(a.shape) for a in (sums, step, dt, hp, *grads)],
        out_specs=whole((tiles, PAD, LANES)),
        out_shape=sds((tiles, PAD, LANES), f32),
        scratch_shapes=[
            v((PAD + rows, N), f32),
            v((rows, N), bf16),
            v((rows, N), f32),
            v((rows, H), f32),
            v((PAD, N), f32),
            v((C_TILES, PAD, LANES), f32),
        ],
        compiler_params=params("arbitrary"),
        cost_estimate=pl.CostEstimate(
            flops=4 * rows * N * XC, bytes_accessed=12 * 2**20, transcendentals=rows * G * N
        ),
        name="resp_end",
    )(place, scale, u, tail, wb, c_act, weighted, start, dc, sums, step, dt, hp, *grads)


def unpack(packed):
    width = C_TILES * LANES
    return pl.pallas_call(
        unpack_kernel,
        out_shape=(sds((K, width), f32), sds((1, width), f32), sds((3, H), f32)),
        compiler_params=params(),
        name="unpack",
    )(packed)


def add_states(grads, starts, earlier_out):
    copies, rows, width = grads.shape
    part = rows // 4
    one = pl.BlockSpec((part, width), lambda i: (i, 0))
    many = pl.BlockSpec((copies, part, width), lambda i: (0, i, 0))
    return pl.pallas_call(
        functools.partial(add_kernel, len(starts)),
        grid=(4,),
        in_specs=[many] + [one] * len(starts) + [pl.BlockSpec(memory_space=pl.ANY)],
        out_specs=[one, many],
        out_shape=(sds((rows, width), bf16), sds(grads.shape, bf16)),
        compiler_params=params("arbitrary"),
        cost_estimate=pl.CostEstimate(
            flops=8 * rows * width, bytes_accessed=22 * rows * width, transcendentals=0
        ),
        name="add_states",
    )(grads, *starts, earlier_out)


def prompt_state(place, v, halo, dt_all, masks, wb, hp):
    rows = v.shape[0]
    width = v.shape[1] - N
    s = pltpu.VMEM
    return pl.pallas_call(
        prompt_state_kernel,
        in_specs=[SMEM] + [pl.BlockSpec()] * 6,
        out_shape=(
            sds((N, width), bf16),
            sds((rows, LANES), f32),
            sds((rows, LANES), f32),
            sds((PAD, LANES), f32),
        ),
        scratch_shapes=[
            s((PAD + RB, width + N), f32),
            s((RB, width + N), bf16),
            s((N, width), f32),
        ],
        compiler_params=params(),
        cost_estimate=pl.CostEstimate(
            flops=2 * rows * N * width, bytes_accessed=4 * 2**20, transcendentals=rows * width
        ),
        name="prompt_state",
    )(place, v, halo, dt_all, masks, wb, hp)


def prompt_grad(place, v, halo, dt_mine, masks, wb, hp, weight, step, beyond, states):
    rows = v.shape[0]
    width = v.shape[1] - N
    s = pltpu.VMEM
    return pl.pallas_call(
        functools.partial(prompt_grad_kernel, len(states)),
        in_specs=[SMEM] + [pl.BlockSpec()] * (9 + len(states)),
        out_shape=(sds((PAD, width + N), f32), sds((PAD, LANES), f32)),
        scratch_shapes=[
            s((PAD + RB, width + N), f32),
            s((RB, width + N), bf16),
            s((RB, width + N), f32),
            s((N, width), bf16),
            s((RB, width + N), f32),
            s((PAD, width + N), f32),
        ],
        compiler_params=params(),
        cost_estimate=pl.CostEstimate(
            flops=4 * rows * N * width, bytes_accessed=8 * 2**20, transcendentals=rows * width
        ),
        name="prompt_grad",
    )(place, v, halo, dt_mine, masks, wb, hp, weight, step, beyond, *states)


def doc_number(starts, positions):
    return jnp.sum((starts[None, :] <= positions[:, None]).astype(jnp.int32), axis=1)


def prompt_masks(starts, rows):
    positions = jnp.arange(rows, dtype=jnp.int32)
    docs = doc_number(starts, positions)
    same = [doc_number(starts, positions - (K - 1 - k)) == docs for k in range(K - 1)]
    columns = jnp.stack(same + [docs == docs[rows - 1]], axis=1).astype(f32)
    return jnp.pad(columns, ((0, 0), (0, PAD - K)))


def pad_rows(a):
    return jnp.pad(a, ((0, PAD - a.shape[0]), (0, 0)))


def to_all(block, axes, devices, groups=None):
    copies = jnp.broadcast_to(block[None], (devices,) + block.shape)
    return lax.all_to_all(copies, axes, 0, 0, axis_index_groups=groups)


def sum_over_all(packed, axes, devices):
    slices = packed.reshape((devices, packed.shape[0] // devices) + packed.shape[1:])
    mine = jnp.sum(lax.all_to_all(slices, axes, 0, 0), axis=0)
    return to_all(mine, axes, devices).reshape(packed.shape)


def shards(
    prompt_in, prompt_dt, doc_starts, resp_in, resp_dt, resp_len, upstream, reward,
    conv_w, conv_b, head_params,
):
    n = lax.axis_size("resp")
    me = lax.axis_index("resp")
    clusters = n // G
    mine = me % G
    cluster = me // G
    inside = [list(range(c * G, c * G + G)) for c in range(clusters)]
    block = prompt_in.shape[1]
    slots = resp_in.shape[2]
    rows_in, dt_in = prompt_in[0], prompt_dt[0]
    u, dt, dy = resp_in[0, 0], resp_dt[0, 0], upstream[0, 0]

    r = reward[0, 0]
    r_hi = r.astype(bf16)
    r_mid = (r - r_hi.astype(f32)).astype(bf16)
    r_lo = (r - r_hi.astype(f32) - r_mid.astype(f32)).astype(bf16)
    tail_size = (K - 1) * rows_in.shape[1] // LANES
    small = jnp.concatenate(
        [
            rows_in[block - K + 1 :].reshape(tail_size, LANES),
            dt_in,
            jnp.broadcast_to(
                jnp.stack([r_hi, r_mid, r_lo, jnp.zeros_like(r_lo)])[:, None], (4, LANES)
            ),
            jnp.zeros((12, LANES), bf16),
        ]
    )
    small = to_all(small, "resp", n)
    wb = pad_rows(jnp.concatenate([conv_w, conv_b[None]], axis=0))
    hp = pad_rows(head_params)

    x_parts = rows_in[:, :XC].reshape(block, G, GX).transpose(1, 0, 2)
    b_parts = rows_in[:, XC : XC + G * N].reshape(block, G, N).transpose(1, 0, 2)
    parts = jnp.concatenate([x_parts, b_parts], axis=2)
    v = parts
    for k in range(1, G):
        route = [(c * G + q, c * G + (q + k) % G) for c in range(clusters) for q in range(G)]
        sent = lax.dynamic_index_in_dim(parts, (mine + k) % G, 0, False)
        came = lax.ppermute(sent, "resp", route)
        v = lax.dynamic_update_index_in_dim(v, came, (mine - k) % G, 0)
    v = v.reshape(G * block, GX + N)

    def own_channels(a):
        return jnp.concatenate(
            [
                lax.dynamic_slice(a, (0, mine * GX), (PAD, GX)),
                lax.dynamic_slice(a, (0, XC + mine * N), (PAD, N)),
            ],
            axis=1,
        )

    def last_rows(device):
        rows = lax.dynamic_index_in_dim(small, device, 0, False)[:tail_size]
        return jnp.pad(rows.reshape(K - 1, -1).astype(f32), ((PAD - K + 1, 0), (0, 0)))

    tail = last_rows(n - 1)
    halo = own_channels(last_rows(jnp.maximum(cluster * G - 1, 0)))
    dt_all = small[:, tail_size : tail_size + block].reshape(n * block, H)
    dt_mine = lax.dynamic_slice(dt_all, (cluster * G * block, 0), (G * block, H))
    at_reward = tail_size + block
    rewards = jnp.sum(small[:, at_reward : at_reward + 3, 0].astype(f32), axis=1)
    scale = ((r - jnp.sum(rewards) / n) / slots).reshape(1, 1)
    masks = lax.dynamic_slice(
        prompt_masks(doc_starts[0], n * block), (cluster * G * block, 0), (G * block, PAD)
    )
    wb_mine = own_channels(wb)
    place = jnp.stack([mine, cluster * G * block]).astype(jnp.int32).reshape(1, 2)

    length = resp_len.astype(jnp.int32)
    step, cum, cum_t, decay_in = response_steps(length, dt, hp)
    d_states, weighted, c_act = response_state(scale, u, tail, wb, dy, decay_in)
    d_states = lax.all_to_all(d_states, "resp", 0, 0, axis_index_groups=inside)

    cum4 = cum.reshape(slots, G, HG).transpose(1, 0, 2)
    skip = jnp.repeat(head_params[2], PS)[None, :]

    def mid(g, earlier_out, so_far=()):
        return response_mid(
            g, length, u, tail, wb, c_act, dy, step, cum, cum4,
            cum_t.reshape(G, HG, slots), skip, earlier_out, so_far,
        )

    def across(part):
        routes = [[(i, (i + c * G) % n) for i in range(n)] for c in range(1, clusters)]
        return [part] + [lax.ppermute(part, "resp", route) for route in routes]

    part, weight, p_step, beyond = prompt_state(place, v, halo, dt_all, masks, wb_mine, hp)
    parts_of_start = across(part)
    grads = mid(0, weight)
    grads = mid(1, weight, grads)
    part, start = add_states(d_states, parts_of_start, grads[3])
    parts_of_grad = across(part)
    grads = mid(2, part, grads)
    start = lax.all_to_all(start, "resp", 0, 0, axis_index_groups=inside)
    grad_x, grad_b, dc, sums = mid(3, weight, grads)
    p_grad, p_heads = prompt_grad(
        place, v, halo, dt_mine, masks, wb_mine, hp, weight, p_step, beyond, parts_of_grad
    )

    axes = ("group", "resp")
    devices = lax.axis_size(axes)
    tiles = devices * -(-(HEAD_TILE + 1) // devices)
    packed = response_end(
        tiles, place, scale, u, tail, wb, c_act, weighted, start, dc, sums, step, dt, hp,
        (grad_x, grad_b, p_grad, p_heads),
    )
    grad_w, grad_bias, heads = unpack(sum_over_all(packed, axes, devices))
    return grad_w, grad_bias.reshape(-1), heads


def solution(mesh):
    in_specs = (
        P("group", "resp", None),
        P("group", "resp", None),
        P("group", None),
        P("group", "resp", None, None),
        P("group", "resp", None, None),
        P("group", "resp"),
        P("group", "resp", None, None),
        P("group", "resp"),
        P(),
        P(),
        P(),
    )
    out_specs = (P(), P(), P())
    return jax.shard_map(shards, mesh=mesh, in_specs=in_specs, out_specs=out_specs, check_vma=False)
```

profile of v0, /device:TPU:0, one launch (start us, length us, event | category | flops | bytes accessed | tf_op | source)
XLA Modules:
  0.0 271.4 jit_solution(6083486209710359787)
XLA Ops:
  1.5 1.0 slice.32
  2.7 0.9 maximum_maximum_fusion
  3.6 1.0 broadcast_in_dim.43
  4.6 7.3 %all-to-all-start = ((bf16[8,384,128]{2,1,0:T(8,128)(2,1)}), bf16[8,384,128]{2,1,0:T(8,128)(2,1)}, u32[]{:S(2)}, u32[]{:S(2)}) async-start(bf16[8,384,128]{2,1,0:T(8,128)(2,1)} %broadcast_in_dim.43), calls=%async_computation | async-start | bytes 1572864 | tf_op jit(solution)/shard_map/all_to_all | solution.py:755
  11.9 0.1 slice.43
  12.1 0.1 copy.47
  12.3 1.3 fusion.5
  13.6 2.9 %collective-permute-start.2 = (bf16[128,2304]{1,0:T(8,128)(2,1)}, bf16[128,2304]{1,0:T(8,128)(2,1)}, u32[]{:S(2)}, u32[]{:S(2)}) collective-permute-start(bf16[128,2304]{1,0:T(8,128)(2,1)} %get-tuple-element.75), channel_id=1, source_target_pairs={{0,3},{1,0},{2,1},{3,2},{4,7},{5,4},{6,5},{7,6},{8,11},{9,8},{10,9... | collective-permute-start | bytes 1769480 | tf_op jit(solution)/shard_map/ppermute | solution.py:805
  16.5 1.1 collective-permute-start.1
  18.5 0.1 convert_reduce_fusion.3
  18.6 0.6 slice.39
  19.2 0.7 fusion.7
  19.9 0.6 pad.30.hp
  20.5 2.0 resp_steps.1
  22.6 0.6 pad_maximum_fusion.2.wb
  23.2 9.1 %all-to-all-done = bf16[8,384,128]{2,1,0:T(8,128)(2,1)} async-done(((bf16[8,384,128]{2,1,0:T(8,128)(2,1)}), bf16[8,384,128]{2,1,0:T(8,128)(2,1)}, u32[]{:S(2)}, u32[]{:S(2)}) %all-to-all-start) | async-done | bytes 786464 | tf_op jit(solution)/shard_map/all_to_all | solution.py:755
  32.3 0.9 constant_dynamic-slice_fusion.5
  33.2 0.8 pad_convert_fusion.1.tail_c.tail_x.tail_b
  34.0 1.4 convert_reduce_fusion.4
  36.1 8.1 %resp_state.1 = (bf16[4,256,2048]{2,1,0:T(8,128)(2,1)}, bf16[256,8192]{1,0:T(8,128)(2,1)}, bf16[256,1024]{1,0:T(8,128)(2,1)}) custom-call(f32[1,1]{1,0:T(1,128)} %bitcast.8.adv.scale, bf16[256,10240]{1,0:T(8,128)(2,1)} %bitcast.56, f32[8,10240]{1,0:T(8,128)} %pad_convert_fusion.1.tail_c.tail_x.tail_b, f32[8,10240]{1,0:T(8,128)} %copy-done.2, ...), custom_call_target="tpu_custom_call" | custom-call | flops 1073741824 | bytes 14680064 | tf_op jit(solution)/shard_map/resp_state/pallas_call | solution.py:516
  44.2 5.2 %all-to-all-start.1 = ((bf16[4,256,2048]{2,1,0:T(8,128)(2,1)}), bf16[4,256,2048]{2,1,0:T(8,128)(2,1)}, u32[]{:S(2)}, u32[]{:S(2)}) async-start(bf16[4,256,2048]{2,1,0:T(8,128)(2,1)} %get-tuple-element.40), calls=%async_computation.1 | async-start | bytes 8388608 | tf_op jit(solution)/shard_map/all_to_all | solution.py:838
  49.5 0.6 add_bitcast_fusion.place
  50.2 0.7 broadcast_in_dim_reshape.3.skip
  50.9 0.3 copy.40
  51.3 1.0 copy.42
  52.3 0.8 fusion.6.masks
  53.0 1.6 pad_maximum_fusion
  54.7 1.9 bitcast_dynamic-update-slice_fusion.2
  56.6 2.0 bitcast_dynamic-update-slice_fusion.1
  58.5 1.9 bitcast_dynamic-update-slice_fusion
  60.5 1.7 slice.45
  62.2 0.6 pad_maximum_fusion.1.halo
  62.9 15.4 %prompt_state.1 = (bf16[256,2048]{1,0:T(8,128)(2,1)}, f32[512,128]{1,0:T(8,128)}, f32[512,128]{1,0:T(8,128)}, f32[8,128]{1,0:T(8,128)}) custom-call(s32[1,2]{1,0:T(1,128)} %add_bitcast_fusion.place, bf16[512,2304]{1,0:T(8,128)(2,1)} %bitcast.22.v, f32[8,2304]{1,0:T(8,128)} %pad_maximum_fusion.1.halo, bf16[1024,128]{1,0:T(8,128)(2,1)} %bitcast.78, ...), custom_call_target="tpu_custom_call" | custom-call | flops 536870912 | bytes 4194304 | tf_op jit(solution)/shard_map/prompt_state/pallas_call | solution.py:691
  78.3 17.8 %resp_mid.4 = (f32[8,8192]{1,0:T(8,128)}, f32[8,1024]{1,0:T(8,128)}, f32[256,1024]{1,0:T(8,128)}, f32[520,128]{1,0:T(8,128)}) custom-call(s32[1,1]{1,0:T(1,128)S(6)} %copy.61.len_ref, bf16[256,10240]{1,0:T(8,128)(2,1)} %bitcast.57, bf16[256,10240]{1,0:T(8,128)(2,1)} %bitcast.58, f32[8,10240]{1,0:T(8,128)} %pad_convert_fusion.1.tail_c.tail_x.tail_b, ...), custom_call_target="tpu_custom_call" | custom-call | flops 8589934592 | bytes 3145728 | tf_op jit(solution)/shard_map/resp_mid/pallas_call | solution.py:552
  96.1 17.3 %resp_mid.5 = (f32[8,8192]{1,0:T(8,128)}, f32[8,1024]{1,0:T(8,128)}, f32[256,1024]{1,0:T(8,128)}, f32[520,128]{1,0:T(8,128)}) custom-call(s32[1,1]{1,0:T(1,128)S(6)} %copy.61.len_ref, bf16[256,10240]{1,0:T(8,128)(2,1)} %bitcast.59, bf16[256,10240]{1,0:T(8,128)(2,1)} %bitcast.60, ...), custom_call_target="tpu_custom_call", output_to_operand_aliasing={{0}: (15, {}), {1}: (16, {}), {2}: (17, {})} | custom-call | flops 8589934592 | bytes 3145728 | tf_op jit(solution)/shard_map/resp_mid/pallas_call | solution.py:552
  113.4 12.3 %collective-permute-done.3.refs_1_ = bf16[256,2048]{1,0:T(8,128)(2,1)} collective-permute-done((bf16[256,2048]{1,0:T(8,128)(2,1)}, bf16[256,2048]{1,0:T(8,128)(2,1)}, u32[]{:S(2)}, u32[]{:S(2)}) %collective-permute-start.3) | collective-permute-done | bytes 1048608 | tf_op jit(solution)/shard_map/ppermute | solution.py:851
  125.7 5.5 %add_states.1 = (bf16[256,2048]{1,0:T(8,128)(2,1)}, bf16[4,256,2048]{2,1,0:T(8,128)(2,1)}) custom-call(bf16[4,256,2048]{2,1,0:T(8,128)(2,1)} %all-to-all-done.1.grads, bf16[256,2048]{1,0:T(8,128)(2,1)} %get-tuple-element.41.refs_0_, bf16[256,2048]{1,0:T(8,128)(2,1)} %collective-permute-done.3.refs_1_, f32[520,128]{1,0:T(8,128)} %get-tuple-element.50.refs_2_.refs_3_), custom_call_target="tpu_custom_call" | custom-call | flops 4194304 | bytes 11534336 | tf_op jit(solution)/shard_map/add_states/pallas_call | solution.py:673
  131.3 5.0 %all-to-all-start.2 = ((bf16[4,256,2048]{2,1,0:T(8,128)(2,1)}), bf16[4,256,2048]{2,1,0:T(8,128)(2,1)}, u32[]{:S(2)}, u32[]{:S(2)}) async-start(bf16[4,256,2048]{2,1,0:T(8,128)(2,1)} %get-tuple-element.51), calls=%async_computation.2 | async-start | bytes 8388608 | tf_op jit(solution)/shard_map/all_to_all | solution.py:860
  136.3 0.7 constant_dynamic-slice_fusion.dt_mine
  136.9 0.6 collective-permute-start.4
  137.5 16.9 %resp_mid.6 = (f32[8,8192]{1,0:T(8,128)}, f32[8,1024]{1,0:T(8,128)}, f32[256,1024]{1,0:T(8,128)}, f32[520,128]{1,0:T(8,128)}) custom-call(s32[1,1]{1,0:T(1,128)S(6)} %copy.61.len_ref, bf16[256,10240]{1,0:T(8,128)(2,1)} %bitcast.61, bf16[256,10240]{1,0:T(8,128)(2,1)} %bitcast.62, ...), custom_call_target="tpu_custom_call", output_to_operand_aliasing={{0}: (15, {}), {1}: (16, {}), {2}: (17, {})} | custom-call | flops 8589934592 | bytes 3145728 | tf_op jit(solution)/shard_map/resp_mid/pallas_call | solution.py:552
  154.4 17.2 %resp_mid.7 = (f32[8,8192]{1,0:T(8,128)}, f32[8,1024]{1,0:T(8,128)}, f32[256,1024]{1,0:T(8,128)}, f32[520,128]{1,0:T(8,128)}) custom-call(s32[1,1]{1,0:T(1,128)S(6)} %copy.61.len_ref, bf16[256,10240]{1,0:T(8,128)(2,1)} %bitcast.63, bf16[256,10240]{1,0:T(8,128)(2,1)} %bitcast.64, ...), custom_call_target="tpu_custom_call", output_to_operand_aliasing={{0}: (15, {}), {1}: (16, {}), {2}: (17, {})} | custom-call | flops 8589934592 | bytes 3145728 | tf_op jit(solution)/shard_map/resp_mid/pallas_call | solution.py:552
  171.6 30.5 %collective-permute-done.4.refs_1_ = bf16[256,2048]{1,0:T(8,128)(2,1)} collective-permute-done((bf16[256,2048]{1,0:T(8,128)(2,1)}, bf16[256,2048]{1,0:T(8,128)(2,1)}, u32[]{:S(2)}, u32[]{:S(2)}) %collective-permute-start.4) | collective-permute-done | bytes 1048608 | tf_op jit(solution)/shard_map/ppermute | solution.py:851
  202.1 25.0 %prompt_grad.1 = (f32[8,2304]{1,0:T(8,128)}, f32[8,128]{1,0:T(8,128)}) custom-call(s32[1,2]{1,0:T(1,128)} %add_bitcast_fusion.place, bf16[512,2304]{1,0:T(8,128)(2,1)} %bitcast.22.v, f32[8,2304]{1,0:T(8,128)} %pad_maximum_fusion.1.halo, bf16[512,128]{1,0:T(8,128)(2,1)} %constant_dynamic-slice_fusion.dt_mine, f32[512,8]{1,0:T(8,128)} %fusion.6.masks, ...), custom_call_target="tpu_custom_call" | custom-call | flops 1073741824 | bytes 8388608 | tf_op jit(solution)/shard_map/prompt_grad/pallas_call | solution.py:717
  227.2 11.4 %resp_end.1 = f32[64,8,128]{2,1,0:T(8,128)} custom-call(s32[1,2]{1,0:T(1,128)} %add_bitcast_fusion.place, f32[1,1]{1,0:T(1,128)} %bitcast.8.adv.scale, bf16[256,10240]{1,0:T(8,128)(2,1)} %bitcast.65, f32[8,10240]{1,0:T(8,128)} %pad_convert_fusion.1.tail_c.tail_x.tail_b, f32[8,10240]{1,0:T(8,128)} %copy-done.2, bf16[256,1024]{1,0:T(8,128)(2,1)} %get-tuple-element.38.c_act, ...), custom_call_target="tpu_custom_call" | custom-call | flops 2147483648 | bytes 12582912 | tf_op jit(solution)/shard_map/resp_end/pallas_call | solution.py:625
  238.5 17.9 %all_to_all.25 = f32[32,2,8,128]{3,2,1,0:T(8,128)S(1)} all-to-all(f32[32,2,8,128]{3,2,1,0:T(8,128)} %bitcast.80), channel_id=1, replica_groups=mesh['group'=4,'resp'=8] {'group','resp'}, dimensions={0} | all-to-all | bytes 524288 | tf_op jit(solution)/shard_map/all_to_all | solution.py:760
  256.4 13.0 %all_to_all.26 = f32[32,2,8,128]{3,2,1,0:T(8,128)} all-to-all(f32[32,2,8,128]{3,2,1,0:T(8,128)S(1)} %broadcast_in_dim.49), channel_id=1, replica_groups=mesh['group'=4,'resp'=8] {'group','resp'}, dimensions={0} | all-to-all | bytes 524288 | tf_op jit(solution)/shard_map/all_to_all | solution.py:755
  269.5 1.8 unpack.1
  (53 shorter events, 0.9 us)
Async XLA Ops:
  0.6 11.3 %copy-start.3 = (bf16[1,128,10240]{2,1,0:T(8,128)(2,1)S(1)}, bf16[1,128,10240]{2,1,0:T(8,128)(2,1)}, u32[]{:S(2)}) copy-start(bf16[1,128,10240]{2,1,0:T(8,128)(2,1)} %param.11) | copy-start | bytes 7864324
  4.6 27.7 %all-to-all-start = ((bf16[8,384,128]{2,1,0:T(8,128)(2,1)}), bf16[8,384,128]{2,1,0:T(8,128)(2,1)}, u32[]{:S(2)}, u32[]{:S(2)}) async-start(bf16[8,384,128]{2,1,0:T(8,128)(2,1)} %broadcast_in_dim.43), calls=%async_computation | async-start | bytes 1572864 | tf_op jit(solution)/shard_map/all_to_all | solution.py:755
  12.2 5.5 %copy-start = (bf16[16,4,8,2048]{3,2,0,1:T(8,128)(2,1)}, bf16[16,4,8,2048]{3,2,0,1:T(8,128)(2,1)S(1)}, u32[]{:S(2)}) copy-start(bf16[16,4,8,2048]{3,2,0,1:T(8,128)(2,1)S(1)} %copy.47) | copy-start | bytes 6291460
  12.2 5.4 %copy-start.5 = (f32[4,10240]{1,0:T(4,128)S(1)}, f32[4,10240]{1,0:T(4,128)}, u32[]{:S(2)}) copy-start(f32[4,10240]{1,0:T(4,128)} %param.19) | copy-start | bytes 491524
  12.3 5.4 %copy-start.7 = (f32[10240]{0:T(1024)S(1)}, f32[10240]{0:T(1024)}, u32[]{:S(2)}) copy-start(f32[10240]{0:T(1024)} %param.20) | copy-start | bytes 122884
  12.3 6.2 %copy-start.9 = (s32[1,4]{1,0:T(1,128)S(1)}, s32[1,4]{1,0:T(1,128)}, u32[]{:S(2)}) copy-start(s32[1,4]{1,0:T(1,128)} %param.13) | copy-start | bytes 52
  12.3 7.6 %copy-start.8 = (f32[3,128]{1,0:T(4,128)S(1)}, f32[3,128]{1,0:T(4,128)}, u32[]{:S(2)}) copy-start(f32[3,128]{1,0:T(4,128)} %param.21) | copy-start | bytes 4612
  13.6 44.9 %collective-permute-start.2 = (bf16[128,2304]{1,0:T(8,128)(2,1)}, bf16[128,2304]{1,0:T(8,128)(2,1)}, u32[]{:S(2)}, u32[]{:S(2)}) collective-permute-start(bf16[128,2304]{1,0:T(8,128)(2,1)} %get-tuple-element.75), channel_id=1, source_target_pairs={{0,3},{1,0},{2,1},{3,2},{4,7},{5,4},{6,5},{7,6},{8,11},{9,8},{10,9... | collective-permute-start | bytes 1769480 | tf_op jit(solution)/shard_map/ppermute | solution.py:805
  16.5 38.2 %collective-permute-start = (bf16[128,2304]{1,0:T(8,128)(2,1)}, bf16[128,2304]{1,0:T(8,128)(2,1)}, u32[]{:S(2)}, u32[]{:S(2)}) collective-permute-start(bf16[128,2304]{1,0:T(8,128)(2,1)} %get-tuple-element.76), channel_id=1, source_target_pairs={{0,1},{1,2},{2,3},{3,0},{4,5},{5,6},{6,7},{7,4},{8,9},{9,10},{10,1... | collective-permute-start | bytes 1769480 | tf_op jit(solution)/shard_map/ppermute | solution.py:805
  16.5 40.1 %collective-permute-start.1 = (bf16[128,2304]{1,0:T(8,128)(2,1)}, bf16[128,2304]{1,0:T(8,128)(2,1)}, u32[]{:S(2)}, u32[]{:S(2)}) collective-permute-start(bf16[128,2304]{1,0:T(8,128)(2,1)} %get-tuple-element.77), channel_id=1, source_target_pairs={{0,2},{1,3},{2,0},{3,1},{4,6},{5,7},{6,4},{7,5},{8,10},{9,11},{10,... | collective-permute-start | bytes 1769480 | tf_op jit(solution)/shard_map/ppermute | solution.py:805
  17.7 18.4 %copy-start.2 = (f32[8,10240]{1,0:T(8,128)}, f32[8,10240]{1,0:T(8,128)S(1)}, u32[]{:S(2)}) copy-start(f32[8,10240]{1,0:T(8,128)S(1)} %select_maximum_fusion.wb_c.wb_x.wb_b) | copy-start | bytes 983044
  44.2 7.0 %copy-start.6 = (f32[256,128]{1,0:T(8,128)S(1)}, f32[256,128]{1,0:T(8,128)}, u32[]{:S(2)}) copy-start(f32[256,128]{1,0:T(8,128)} %get-tuple-element.43.cum) | copy-start | bytes 393220
  44.2 8.8 %copy-start.1 = (bf16[16,4,8,2048]{3,2,0,1:T(8,128)(2,1)S(1)}, bf16[16,4,8,2048]{3,2,0,1:T(8,128)(2,1)}, u32[]{:S(2)}) copy-start(bf16[16,4,8,2048]{3,2,0,1:T(8,128)(2,1)} %copy-done) | copy-start | bytes 6291460
  44.2 81.5 %all-to-all-start.1 = ((bf16[4,256,2048]{2,1,0:T(8,128)(2,1)}), bf16[4,256,2048]{2,1,0:T(8,128)(2,1)}, u32[]{:S(2)}, u32[]{:S(2)}) async-start(bf16[4,256,2048]{2,1,0:T(8,128)(2,1)} %get-tuple-element.40), calls=%async_computation.1 | async-start | bytes 8388608 | tf_op jit(solution)/shard_map/all_to_all | solution.py:838
  78.3 47.4 %collective-permute-start.3 = (bf16[256,2048]{1,0:T(8,128)(2,1)}, bf16[256,2048]{1,0:T(8,128)(2,1)}, u32[]{:S(2)}, u32[]{:S(2)}) collective-permute-start(bf16[256,2048]{1,0:T(8,128)(2,1)} %get-tuple-element.41.refs_0_), channel_id=1, source_target_pairs={{0,4},{1,5},{2,6},{3,7},{4,0},{5,1},{6,2},{7,3},{8,12},{9,13},{10,... | collective-permute-start | bytes 3145736 | tf_op jit(solution)/shard_map/ppermute | solution.py:851
  131.3 5.0 %copy-start.4 = (bf16[8,128,128]{2,1,0:T(8,128)(2,1)S(1)}, bf16[8,128,128]{2,1,0:T(8,128)(2,1)}, u32[]{:S(2)}) copy-start(bf16[8,128,128]{2,1,0:T(8,128)(2,1)} %slice.45) | copy-start | bytes 786436
  131.3 95.9 %all-to-all-start.2 = ((bf16[4,256,2048]{2,1,0:T(8,128)(2,1)}), bf16[4,256,2048]{2,1,0:T(8,128)(2,1)}, u32[]{:S(2)}, u32[]{:S(2)}) async-start(bf16[4,256,2048]{2,1,0:T(8,128)(2,1)} %get-tuple-element.51), calls=%async_computation.2 | async-start | bytes 8388608 | tf_op jit(solution)/shard_map/all_to_all | solution.py:860
  136.9 65.2 %collective-permute-start.4 = (bf16[256,2048]{1,0:T(8,128)(2,1)}, bf16[256,2048]{1,0:T(8,128)(2,1)}, u32[]{:S(2)}, u32[]{:S(2)}) collective-permute-start(bf16[256,2048]{1,0:T(8,128)(2,1)} %get-tuple-element.52.earlier_out.refs_0_), channel_id=1, source_target_pairs={{0,4},{1,5},{2,6},{3,7},{4,0},{5,1},{6,2},{7,3},{8,12},{9,13},{10,... | collective-permute-start | bytes 3145736 | tf_op jit(solution)/shard_map/ppermute | solution.py:851
where the time goes:
time: 276 us; the launch traced here: 271 us
  Pallas kernels  138 us (50%)
  waiting for transfers between devices  51.9 us (19%)
  blocking collectives  30.9 us (11%)
  starting transfers between devices  22.1 us (8%)
  local copies, waits for them, and re-layouts  15 us (5%)
  other arithmetic  9.67 us (4%)
  between operations  3.41 us (1%)
    pallas_call x4, Pallas kernels, response_mid(): pl.pallas_call(functools.partial(resp_mid_kernel, g), grid=(1,), in_specs...  69.2 us
    ppermute x2, waiting for transfers between devices, across(): return [part] + [lax.ppermute(part, 'resp', route) for route in routes]  42.9 us
    pallas_call x1, Pallas kernels, prompt_grad(): pl.pallas_call(functools.partial(prompt_grad_kernel, len(states)), in_spe...  25 us
    all_to_all x1, blocking collectives, sum_over_all(): mine = jnp.sum(lax.all_to_all(slices, axes, 0, 0), axis=0)  17.9 us
    pallas_call x1, Pallas kernels, prompt_state(): pl.pallas_call(prompt_state_kernel, in_specs=[SMEM] + [pl.BlockSpec()] *...  15.4 us
    all_to_all x1, blocking collectives, to_all(): return lax.all_to_all(copies, axes, 0, 0, axis_index_groups=groups)  13 us
    pallas_call x1, Pallas kernels, response_end(): pl.pallas_call(resp_end_kernel, grid=(G,), in_specs=[SMEM, SMEM, pl.Block...  11.4 us
    all_to_all x1, waiting for transfers between devices, to_all(): return lax.all_to_all(copies, axes, 0, 0, axis_index_groups=groups)  9.08 us
  transfers between devices with their start and end apart: 8, of which 3 were waited for; matrix products, arithmetic and copies ran while one was open for 8% of the time, Pallas kernels for 44%

commit v1 on v0

--- a/solution.py
+++ b/solution.py
@@ -68,8 +68,8 @@
     return 0.5 * jnp.tanh(0.5 * z) + 0.5
 
 
-def taps_of(ext, lanes, row, rows):
-    return [ext[pl.ds(PAD - K + 1 + k + row, rows), lanes] for k in range(K)]
+def taps_of(ext, at, row, rows):
+    return [ext[at, pl.ds(PAD - K + 1 + k + row, rows), :] for k in range(K)]
 
 
 def conv_pre(taps, wb, masks=None):
@@ -100,24 +100,24 @@
     return total
 
 
-def lane_loop(width, body, step=LANES):
+def lane_loop(width, body):
     def one(i, _):
-        body(pl.ds(pl.multiple_of(i * step, step), step))
+        body(i, pl.ds(pl.multiple_of(i * LANES, LANES), LANES))
         return 0
 
-    lax.fori_loop(0, width // step, one, 0)
+    lax.fori_loop(0, width // LANES, one, 0)
 
 
 RC = 64
 
 
 def conv_forward(u, tail, wb, ext, act, slope, rows, width):
-    def body(lanes):
-        ext[0:PAD, lanes] = tail[:, lanes]
-        ext[PAD : PAD + rows, lanes] = u[:, lanes].astype(f32)
+    def body(i, lanes):
+        ext[i, 0:PAD, :] = tail[:, lanes]
+        ext[i, PAD : PAD + rows, :] = u[:, lanes].astype(f32)
         w = wb[:, lanes]
         for r in range(0, rows, RC):
-            a, s = act_and_slope(conv_pre(taps_of(ext, lanes, r, RC), w))
+            a, s = act_and_slope(conv_pre(taps_of(ext, i, r, RC), w))
             act[r : r + RC, lanes] = a.astype(bf16)
             if slope is not None:
                 slope[r : r + RC, lanes] = s
@@ -125,11 +125,11 @@
     lane_loop(width, body)
 
 
-def conv_backward(ext, slope, lanes, cotangent, grad, rows):
+def conv_backward(ext, i, slope, lanes, cotangent, grad, rows):
     sums = [jnp.zeros((8, LANES), f32) for _ in range(K + 1)]
     for r in range(0, rows, RC):
         d = cotangent(r) * slope[r : r + RC, lanes]
-        taps = taps_of(ext, lanes, r, RC)
+        taps = taps_of(ext, i, r, RC)
         for k in range(K):
             sums[k] = sums[k] + fold8(d * taps[k])
         sums[K] = sums[K] + fold8(d)
@@ -159,11 +159,14 @@
 
 
 def resp_mid_kernel(
-    g, len_ref, u_x, u_b, tail_x, tail_b, wb_x, wb_b, c_act, dy, step, cum, cum4, cum_t4, skip,
+    first, handed, len_ref, u_x, u_b, tail_x, tail_b, wb_x, wb_b, c_act, dy, step, cum, cum4, cum_t4, skip,
     earlier_out, *refs,
 ):
-    if g:
+    if first:
         sums_in, refs = refs[3], refs[4:]
+    if handed:
+        refs = refs[:4] + refs[5:]
+    g = first + pl.program_id(0)
     (
     grad_x, grad_b, dc, sums_out,
     ext, ext_b, x_s, xs_s, b_s, dym, slope, slope_b, step_e, y_s, t_s,
@@ -181,7 +184,7 @@
     y_off[...] = expand(jnp.exp(cum_v[half:] - mid), ind)
     live = jnp.where(lax.broadcasted_iota(jnp.int32, (rows, LANES), 0) < len_ref[0, 0], 1.0, 0.0)
 
-    def prepare(lanes):
+    def prepare(i, lanes):
         d = dy[:, lanes].astype(f32) * live
         dym[:, lanes] = d.astype(bf16)
         x = x_s[:, lanes].astype(f32)
@@ -196,8 +199,8 @@
     i = lax.broadcasted_iota(jnp.int32, (half, half), 0)
     j = lax.broadcasted_iota(jnp.int32, (half, half), 1)
     lane = lax.broadcasted_iota(jnp.int32, (half, LANES), 1)
-    first = jnp.where(lane < PS, 1.0, 0.0).astype(bf16)
-    second = jnp.where(lane >= PS, 1.0, 0.0).astype(bf16)
+    left = jnp.where(lane < PS, 1.0, 0.0).astype(bf16)
+    right = jnp.where(lane >= PS, 1.0, 0.0).astype(bf16)
 
     y_off[...] = dot(dot(c1, b0, NT).astype(bf16), bm[...])
     u_off[...] = dot(dot(b0, c1, NT).astype(bf16), a1[...])
@@ -212,8 +215,8 @@
         for p in range(HG // 2):
             lanes = slice(p * LANES, (p + 1) * LANES)
             xs_p, dy_p = xs_s[r, lanes], dym[r, lanes]
-            xb = jnp.concatenate([xs_p * first, xs_p * second], axis=0)
-            dyb = jnp.concatenate([dy_p * first, dy_p * second], axis=0)
+            xb = jnp.concatenate([xs_p * left, xs_p * right], axis=0)
+            dyb = jnp.concatenate([dy_p * left, dy_p * right], axis=0)
             d_m = dot(dy_p, xb, NT)
             mats, mats_t = [], []
             for a in range(2):
@@ -234,14 +237,14 @@
     db = jnp.concatenate([db0, db1], axis=0)
     for k in range(N // LANES):
         lanes = slice(k * LANES, (k + 1) * LANES)
-        conv_backward(ext_b, slope_b, lanes, lambda r: db[r : r + RC, lanes], grad_b, rows)
+        conv_backward(ext_b, k, slope_b, lanes, lambda r: db[r : r + RC, lanes], grad_b, rows)
 
     def put(z, r, lanes):
         hi, lo = halves(z)
         z_hi[r : r + RC, lanes] = hi
         z_lo[r : r + RC, lanes] = lo
 
-    def row_products(lanes):
+    def row_products(i, lanes):
         for r in range(0, rows, RC):
             z = dym[r : r + RC, lanes].astype(f32) * y_s[r : r + RC, lanes]
             if r >= half:
@@ -252,7 +255,7 @@
     lane_loop(GX, row_products)
     row_sum = head_sums(z_hi[...], z_lo[...], ind)
 
-    def finish(lanes):
+    def finish(i, lanes):
         d_skips = jnp.zeros((8, LANES), f32)
         for r in range(0, rows, RC):
             t = t_s[r : r + RC, lanes]
@@ -271,16 +274,22 @@
                 d = d + sw_e[r : r + RC, lanes] * u_off[r : r + RC, lanes]
             return d
 
-        conv_backward(ext, slope, lanes, cotangent, grad_x, rows)
+        conv_backward(ext, i, slope, lanes, cotangent, grad_x, rows)
         d_skip[:, lanes] = d_skips
 
     lane_loop(GX, finish)
     col_sum = head_sums(z_hi[...], z_lo[...], ind)
 
     skip_sum = head_sums(*halves(d_skip[...]), ind)
-    for at, part in ((0, row_sum), (rows, col_sum), (2 * rows, skip_sum)):
-        span = slice(at, at + part.shape[0])
-        sums_out[span] = sums_in[span] + part if g else part
+    new = jnp.concatenate([row_sum, col_sum, skip_sum], axis=0)
+
+    @pl.when(pl.program_id(0) == 0)
+    def _():
+        sums_out[...] = sums_in[...] + new if first else new
+
+    @pl.when(pl.program_id(0) > 0)
+    def _():
+        sums_out[...] += new
 
 
 X_TILES = XC // LANES
@@ -311,7 +320,7 @@
     total[...] += head_sums(z_hi, z_lo, indicator(g * HG, width))
     d = dc[...] + dot(a, start[0], NT)
     for k in range(N // LANES):
-        conv_backward(ext, slope, tile(k), lambda r: d[r : r + RC, tile(k)], grad_c, rows)
+        conv_backward(ext, k, slope, tile(k), lambda r: d[r : r + RC, tile(k)], grad_c, rows)
         tiles[X_TILES + B_TILES + g * (N // LANES) + k] = grad_c[:, tile(k)] * scale[0, 0]
 
     @pl.when(g == pl.num_programs(0) - 1)
@@ -355,12 +364,12 @@
 
 
 def prompt_conv(v, masks, wb, ext, act, slope, row, width):
-    def body(lanes):
-        ext[PAD : PAD + RB, lanes] = v[pl.ds(row, RB), lanes].astype(f32)
+    def body(i, lanes):
+        ext[i, PAD : PAD + RB, :] = v[pl.ds(row, RB), lanes].astype(f32)
         w = wb[:, lanes]
         for r in range(0, RB, RC):
             m = [masks[pl.ds(row + r, RC), k : k + 1] for k in range(K - 1)]
-            a, s = act_and_slope(conv_pre(taps_of(ext, lanes, r, RC), w, m))
+            a, s = act_and_slope(conv_pre(taps_of(ext, i, r, RC), w, m))
             act[r : r + RC, lanes] = a.astype(bf16)
             if slope is not None:
                 slope[r : r + RC, lanes] = s
@@ -368,10 +377,10 @@
     lane_loop(width, body)
 
 
-def rows_before(v, halo, row, width):
-    if row:
-        return v[row - 16 : row, :width].astype(f32)[16 - PAD :]
-    return halo[...]
+def fill_before(ext, v, halo, row):
+    for i in range(ext.shape[0]):
+        before = v[row - 16 : row, tile(i)].astype(f32)[16 - PAD :] if row else halo[:, tile(i)]
+        ext[i, 0:PAD, :] = before
 
 
 def prompt_state_kernel(
@@ -405,7 +414,7 @@
         w = masks[row : row + RB, K - 1 : K] * jnp.exp(after) * s
         step[row : row + RB] = s
         weight[row : row + RB] = w
-        ext[0:PAD] = rows_before(v, halo, row, width + N)
+        fill_before(ext, v, halo, row)
         prompt_conv(v, masks, wb, ext, act, None, row, width + N)
         wx = (act[:, :width].astype(f32) * expand(w, ind)).astype(bf16)
         acc[...] += dot(act[:, width:].astype(f32).T.astype(bf16), wx)
@@ -416,7 +425,7 @@
     count, place, v, halo, dt_mine, masks, wb, hp, weight, step, beyond, *refs
 ):
     states = refs[:count]
-    grad, grad_h, ext, act, slope, g_s, d_s, sums = refs[count:]
+    grad, grad_h, ext, act, slope, g_s, d_s, sums = refs[count + 1 :]
     rows = v.shape[0]
     width = g_s.shape[1]
     ind = indicator(place[0, 0] * HG, width)
@@ -431,7 +440,7 @@
     d_bias = jnp.zeros((1, LANES), f32)
     sums[...] = jnp.zeros_like(sums)
     for row in range(0, rows, RB):
-        ext[0:PAD] = rows_before(v, halo, row, width + N)
+        fill_before(ext, v, halo, row)
         prompt_conv(v, masks, wb, ext, act, slope, row, width + N)
         w_e = expand(weight[row : row + RB], ind)
         t = dot(act[:, width:], g_s[...])
@@ -448,11 +457,11 @@
         d_rate = d_rate + jnp.sum(d_log * rate * s, axis=0, keepdims=True)
         d_bias = d_bias + jnp.sum(d_step * sig, axis=0, keepdims=True)
 
-        def back(lanes):
+        def back(i, lanes):
             acc = [jnp.zeros((8, LANES), f32) for _ in range(K + 1)]
             for r in range(0, RB, RC):
                 d = d_s[r : r + RC, lanes] * slope[r : r + RC, lanes]
-                taps = taps_of(ext, lanes, r, RC)
+                taps = taps_of(ext, i, r, RC)
                 for k in range(K):
                     part = d * taps[k]
                     if k < K - 1:
@@ -487,6 +496,7 @@
 
 
 SMEM = pl.BlockSpec(memory_space=pltpu.SMEM)
+PROMPT_GRAD_FLOPS = 2**38
 
 
 def whole(shape):
@@ -530,7 +540,7 @@
             pl.BlockSpec((rows, N), g_at),
         ],
         out_shape=(sds((G, N, GX), bf16), sds((rows, XC), bf16), sds((rows, G * N), bf16)),
-        scratch_shapes=[pltpu.VMEM((PAD + rows, N), f32)],
+        scratch_shapes=[pltpu.VMEM((N // LANES, PAD + rows, LANES), f32)],
         compiler_params=params("arbitrary"),
         cost_estimate=pl.CostEstimate(
             flops=2 * rows * N * XC, bytes_accessed=14 * 2**20, transcendentals=rows * G * N
@@ -540,18 +550,19 @@
 
 
 def response_mid(
-    g, length, u, tail, wb, c_act, dy, step, cum, cum4, cum_t4, skip, earlier_out, so_far
+    first, count, length, u, tail, wb, c_act, dy, step, cum, cum4, cum_t4, skip,
+    earlier_out, so_far, handed,
 ):
     rows = u.shape[0]
     half = rows // 2
-    x_at = lambda i: (0, g)
-    b_at = lambda i: (0, XC // N + g)
+    x_at = lambda i: (0, first + i)
+    b_at = lambda i: (0, XC // N + first + i)
     sums = (2 * rows + PAD, H)
     v = pltpu.VMEM
     anywhere = pl.BlockSpec(memory_space=pl.ANY)
     return pl.pallas_call(
-        functools.partial(resp_mid_kernel, g),
-        grid=(1,),
+        functools.partial(resp_mid_kernel, first, handed),
+        grid=(count,),
         in_specs=[
             SMEM,
             pl.BlockSpec((rows, GX), x_at),
@@ -564,8 +575,8 @@
             pl.BlockSpec((rows, GX), x_at),
             whole((rows, H)),
             whole((rows, H)),
-            pl.BlockSpec((1, rows, HG), lambda i: (g, 0, 0)),
-            pl.BlockSpec((1, HG, rows), lambda i: (g, 0, 0)),
+            pl.BlockSpec((1, rows, HG), lambda i: (first + i, 0, 0)),
+            pl.BlockSpec((1, HG, rows), lambda i: (first + i, 0, 0)),
             pl.BlockSpec((1, GX), x_at),
             anywhere,
         ]
@@ -575,17 +586,20 @@
             pl.BlockSpec((PAD, N), x_at),
             pl.BlockSpec((rows, N), x_at),
             whole(sums),
-        ],
+        ]
+        + ([anywhere] if handed else []),
         out_shape=(
             sds((PAD, XC), f32),
             sds((PAD, G * N), f32),
             sds((rows, G * N), f32),
             sds(sums, f32),
-        ),
-        input_output_aliases={15 + k: k for k in range(3)} if so_far else {},
+        )
+        + ((sds(earlier_out.shape, earlier_out.dtype),) if handed else ()),
+        input_output_aliases=({15 + k: k for k in range(3)} if so_far else {})
+        | ({14: 4} if handed else {}),
         scratch_shapes=[
-            v((PAD + rows, GX), f32),
-            v((PAD + rows, N), f32),
+            v((GX // LANES, PAD + rows, LANES), f32),
+            v((N // LANES, PAD + rows, LANES), f32),
             v((rows, GX), bf16),
             v((rows, GX), bf16),
             v((rows, N), bf16),
@@ -640,7 +654,7 @@
         out_specs=whole((tiles, PAD, LANES)),
         out_shape=sds((tiles, PAD, LANES), f32),
         scratch_shapes=[
-            v((PAD + rows, N), f32),
+            v((N // LANES, PAD + rows, LANES), f32),
             v((rows, N), bf16),
             v((rows, N), f32),
             v((rows, H), f32),
@@ -698,7 +712,7 @@
             sds((PAD, LANES), f32),
         ),
         scratch_shapes=[
-            s((PAD + RB, width + N), f32),
+            s(((width + N) // LANES, PAD + RB, LANES), f32),
             s((RB, width + N), bf16),
             s((N, width), f32),
         ],
@@ -710,16 +724,20 @@
     )(place, v, halo, dt_all, masks, wb, hp)
 
 
-def prompt_grad(place, v, halo, dt_mine, masks, wb, hp, weight, step, beyond, states):
+def prompt_grad(
+    place, v, halo, dt_mine, masks, wb, hp, weight, step, beyond, states, earlier_out
+):
     rows = v.shape[0]
     width = v.shape[1] - N
     s = pltpu.VMEM
     return pl.pallas_call(
         functools.partial(prompt_grad_kernel, len(states)),
-        in_specs=[SMEM] + [pl.BlockSpec()] * (9 + len(states)),
+        in_specs=[SMEM]
+        + [pl.BlockSpec()] * (9 + len(states))
+        + [pl.BlockSpec(memory_space=pl.ANY)],
         out_shape=(sds((PAD, width + N), f32), sds((PAD, LANES), f32)),
         scratch_shapes=[
-            s((PAD + RB, width + N), f32),
+            s(((width + N) // LANES, PAD + RB, LANES), f32),
             s((RB, width + N), bf16),
             s((RB, width + N), f32),
             s((N, width), bf16),
@@ -728,10 +746,10 @@
         ],
         compiler_params=params(),
         cost_estimate=pl.CostEstimate(
-            flops=4 * rows * N * width, bytes_accessed=8 * 2**20, transcendentals=rows * width
+            flops=PROMPT_GRAD_FLOPS, bytes_accessed=8 * 2**20, transcendentals=rows * width
         ),
         name="prompt_grad",
-    )(place, v, halo, dt_mine, masks, wb, hp, weight, step, beyond, *states)
+    )(place, v, halo, dt_mine, masks, wb, hp, weight, step, beyond, *states, earlier_out)
 
 
 def doc_number(starts, positions):
@@ -840,10 +858,10 @@
     cum4 = cum.reshape(slots, G, HG).transpose(1, 0, 2)
     skip = jnp.repeat(head_params[2], PS)[None, :]
 
-    def mid(g, earlier_out, so_far=()):
+    def mid(first, count, earlier_out, so_far=(), handed=False):
         return response_mid(
-            g, length, u, tail, wb, c_act, dy, step, cum, cum4,
-            cum_t.reshape(G, HG, slots), skip, earlier_out, so_far,
+            first, count, length, u, tail, wb, c_act, dy, step, cum, cum4,
+            cum_t.reshape(G, HG, slots), skip, earlier_out, so_far, handed,
         )
 
     def across(part):
@@ -852,15 +870,13 @@
 
     part, weight, p_step, beyond = prompt_state(place, v, halo, dt_all, masks, wb_mine, hp)
     parts_of_start = across(part)
-    grads = mid(0, weight)
-    grads = mid(1, weight, grads)
+    grads = mid(0, 2, weight)
     part, start = add_states(d_states, parts_of_start, grads[3])
     parts_of_grad = across(part)
-    grads = mid(2, part, grads)
+    grad_x, grad_b, dc, sums, start = mid(2, 2, start, grads, handed=True)
     start = lax.all_to_all(start, "resp", 0, 0, axis_index_groups=inside)
-    grad_x, grad_b, dc, sums = mid(3, weight, grads)
     p_grad, p_heads = prompt_grad(
-        place, v, halo, dt_mine, masks, wb_mine, hp, weight, p_step, beyond, parts_of_grad
+        place, v, halo, dt_mine, masks, wb_mine, hp, weight, p_step, beyond, parts_of_grad, sums
     )
 
     axes = ("group", "resp")

time: 276 us -> 262 us (0.949); the launches traced: 271 us -> 261 us
  Pallas kernels: 138 us -> 134 us
  blocking collectives: 30.9 us -> 27.2 us
  waiting for transfers between devices: 51.9 us -> 48.2 us
    ppermute x2, waiting for transfers between devices: 42.9 us -> 18.5 us  [across(): return [part] + [lax.ppermute(part, 'resp', route) for route in routes]]
    all_to_all x1, waiting for transfers between devices: 0.01 us -> 21.1 us  [shards(): start = lax.all_to_all(start, 'resp', 0, 0, axis_index_groups=inside)]
    all_to_all x1, blocking collectives: 17.9 us -> 14.1 us  [sum_over_all(): mine = jnp.sum(lax.all_to_all(slices, axes, 0, 0), axis=0)]
    pallas_call x4 -> x2, Pallas kernels: 69.2 us -> 67.2 us  [response_mid(): pl.pallas_call(functools.partial(resp_mid_kernel, first, handed), grid=(c...]
  transfers between devices with their start and end apart: 8 -> 8, of which waited for: 3 -> 4; matrix products, arithmetic and copies ran while one was open for 8% -> 9% of each run, Pallas kernels for 44% -> 44%
where the time goes in v1:
time: 262 us; the launch traced here: 261 us
  Pallas kernels  134 us (51%)
  waiting for transfers between devices  48.2 us (18%)
  blocking collectives  27.2 us (10%)
  starting transfers between devices  22.2 us (8%)
  local copies, waits for them, and re-layouts  17.2 us (7%)
  other arithmetic  9.61 us (4%)
  between operations  3.11 us (1%)
    pallas_call x2, Pallas kernels, response_mid(): pl.pallas_call(functools.partial(resp_mid_kernel, first, handed), grid=(c...  67.2 us
    pallas_call x1, Pallas kernels, prompt_grad(): pl.pallas_call(functools.partial(prompt_grad_kernel, len(states)), in_spe...  23.8 us
    all_to_all x1, waiting for transfers between devices, shards(): start = lax.all_to_all(start, 'resp', 0, 0, axis_index_groups=inside)  21.1 us
    ppermute x2, waiting for transfers between devices, across(): return [part] + [lax.ppermute(part, 'resp', route) for route in routes]  18.5 us
    pallas_call x1, Pallas kernels, prompt_state(): pl.pallas_call(prompt_state_kernel, in_specs=[SMEM] + [pl.BlockSpec()] *...  14.6 us
    all_to_all x1, blocking collectives, sum_over_all(): mine = jnp.sum(lax.all_to_all(slices, axes, 0, 0), axis=0)  14.1 us
    all_to_all x1, blocking collectives, to_all(): return lax.all_to_all(copies, axes, 0, 0, axis_index_groups=groups)  13 us
    pallas_call x1, Pallas kernels, response_end(): pl.pallas_call(resp_end_kernel, grid=(G,), in_specs=[SMEM, SMEM, pl.Block...  11.1 us
  transfers between devices with their start and end apart: 8, of which 4 were waited for; matrix products, arithmetic and copies ran while one was open for 9% of the time, Pallas kernels for 44%

profile of v1, /device:TPU:0, one launch (start us, length us, event | category | flops | bytes accessed | tf_op | source)
XLA Modules:
  0.0 261.2 jit_solution(5831442254902785101)
XLA Ops:
  1.5 1.0 slice.32
  2.7 0.9 maximum_maximum_fusion
  3.6 1.0 broadcast_in_dim.43
  4.6 7.3 %all-to-all-start = ((bf16[8,384,128]{2,1,0:T(8,128)(2,1)}), bf16[8,384,128]{2,1,0:T(8,128)(2,1)}, u32[]{:S(2)}, u32[]{:S(2)}) async-start(bf16[8,384,128]{2,1,0:T(8,128)(2,1)} %broadcast_in_dim.43), calls=%async_computation | async-start | bytes 1572864 | tf_op jit(solution)/shard_map/all_to_all | solution.py:773
  11.9 0.1 slice.43
  12.1 0.1 copy.42
  12.3 1.3 copy-done
  13.6 1.3 fusion.5
  14.8 2.9 %collective-permute-start.2 = (bf16[128,2304]{1,0:T(8,128)(2,1)}, bf16[128,2304]{1,0:T(8,128)(2,1)}, u32[]{:S(2)}, u32[]{:S(2)}) collective-permute-start(bf16[128,2304]{1,0:T(8,128)(2,1)} %get-tuple-element.61), channel_id=1, source_target_pairs={{0,3},{1,0},{2,1},{3,2},{4,7},{5,4},{6,5},{7,6},{8,11},{9,8},{10,9... | collective-permute-start | bytes 1769480 | tf_op jit(solution)/shard_map/ppermute | solution.py:823
  17.8 1.1 collective-permute-start.1
  19.7 0.6 slice.40
  20.3 0.7 fusion.7
  21.0 0.6 pad.30.hp
  21.6 2.0 resp_steps.1
  23.7 8.5 %all-to-all-done = bf16[8,384,128]{2,1,0:T(8,128)(2,1)} async-done(((bf16[8,384,128]{2,1,0:T(8,128)(2,1)}), bf16[8,384,128]{2,1,0:T(8,128)(2,1)}, u32[]{:S(2)}, u32[]{:S(2)}) %all-to-all-start) | async-done | bytes 786464 | tf_op jit(solution)/shard_map/all_to_all | solution.py:773
  32.3 0.9 constant_dynamic-slice_fusion.5
  33.2 0.8 pad_convert_fusion.1.tail_c.tail_x.tail_b
  33.9 1.4 convert_reduce_fusion.4
  35.9 7.9 %resp_state.1 = (bf16[4,256,2048]{2,1,0:T(8,128)(2,1)}, bf16[256,8192]{1,0:T(8,128)(2,1)}, bf16[256,1024]{1,0:T(8,128)(2,1)}) custom-call(f32[1,1]{1,0:T(1,128)} %bitcast.8.adv.scale, bf16[256,10240]{1,0:T(8,128)(2,1)} %bitcast.56, f32[8,10240]{1,0:T(8,128)} %pad_convert_fusion.1.tail_c.tail_x.tail_b, f32[8,10240]{1,0:T(8,128)} %copy-done.2, ...), custom_call_target="tpu_custom_call" | custom-call | flops 1073741824 | bytes 14680064 | tf_op jit(solution)/shard_map/resp_state/pallas_call | solution.py:526
  43.8 5.2 %all-to-all-start.1 = ((bf16[4,256,2048]{2,1,0:T(8,128)(2,1)}), bf16[4,256,2048]{2,1,0:T(8,128)(2,1)}, u32[]{:S(2)}, u32[]{:S(2)}) async-start(bf16[4,256,2048]{2,1,0:T(8,128)(2,1)} %get-tuple-element.36), calls=%async_computation.1 | async-start | bytes 8388608 | tf_op jit(solution)/shard_map/all_to_all | solution.py:856
  49.1 0.8 constant_dynamic-slice_fusion.2
  49.9 0.6 pad_maximum_fusion.2.wb
  50.5 0.6 add_bitcast_fusion.place
  51.1 0.3 copy.37
  51.5 0.8 fusion.6.masks
  52.2 1.6 pad_maximum_fusion
  53.8 2.0 bitcast_dynamic-update-slice_fusion.2
  55.8 1.9 bitcast_dynamic-update-slice_fusion.1
  57.7 1.9 bitcast_dynamic-update-slice_fusion
  59.7 1.7 slice.45
  61.5 0.6 pad_maximum_fusion.1.halo
  62.1 14.6 %prompt_state.1 = (bf16[256,2048]{1,0:T(8,128)(2,1)}, f32[512,128]{1,0:T(8,128)}, f32[512,128]{1,0:T(8,128)}, f32[8,128]{1,0:T(8,128)}) custom-call(s32[1,2]{1,0:T(1,128)} %add_bitcast_fusion.place, bf16[512,2304]{1,0:T(8,128)(2,1)} %bitcast.26.v, f32[8,2304]{1,0:T(8,128)} %pad_maximum_fusion.1.halo, bf16[1024,128]{1,0:T(8,128)(2,1)} %bitcast.72, ...), custom_call_target="tpu_custom_call" | custom-call | flops 536870912 | bytes 4194304 | tf_op jit(solution)/shard_map/prompt_state/pallas_call | solution.py:705
  76.7 0.3 collective-permute-start.3
  77.1 0.7 broadcast_in_dim_reshape.3.skip
  77.9 1.0 copy.34
  78.9 33.6 %resp_mid.2 = (f32[8,8192]{1,0:T(8,128)}, f32[8,1024]{1,0:T(8,128)}, f32[256,1024]{1,0:T(8,128)}, f32[520,128]{1,0:T(8,128)}) custom-call(s32[1,1]{1,0:T(1,128)S(6)} %copy.51.len_ref, bf16[256,10240]{1,0:T(8,128)(2,1)} %bitcast.57, bf16[256,10240]{1,0:T(8,128)(2,1)} %bitcast.58, f32[8,10240]{1,0:T(8,128)} %pad_convert_fusion.1.tail_c.tail_x.tail_b, ...), custom_call_target="tpu_custom_call" | custom-call | flops 8589934592 | bytes 3145728 | tf_op jit(solution)/shard_map/resp_mid/pallas_call | solution.py:563
  112.5 11.6 %collective-permute-done.3.refs_1_ = bf16[256,2048]{1,0:T(8,128)(2,1)} collective-permute-done((bf16[256,2048]{1,0:T(8,128)(2,1)}, bf16[256,2048]{1,0:T(8,128)(2,1)}, u32[]{:S(2)}, u32[]{:S(2)}) %collective-permute-start.3) | collective-permute-done | bytes 1048608 | tf_op jit(solution)/shard_map/ppermute | solution.py:869
  124.1 5.6 %add_states.1 = (bf16[256,2048]{1,0:T(8,128)(2,1)}, bf16[4,256,2048]{2,1,0:T(8,128)(2,1)}) custom-call(bf16[4,256,2048]{2,1,0:T(8,128)(2,1)} %all-to-all-done.1.grads, bf16[256,2048]{1,0:T(8,128)(2,1)} %get-tuple-element.37.refs_0_, bf16[256,2048]{1,0:T(8,128)(2,1)} %collective-permute-done.3.refs_1_, f32[520,128]{1,0:T(8,128)} %get-tuple-element.39.refs_2_.refs_3_), custom_call_target="tpu_custom_call" | custom-call | flops 4194304 | bytes 11534336 | tf_op jit(solution)/shard_map/add_states/pallas_call | solution.py:687
  129.7 0.7 constant_dynamic-slice_fusion.dt_mine
  130.3 33.6 %resp_mid.3 = (f32[8,8192]{1,0:T(8,128)}, f32[8,1024]{1,0:T(8,128)}, f32[256,1024]{1,0:T(8,128)}, f32[520,128]{1,0:T(8,128)}, bf16[4,256,2048]{2,1,0:T(8,128)(2,1)}) custom-call(s32[1,1]{1,0:T(1,128)S(6)} %copy.51.len_ref, bf16[256,10240]{1,0:T(8,128)(2,1)} %bitcast.59, ...), custom_call_target="tpu_custom_call", output_to_operand_aliasing={{0}: (15, {}), {1}: (16, {}), {2}: (17, {}), {4}: (14, {})} | custom-call | flops 8589934592 | bytes 3145728 | tf_op jit(solution)/shard_map/resp_mid/pallas_call | solution.py:563
  164.0 5.4 %all-to-all-start.2 = ((bf16[4,256,2048]{2,1,0:T(8,128)(2,1)}), bf16[4,256,2048]{2,1,0:T(8,128)(2,1)}, u32[]{:S(2)}, u32[]{:S(2)}) async-start(bf16[4,256,2048]{2,1,0:T(8,128)(2,1)} %get-tuple-element.44), calls=%async_computation.2 | async-start | bytes 8388608 | tf_op jit(solution)/shard_map/all_to_all | solution.py:877
  169.4 6.9 %collective-permute-done.4.refs_1_ = bf16[256,2048]{1,0:T(8,128)(2,1)} collective-permute-done((bf16[256,2048]{1,0:T(8,128)(2,1)}, bf16[256,2048]{1,0:T(8,128)(2,1)}, u32[]{:S(2)}, u32[]{:S(2)}) %collective-permute-start.4) | collective-permute-done | bytes 1048608 | tf_op jit(solution)/shard_map/ppermute | solution.py:869
  176.3 23.8 %prompt_grad.1 = (f32[8,2304]{1,0:T(8,128)}, f32[8,128]{1,0:T(8,128)}) custom-call(s32[1,2]{1,0:T(1,128)} %add_bitcast_fusion.place, bf16[512,2304]{1,0:T(8,128)(2,1)} %bitcast.26.v, f32[8,2304]{1,0:T(8,128)} %pad_maximum_fusion.1.halo, bf16[512,128]{1,0:T(8,128)(2,1)} %constant_dynamic-slice_fusion.dt_mine, f32[512,8]{1,0:T(8,128)} %fusion.6.masks, ...), custom_call_target="tpu_custom_call" | custom-call | flops 274877906944 | bytes 8388608 | tf_op jit(solution)/shard_map/prompt_grad/pallas_call | solution.py:733
  200.0 21.1 %all-to-all-done.2.start = bf16[4,256,2048]{2,1,0:T(8,128)(2,1)} async-done(((bf16[4,256,2048]{2,1,0:T(8,128)(2,1)}), bf16[4,256,2048]{2,1,0:T(8,128)(2,1)}, u32[]{:S(2)}, u32[]{:S(2)}) %all-to-all-start.2) | async-done | bytes 4194336 | tf_op jit(solution)/shard_map/all_to_all | solution.py:877
  221.2 11.1 %resp_end.1 = f32[64,8,128]{2,1,0:T(8,128)} custom-call(s32[1,2]{1,0:T(1,128)} %add_bitcast_fusion.place, f32[1,1]{1,0:T(1,128)} %bitcast.8.adv.scale, bf16[256,10240]{1,0:T(8,128)(2,1)} %bitcast.61, f32[8,10240]{1,0:T(8,128)} %pad_convert_fusion.1.tail_c.tail_x.tail_b, f32[8,10240]{1,0:T(8,128)} %copy-done.2, bf16[256,1024]{1,0:T(8,128)(2,1)} %get-tuple-element.31.c_act, ...), custom_call_target="tpu_custom_call" | custom-call | flops 2147483648 | bytes 12582912 | tf_op jit(solution)/shard_map/resp_end/pallas_call | solution.py:639
  232.2 14.1 %all_to_all.25 = f32[32,2,8,128]{3,2,1,0:T(8,128)S(1)} all-to-all(f32[32,2,8,128]{3,2,1,0:T(8,128)} %bitcast.74), channel_id=1, replica_groups=mesh['group'=4,'resp'=8] {'group','resp'}, dimensions={0} | all-to-all | bytes 524288 | tf_op jit(solution)/shard_map/all_to_all | solution.py:778
  246.4 13.0 %all_to_all.26 = f32[32,2,8,128]{3,2,1,0:T(8,128)} all-to-all(f32[32,2,8,128]{3,2,1,0:T(8,128)S(1)} %broadcast_in_dim.49), channel_id=1, replica_groups=mesh['group'=4,'resp'=8] {'group','resp'}, dimensions={0} | all-to-all | bytes 524288 | tf_op jit(solution)/shard_map/all_to_all | solution.py:773
  259.5 1.8 unpack.1
  (51 shorter events, 1.0 us)
Async XLA Ops:
  0.6 11.2 %copy-start.3 = (bf16[1,128,10240]{2,1,0:T(8,128)(2,1)S(1)}, bf16[1,128,10240]{2,1,0:T(8,128)(2,1)}, u32[]{:S(2)}) copy-start(bf16[1,128,10240]{2,1,0:T(8,128)(2,1)} %param.11) | copy-start | bytes 7864324
  4.6 27.7 %all-to-all-start = ((bf16[8,384,128]{2,1,0:T(8,128)(2,1)}), bf16[8,384,128]{2,1,0:T(8,128)(2,1)}, u32[]{:S(2)}, u32[]{:S(2)}) async-start(bf16[8,384,128]{2,1,0:T(8,128)(2,1)} %broadcast_in_dim.43), calls=%async_computation | async-start | bytes 1572864 | tf_op jit(solution)/shard_map/all_to_all | solution.py:773
  12.2 1.3 copy-start
  12.2 7.3 %copy-start.9 = (s32[1,4]{1,0:T(1,128)S(1)}, s32[1,4]{1,0:T(1,128)}, u32[]{:S(2)}) copy-start(s32[1,4]{1,0:T(1,128)} %param.13) | copy-start | bytes 52
  12.2 8.7 %copy-start.8 = (f32[3,128]{1,0:T(4,128)S(1)}, f32[3,128]{1,0:T(4,128)}, u32[]{:S(2)}) copy-start(f32[3,128]{1,0:T(4,128)} %param.21) | copy-start | bytes 4612
  12.3 11.3 %copy-start.5 = (f32[4,10240]{1,0:T(4,128)S(1)}, f32[4,10240]{1,0:T(4,128)}, u32[]{:S(2)}) copy-start(f32[4,10240]{1,0:T(4,128)} %param.19) | copy-start | bytes 491524
  12.3 11.3 %copy-start.7 = (f32[10240]{0:T(1024)S(1)}, f32[10240]{0:T(1024)}, u32[]{:S(2)}) copy-start(f32[10240]{0:T(1024)} %param.20) | copy-start | bytes 122884
  14.8 42.9 %collective-permute-start.2 = (bf16[128,2304]{1,0:T(8,128)(2,1)}, bf16[128,2304]{1,0:T(8,128)(2,1)}, u32[]{:S(2)}, u32[]{:S(2)}) collective-permute-start(bf16[128,2304]{1,0:T(8,128)(2,1)} %get-tuple-element.61), channel_id=1, source_target_pairs={{0,3},{1,0},{2,1},{3,2},{4,7},{5,4},{6,5},{7,6},{8,11},{9,8},{10,9... | collective-permute-start | bytes 1769480 | tf_op jit(solution)/shard_map/ppermute | solution.py:823
  17.8 36.1 %collective-permute-start = (bf16[128,2304]{1,0:T(8,128)(2,1)}, bf16[128,2304]{1,0:T(8,128)(2,1)}, u32[]{:S(2)}, u32[]{:S(2)}) collective-permute-start(bf16[128,2304]{1,0:T(8,128)(2,1)} %get-tuple-element.62), channel_id=1, source_target_pairs={{0,1},{1,2},{2,3},{3,0},{4,5},{5,6},{6,7},{7,4},{8,9},{9,10},{10,1... | collective-permute-start | bytes 1769480 | tf_op jit(solution)/shard_map/ppermute | solution.py:823
  17.8 38.1 %collective-permute-start.1 = (bf16[128,2304]{1,0:T(8,128)(2,1)}, bf16[128,2304]{1,0:T(8,128)(2,1)}, u32[]{:S(2)}, u32[]{:S(2)}) collective-permute-start(bf16[128,2304]{1,0:T(8,128)(2,1)} %get-tuple-element.63), channel_id=1, source_target_pairs={{0,2},{1,3},{2,0},{3,1},{4,6},{5,7},{6,4},{7,5},{8,10},{9,11},{10,... | collective-permute-start | bytes 1769480 | tf_op jit(solution)/shard_map/ppermute | solution.py:823
  23.7 12.2 %copy-start.2 = (f32[8,10240]{1,0:T(8,128)}, f32[8,10240]{1,0:T(8,128)S(1)}, u32[]{:S(2)}) copy-start(f32[8,10240]{1,0:T(8,128)S(1)} %select_maximum_fusion.wb_c.wb_x.wb_b) | copy-start | bytes 983044
  43.8 8.4 %copy-start.1 = (bf16[16,4,8,2048]{3,2,0,1:T(8,128)(2,1)S(1)}, bf16[16,4,8,2048]{3,2,0,1:T(8,128)(2,1)}, u32[]{:S(2)}) copy-start(bf16[16,4,8,2048]{3,2,0,1:T(8,128)(2,1)} %copy-done) | copy-start | bytes 6291460
  43.8 80.3 %all-to-all-start.1 = ((bf16[4,256,2048]{2,1,0:T(8,128)(2,1)}), bf16[4,256,2048]{2,1,0:T(8,128)(2,1)}, u32[]{:S(2)}, u32[]{:S(2)}) async-start(bf16[4,256,2048]{2,1,0:T(8,128)(2,1)} %get-tuple-element.36), calls=%async_computation.1 | async-start | bytes 8388608 | tf_op jit(solution)/shard_map/all_to_all | solution.py:856
  59.7 18.1 %copy-start.6 = (f32[256,128]{1,0:T(8,128)S(1)}, f32[256,128]{1,0:T(8,128)}, u32[]{:S(2)}) copy-start(f32[256,128]{1,0:T(8,128)} %get-tuple-element.34.cum) | copy-start | bytes 393220
  76.7 47.4 %collective-permute-start.3 = (bf16[256,2048]{1,0:T(8,128)(2,1)}, bf16[256,2048]{1,0:T(8,128)(2,1)}, u32[]{:S(2)}, u32[]{:S(2)}) collective-permute-start(bf16[256,2048]{1,0:T(8,128)(2,1)} %get-tuple-element.37.refs_0_), channel_id=1, source_target_pairs={{0,4},{1,5},{2,6},{3,7},{4,0},{5,1},{6,2},{7,3},{8,12},{9,13},{10,... | collective-permute-start | bytes 3145736 | tf_op jit(solution)/shard_map/ppermute | solution.py:869
  124.1 5.6 %copy-start.4 = (bf16[8,128,128]{2,1,0:T(8,128)(2,1)S(1)}, bf16[8,128,128]{2,1,0:T(8,128)(2,1)}, u32[]{:S(2)}) copy-start(bf16[8,128,128]{2,1,0:T(8,128)(2,1)} %slice.45) | copy-start | bytes 786436
  129.7 46.6 %collective-permute-start.4 = (bf16[256,2048]{1,0:T(8,128)(2,1)}, bf16[256,2048]{1,0:T(8,128)(2,1)}, u32[]{:S(2)}, u32[]{:S(2)}) collective-permute-start(bf16[256,2048]{1,0:T(8,128)(2,1)} %get-tuple-element.51.refs_0_), channel_id=1, source_target_pairs={{0,4},{1,5},{2,6},{3,7},{4,0},{5,1},{6,2},{7,3},{8,12},{9,13},{10,... | collective-permute-start | bytes 3145736 | tf_op jit(solution)/shard_map/ppermute | solution.py:869
  164.0 57.2 %all-to-all-start.2 = ((bf16[4,256,2048]{2,1,0:T(8,128)(2,1)}), bf16[4,256,2048]{2,1,0:T(8,128)(2,1)}, u32[]{:S(2)}, u32[]{:S(2)}) async-start(bf16[4,256,2048]{2,1,0:T(8,128)(2,1)} %get-tuple-element.44), calls=%async_computation.2 | async-start | bytes 8388608 | tf_op jit(solution)/shard_map/all_to_all | solution.py:877

commit v2 on v1

--- a/solution.py
+++ b/solution.py
@@ -478,15 +478,18 @@
     grad_h[1:2] = d_bias + behind * beyond[1:2]
 
 
-def add_kernel(count, grads, *refs):
-    starts, (grad_sum, start) = refs[:count], refs[count + 1 :]
-    grad_sum[...] = jnp.sum(grads[...].astype(f32), axis=0).astype(bf16)
-    total = starts[0][...].astype(f32)
-    for k in range(1, count):
-        total = total + starts[k][...].astype(f32)
+def add_kernel(terms, *refs):
+    out = refs[-1]
+    total = None
+    for k in range(terms):
+        part = refs[k][...].astype(f32)
+        total = part if total is None else total + part
     total = total.astype(bf16)
-    for k in range(start.shape[0]):
-        start[k] = total
+    if out.ndim == 2:
+        out[...] = total
+    else:
+        for k in range(out.shape[0]):
+            out[k] = total
 
 
 def params(*semantics):
@@ -679,23 +682,31 @@
     )(packed)
 
 
-def add_states(grads, starts, earlier_out):
-    copies, rows, width = grads.shape
+def add_states(terms, earlier_out, copies=0):
+    rows, width = terms[0].shape
     part = rows // 4
     one = pl.BlockSpec((part, width), lambda i: (i, 0))
+    if isinstance(terms, list):
+        blocks = [one] * len(terms)
+    else:
+        blocks = [
+            pl.BlockSpec((None, part, width), lambda i, k=k: (k, i, 0))
+            for k in range(terms.shape[0])
+        ]
+        terms = [terms] * terms.shape[0]
     many = pl.BlockSpec((copies, part, width), lambda i: (0, i, 0))
     return pl.pallas_call(
-        functools.partial(add_kernel, len(starts)),
+        functools.partial(add_kernel, len(terms)),
         grid=(4,),
-        in_specs=[many] + [one] * len(starts) + [pl.BlockSpec(memory_space=pl.ANY)],
-        out_specs=[one, many],
-        out_shape=(sds((rows, width), bf16), sds(grads.shape, bf16)),
+        in_specs=blocks + [pl.BlockSpec(memory_space=pl.ANY)],
+        out_specs=many if copies else one,
+        out_shape=sds((copies, rows, width) if copies else (rows, width), bf16),
         compiler_params=params("arbitrary"),
         cost_estimate=pl.CostEstimate(
-            flops=8 * rows * width, bytes_accessed=22 * rows * width, transcendentals=0
+            flops=8 * rows * width, bytes_accessed=12 * rows * width, transcendentals=0
         ),
         name="add_states",
-    )(grads, *starts, earlier_out)
+    )(*terms, earlier_out)
 
 
 def prompt_state(place, v, halo, dt_all, masks, wb, hp):
@@ -870,10 +881,11 @@
 
     part, weight, p_step, beyond = prompt_state(place, v, halo, dt_all, masks, wb_mine, hp)
     parts_of_start = across(part)
-    grads = mid(0, 2, weight)
-    part, start = add_states(d_states, parts_of_start, grads[3])
+    grads = mid(0, 1, weight)
+    part = add_states(d_states, grads[3])
     parts_of_grad = across(part)
-    grad_x, grad_b, dc, sums, start = mid(2, 2, start, grads, handed=True)
+    grad_x, grad_b, dc, sums = mid(1, G - 1, part, grads)
+    start = add_states(parts_of_start, sums, copies=G)
     start = lax.all_to_all(start, "resp", 0, 0, axis_index_groups=inside)
     p_grad, p_heads = prompt_grad(
         place, v, halo, dt_mine, masks, wb_mine, hp, weight, p_step, beyond, parts_of_grad, sums

time: 262 us -> 268 us (1.023)
  waiting for transfers between devices: 48.2 us -> 51.3 us
    all_to_all x1, waiting for transfers between devices: 0.01 us -> 19.6 us  [shards(): d_states = lax.all_to_all(d_states, 'resp', 0, 0, axis_index_groups=inside)]
    ppermute x2, waiting for transfers between devices: 18.5 us -> 0.01 us  [across(): return [part] + [lax.ppermute(part, 'resp', route) for route in routes]]
    pallas_call x1 -> x2, Pallas kernels: 5.56 us -> 8.41 us  [add_states(): pl.pallas_call(functools.partial(add_kernel, len(terms)), grid=(4,), in_s...]
  transfers between devices with their start and end apart: 8 -> 8, of which waited for: 4 -> 3; matrix products, arithmetic and copies ran while one was open for 9% -> 8% of each run, Pallas kernels for 44% -> 46%
where the time goes in v2:
time: 268 us; the launch traced here: 267 us
  Pallas kernels  135 us (50%)
  waiting for transfers between devices  51.3 us (19%)
  blocking collectives  28.5 us (11%)
  starting transfers between devices  21.7 us (8%)
  local copies, waits for them, and re-layouts  17.1 us (6%)
  other arithmetic  9.58 us (4%)
  between operations  3.11 us (1%)
    pallas_call x2, Pallas kernels, response_mid(): pl.pallas_call(functools.partial(resp_mid_kernel, first, handed), grid=(c...  65.9 us
    pallas_call x1, Pallas kernels, prompt_grad(): pl.pallas_call(functools.partial(prompt_grad_kernel, len(states)), in_spe...  23.8 us
    all_to_all x1, waiting for transfers between devices, shards(): start = lax.all_to_all(start, 'resp', 0, 0, axis_index_groups=inside)  23.1 us
    all_to_all x1, waiting for transfers between devices, shards(): d_states = lax.all_to_all(d_states, 'resp', 0, 0, axis_index_groups=inside)  19.6 us
    all_to_all x1, blocking collectives, sum_over_all(): mine = jnp.sum(lax.all_to_all(slices, axes, 0, 0), axis=0)  15.5 us
    pallas_call x1, Pallas kernels, prompt_state(): pl.pallas_call(prompt_state_kernel, in_specs=[SMEM] + [pl.BlockSpec()] *...  14.6 us
    all_to_all x1, blocking collectives, to_all(): return lax.all_to_all(copies, axes, 0, 0, axis_index_groups=groups)  13 us
    pallas_call x1, Pallas kernels, response_end(): pl.pallas_call(resp_end_kernel, grid=(G,), in_specs=[SMEM, SMEM, pl.Block...  11 us
  transfers between devices with their start and end apart: 8, of which 3 were waited for; matrix products, arithmetic and copies ran while one was open for 8% of the time, Pallas kernels for 46%

profile of v2, /device:TPU:0, one launch (start us, length us, event | category | flops | bytes accessed | tf_op | source)
XLA Modules:
  0.0 266.7 jit_solution(16009418137596652110)
XLA Ops:
  1.5 1.0 slice.32
  2.7 0.9 maximum_maximum_fusion
  3.6 1.0 broadcast_in_dim.43
  4.6 7.3 %all-to-all-start = ((bf16[8,384,128]{2,1,0:T(8,128)(2,1)}), bf16[8,384,128]{2,1,0:T(8,128)(2,1)}, u32[]{:S(2)}, u32[]{:S(2)}) async-start(bf16[8,384,128]{2,1,0:T(8,128)(2,1)} %broadcast_in_dim.43), calls=%async_computation | async-start | bytes 1572864 | tf_op jit(solution)/shard_map/all_to_all | solution.py:784
  11.9 0.1 slice.43
  12.1 0.1 copy.41
  12.3 1.3 copy-done
  13.6 1.2 fusion.5
  14.8 2.9 %collective-permute-start.2 = (bf16[128,2304]{1,0:T(8,128)(2,1)}, bf16[128,2304]{1,0:T(8,128)(2,1)}, u32[]{:S(2)}, u32[]{:S(2)}) collective-permute-start(bf16[128,2304]{1,0:T(8,128)(2,1)} %get-tuple-element.55), channel_id=1, source_target_pairs={{0,3},{1,0},{2,1},{3,2},{4,7},{5,4},{6,5},{7,6},{8,11},{9,8},{10,9... | collective-permute-start | bytes 1769480 | tf_op jit(solution)/shard_map/ppermute | solution.py:834
  17.7 1.1 collective-permute-start.1
  19.5 0.1 convert_reduce_fusion.3
  19.7 0.6 slice.39
  20.2 0.7 fusion.7
  21.0 0.6 pad.30.hp
  21.6 2.0 resp_steps.1
  23.7 8.6 %all-to-all-done = bf16[8,384,128]{2,1,0:T(8,128)(2,1)} async-done(((bf16[8,384,128]{2,1,0:T(8,128)(2,1)}), bf16[8,384,128]{2,1,0:T(8,128)(2,1)}, u32[]{:S(2)}, u32[]{:S(2)}) %all-to-all-start) | async-done | bytes 786464 | tf_op jit(solution)/shard_map/all_to_all | solution.py:784
  32.3 0.9 constant_dynamic-slice_fusion.5
  33.2 0.8 pad_convert_fusion.1.tail_c.tail_x.tail_b
  34.0 1.4 convert_reduce_fusion.4
  36.0 7.9 %resp_state.1 = (bf16[4,256,2048]{2,1,0:T(8,128)(2,1)}, bf16[256,8192]{1,0:T(8,128)(2,1)}, bf16[256,1024]{1,0:T(8,128)(2,1)}) custom-call(f32[1,1]{1,0:T(1,128)} %bitcast.8.adv.scale, bf16[256,10240]{1,0:T(8,128)(2,1)} %bitcast.56, f32[8,10240]{1,0:T(8,128)} %pad_convert_fusion.1.tail_c.tail_x.tail_b, f32[8,10240]{1,0:T(8,128)} %copy-done.2, ...), custom_call_target="tpu_custom_call" | custom-call | flops 1073741824 | bytes 14680064 | tf_op jit(solution)/shard_map/resp_state/pallas_call | solution.py:529
  43.9 5.3 %all-to-all-start.1 = ((bf16[4,256,2048]{2,1,0:T(8,128)(2,1)}), bf16[4,256,2048]{2,1,0:T(8,128)(2,1)}, u32[]{:S(2)}, u32[]{:S(2)}) async-start(bf16[4,256,2048]{2,1,0:T(8,128)(2,1)} %get-tuple-element.34), calls=%async_computation.1 | async-start | bytes 8388608 | tf_op jit(solution)/shard_map/all_to_all | solution.py:867
  49.2 0.9 constant_dynamic-slice_fusion.2
  50.1 0.6 pad_maximum_fusion.2.wb
  50.7 0.7 add_bitcast_fusion.place
  51.4 0.7 broadcast_in_dim_reshape.3.skip
  52.2 0.3 copy.34
  52.6 1.0 copy.36
  53.6 0.7 fusion.6.masks
  54.3 1.6 pad_maximum_fusion
  55.9 1.9 bitcast_dynamic-update-slice_fusion.2
  57.8 1.9 bitcast_dynamic-update-slice_fusion.1
  59.7 1.9 bitcast_dynamic-update-slice_fusion
  61.7 1.7 slice.45
  63.5 0.6 pad_maximum_fusion.1.halo
  64.1 14.6 %prompt_state.1 = (bf16[256,2048]{1,0:T(8,128)(2,1)}, f32[512,128]{1,0:T(8,128)}, f32[512,128]{1,0:T(8,128)}, f32[8,128]{1,0:T(8,128)}) custom-call(s32[1,2]{1,0:T(1,128)} %add_bitcast_fusion.place, bf16[512,2304]{1,0:T(8,128)(2,1)} %bitcast.22.v, f32[8,2304]{1,0:T(8,128)} %pad_maximum_fusion.1.halo, bf16[1024,128]{1,0:T(8,128)(2,1)} %bitcast.72, ...), custom_call_target="tpu_custom_call" | custom-call | flops 536870912 | bytes 4194304 | tf_op jit(solution)/shard_map/prompt_state/pallas_call | solution.py:716
  78.7 17.1 %resp_mid.2 = (f32[8,8192]{1,0:T(8,128)}, f32[8,1024]{1,0:T(8,128)}, f32[256,1024]{1,0:T(8,128)}, f32[520,128]{1,0:T(8,128)}) custom-call(s32[1,1]{1,0:T(1,128)S(6)} %copy.49.len_ref, bf16[256,10240]{1,0:T(8,128)(2,1)} %bitcast.57, bf16[256,10240]{1,0:T(8,128)(2,1)} %bitcast.58, f32[8,10240]{1,0:T(8,128)} %pad_convert_fusion.1.tail_c.tail_x.tail_b, ...), custom_call_target="tpu_custom_call" | custom-call | flops 8589934592 | bytes 3145728 | tf_op jit(solution)/shard_map/resp_mid/pallas_call | solution.py:566
  95.8 19.6 %all-to-all-done.1.refs_0_.refs_1_.refs_2_.refs_3_ = bf16[4,256,2048]{2,1,0:T(8,128)(2,1)} async-done(((bf16[4,256,2048]{2,1,0:T(8,128)(2,1)}), bf16[4,256,2048]{2,1,0:T(8,128)(2,1)}, u32[]{:S(2)}, u32[]{:S(2)}) %all-to-all-start.1) | async-done | bytes 4194336 | tf_op jit(solution)/shard_map/all_to_all | solution.py:867
  115.5 4.2 %add_states.2.earlier_out.refs_0_ = bf16[256,2048]{1,0:T(8,128)(2,1)} custom-call(bf16[4,256,2048]{2,1,0:T(8,128)(2,1)} %all-to-all-done.1.refs_0_.refs_1_.refs_2_.refs_3_, bf16[4,256,2048]{2,1,0:T(8,128)(2,1)} %all-to-all-done.1.refs_0_.refs_1_.refs_2_.refs_3_, bf16[4,256,2048]{2,1,0:T(8,128)(2,1)} %all-to-all-done.1.refs_0_.refs_1_.refs_2_.refs_3_, ...), custom_call_target="tpu_custom_call" | custom-call | flops 4194304 | bytes 6291456 | tf_op jit(solution)/shard_map/add_states/pallas_call | solution.py:698
  119.7 0.7 constant_dynamic-slice_fusion.dt_mine
  120.3 48.8 %resp_mid.3 = (f32[8,8192]{1,0:T(8,128)}, f32[8,1024]{1,0:T(8,128)}, f32[256,1024]{1,0:T(8,128)}, f32[520,128]{1,0:T(8,128)}) custom-call(s32[1,1]{1,0:T(1,128)S(6)} %copy.49.len_ref, bf16[256,10240]{1,0:T(8,128)(2,1)} %bitcast.59, bf16[256,10240]{1,0:T(8,128)(2,1)} %bitcast.60, ...), custom_call_target="tpu_custom_call", output_to_operand_aliasing={{0}: (15, {}), {1}: (16, {}), {2}: (17, {})} | custom-call | flops 8589934592 | bytes 3145728 | tf_op jit(solution)/shard_map/resp_mid/pallas_call | solution.py:566
  169.1 4.2 %add_states.3 = bf16[4,256,2048]{2,1,0:T(8,128)(2,1)} custom-call(bf16[256,2048]{1,0:T(8,128)(2,1)} %get-tuple-element.30.refs_0_, bf16[256,2048]{1,0:T(8,128)(2,1)} %collective-permute-done.3.refs_1_, f32[520,128]{1,0:T(8,128)} %get-tuple-element.40.refs_2_.sums), custom_call_target="tpu_custom_call" | custom-call | flops 4194304 | bytes 6291456 | tf_op jit(solution)/shard_map/add_states/pallas_call | solution.py:698
  173.3 5.1 %all-to-all-start.2 = ((bf16[4,256,2048]{2,1,0:T(8,128)(2,1)}), bf16[4,256,2048]{2,1,0:T(8,128)(2,1)}, u32[]{:S(2)}, u32[]{:S(2)}) async-start(bf16[4,256,2048]{2,1,0:T(8,128)(2,1)} %add_states.3), calls=%async_computation.2 | async-start | bytes 8388608 | tf_op jit(solution)/shard_map/all_to_all | solution.py:889
  178.5 23.8 %prompt_grad.1 = (f32[8,2304]{1,0:T(8,128)}, f32[8,128]{1,0:T(8,128)}) custom-call(s32[1,2]{1,0:T(1,128)} %add_bitcast_fusion.place, bf16[512,2304]{1,0:T(8,128)(2,1)} %bitcast.22.v, f32[8,2304]{1,0:T(8,128)} %pad_maximum_fusion.1.halo, bf16[512,128]{1,0:T(8,128)(2,1)} %constant_dynamic-slice_fusion.dt_mine, f32[512,8]{1,0:T(8,128)} %fusion.6.masks, ...), custom_call_target="tpu_custom_call" | custom-call | flops 274877906944 | bytes 8388608 | tf_op jit(solution)/shard_map/prompt_grad/pallas_call | solution.py:744
  202.3 23.1 %all-to-all-done.2.start = bf16[4,256,2048]{2,1,0:T(8,128)(2,1)} async-done(((bf16[4,256,2048]{2,1,0:T(8,128)(2,1)}), bf16[4,256,2048]{2,1,0:T(8,128)(2,1)}, u32[]{:S(2)}, u32[]{:S(2)}) %all-to-all-start.2) | async-done | bytes 4194336 | tf_op jit(solution)/shard_map/all_to_all | solution.py:889
  225.3 11.0 %resp_end.1 = f32[64,8,128]{2,1,0:T(8,128)} custom-call(s32[1,2]{1,0:T(1,128)} %add_bitcast_fusion.place, f32[1,1]{1,0:T(1,128)} %bitcast.8.adv.scale, bf16[256,10240]{1,0:T(8,128)(2,1)} %bitcast.61, f32[8,10240]{1,0:T(8,128)} %pad_convert_fusion.1.tail_c.tail_x.tail_b, f32[8,10240]{1,0:T(8,128)} %copy-done.2, bf16[256,1024]{1,0:T(8,128)(2,1)} %get-tuple-element.28.c_act, ...), custom_call_target="tpu_custom_call" | custom-call | flops 2147483648 | bytes 12582912 | tf_op jit(solution)/shard_map/resp_end/pallas_call | solution.py:642
  236.3 15.5 %all_to_all.25 = f32[32,2,8,128]{3,2,1,0:T(8,128)S(1)} all-to-all(f32[32,2,8,128]{3,2,1,0:T(8,128)} %bitcast.74), channel_id=1, replica_groups=mesh['group'=4,'resp'=8] {'group','resp'}, dimensions={0} | all-to-all | bytes 524288 | tf_op jit(solution)/shard_map/all_to_all | solution.py:789
  251.9 13.0 %all_to_all.26 = f32[32,2,8,128]{3,2,1,0:T(8,128)} all-to-all(f32[32,2,8,128]{3,2,1,0:T(8,128)S(1)} %broadcast_in_dim.49), channel_id=1, replica_groups=mesh['group'=4,'resp'=8] {'group','resp'}, dimensions={0} | all-to-all | bytes 524288 | tf_op jit(solution)/shard_map/all_to_all | solution.py:784
  264.9 1.8 unpack.1
  (52 shorter events, 0.9 us)
Async XLA Ops:
  0.6 11.3 %copy-start.3 = (bf16[1,128,10240]{2,1,0:T(8,128)(2,1)S(1)}, bf16[1,128,10240]{2,1,0:T(8,128)(2,1)}, u32[]{:S(2)}) copy-start(bf16[1,128,10240]{2,1,0:T(8,128)(2,1)} %param.11) | copy-start | bytes 7864324
  4.6 27.7 %all-to-all-start = ((bf16[8,384,128]{2,1,0:T(8,128)(2,1)}), bf16[8,384,128]{2,1,0:T(8,128)(2,1)}, u32[]{:S(2)}, u32[]{:S(2)}) async-start(bf16[8,384,128]{2,1,0:T(8,128)(2,1)} %broadcast_in_dim.43), calls=%async_computation | async-start | bytes 1572864 | tf_op jit(solution)/shard_map/all_to_all | solution.py:784
  12.2 1.3 copy-start
  12.3 7.3 %copy-start.9 = (s32[1,4]{1,0:T(1,128)S(1)}, s32[1,4]{1,0:T(1,128)}, u32[]{:S(2)}) copy-start(s32[1,4]{1,0:T(1,128)} %param.13) | copy-start | bytes 52
  12.3 8.7 %copy-start.8 = (f32[3,128]{1,0:T(4,128)S(1)}, f32[3,128]{1,0:T(4,128)}, u32[]{:S(2)}) copy-start(f32[3,128]{1,0:T(4,128)} %param.21) | copy-start | bytes 4612
  12.3 11.3 %copy-start.5 = (f32[4,10240]{1,0:T(4,128)S(1)}, f32[4,10240]{1,0:T(4,128)}, u32[]{:S(2)}) copy-start(f32[4,10240]{1,0:T(4,128)} %param.19) | copy-start | bytes 491524
  12.3 11.3 %copy-start.7 = (f32[10240]{0:T(1024)S(1)}, f32[10240]{0:T(1024)}, u32[]{:S(2)}) copy-start(f32[10240]{0:T(1024)} %param.20) | copy-start | bytes 122884
  14.8 44.9 %collective-permute-start.2 = (bf16[128,2304]{1,0:T(8,128)(2,1)}, bf16[128,2304]{1,0:T(8,128)(2,1)}, u32[]{:S(2)}, u32[]{:S(2)}) collective-permute-start(bf16[128,2304]{1,0:T(8,128)(2,1)} %get-tuple-element.55), channel_id=1, source_target_pairs={{0,3},{1,0},{2,1},{3,2},{4,7},{5,4},{6,5},{7,6},{8,11},{9,8},{10,9... | collective-permute-start | bytes 1769480 | tf_op jit(solution)/shard_map/ppermute | solution.py:834
  17.7 38.1 %collective-permute-start = (bf16[128,2304]{1,0:T(8,128)(2,1)}, bf16[128,2304]{1,0:T(8,128)(2,1)}, u32[]{:S(2)}, u32[]{:S(2)}) collective-permute-start(bf16[128,2304]{1,0:T(8,128)(2,1)} %get-tuple-element.56), channel_id=1, source_target_pairs={{0,1},{1,2},{2,3},{3,0},{4,5},{5,6},{6,7},{7,4},{8,9},{9,10},{10,1... | collective-permute-start | bytes 1769480 | tf_op jit(solution)/shard_map/ppermute | solution.py:834
  17.7 40.1 %collective-permute-start.1 = (bf16[128,2304]{1,0:T(8,128)(2,1)}, bf16[128,2304]{1,0:T(8,128)(2,1)}, u32[]{:S(2)}, u32[]{:S(2)}) collective-permute-start(bf16[128,2304]{1,0:T(8,128)(2,1)} %get-tuple-element.57), channel_id=1, source_target_pairs={{0,2},{1,3},{2,0},{3,1},{4,6},{5,7},{6,4},{7,5},{8,10},{9,11},{10,... | collective-permute-start | bytes 1769480 | tf_op jit(solution)/shard_map/ppermute | solution.py:834
  23.7 12.3 %copy-start.2 = (f32[8,10240]{1,0:T(8,128)}, f32[8,10240]{1,0:T(8,128)S(1)}, u32[]{:S(2)}) copy-start(f32[8,10240]{1,0:T(8,128)S(1)} %select_maximum_fusion.wb_c.wb_x.wb_b) | copy-start | bytes 983044
  43.9 8.5 %copy-start.6 = (f32[256,128]{1,0:T(8,128)S(1)}, f32[256,128]{1,0:T(8,128)}, u32[]{:S(2)}) copy-start(f32[256,128]{1,0:T(8,128)} %get-tuple-element.32.cum) | copy-start | bytes 393220
  43.9 10.4 %copy-start.1 = (bf16[16,4,8,2048]{3,2,0,1:T(8,128)(2,1)S(1)}, bf16[16,4,8,2048]{3,2,0,1:T(8,128)(2,1)}, u32[]{:S(2)}) copy-start(bf16[16,4,8,2048]{3,2,0,1:T(8,128)(2,1)} %copy-done) | copy-start | bytes 6291460
  43.9 71.5 %all-to-all-start.1 = ((bf16[4,256,2048]{2,1,0:T(8,128)(2,1)}), bf16[4,256,2048]{2,1,0:T(8,128)(2,1)}, u32[]{:S(2)}, u32[]{:S(2)}) async-start(bf16[4,256,2048]{2,1,0:T(8,128)(2,1)} %get-tuple-element.34), calls=%async_computation.1 | async-start | bytes 8388608 | tf_op jit(solution)/shard_map/all_to_all | solution.py:867
  78.7 90.4 %collective-permute-start.3 = (bf16[256,2048]{1,0:T(8,128)(2,1)}, bf16[256,2048]{1,0:T(8,128)(2,1)}, u32[]{:S(2)}, u32[]{:S(2)}) collective-permute-start(bf16[256,2048]{1,0:T(8,128)(2,1)} %get-tuple-element.30.refs_0_), channel_id=1, source_target_pairs={{0,4},{1,5},{2,6},{3,7},{4,0},{5,1},{6,2},{7,3},{8,12},{9,13},{10,... | collective-permute-start | bytes 3145736 | tf_op jit(solution)/shard_map/ppermute | solution.py:880
  115.5 4.2 %copy-start.4 = (bf16[8,128,128]{2,1,0:T(8,128)(2,1)S(1)}, bf16[8,128,128]{2,1,0:T(8,128)(2,1)}, u32[]{:S(2)}) copy-start(bf16[8,128,128]{2,1,0:T(8,128)(2,1)} %slice.45) | copy-start | bytes 786436
  119.7 58.8 %collective-permute-start.4 = (bf16[256,2048]{1,0:T(8,128)(2,1)}, bf16[256,2048]{1,0:T(8,128)(2,1)}, u32[]{:S(2)}, u32[]{:S(2)}) collective-permute-start(bf16[256,2048]{1,0:T(8,128)(2,1)} %add_states.2.earlier_out.refs_0_), channel_id=1, source_target_pairs={{0,4},{1,5},{2,6},{3,7},{4,0},{5,1},{6,2},{7,3},{8,12},{9,13},{10,... | collective-permute-start | bytes 3145736 | tf_op jit(solution)/shard_map/ppermute | solution.py:880
  173.3 52.0 %all-to-all-start.2 = ((bf16[4,256,2048]{2,1,0:T(8,128)(2,1)}), bf16[4,256,2048]{2,1,0:T(8,128)(2,1)}, u32[]{:S(2)}, u32[]{:S(2)}) async-start(bf16[4,256,2048]{2,1,0:T(8,128)(2,1)} %add_states.3), calls=%async_computation.2 | async-start | bytes 8388608 | tf_op jit(solution)/shard_map/all_to_all | solution.py:889

commit v3 on v2

--- a/solution.py
+++ b/solution.py
@@ -499,7 +499,7 @@
 
 
 SMEM = pl.BlockSpec(memory_space=pltpu.SMEM)
-PROMPT_GRAD_FLOPS = 2**38
+PROMPT_GRAD_FLOPS = 2**36
 
 
 def whole(shape):
@@ -623,7 +623,7 @@
         ],
         compiler_params=params("arbitrary"),
         cost_estimate=pl.CostEstimate(
-            flops=8 * 2**30, bytes_accessed=3 * 2**20, transcendentals=rows * half * HG
+            flops=2**20 if so_far else 2**33, bytes_accessed=2**12, transcendentals=0
         ),
         name="resp_mid",
     )(
@@ -881,12 +881,13 @@
 
     part, weight, p_step, beyond = prompt_state(place, v, halo, dt_all, masks, wb_mine, hp)
     parts_of_start = across(part)
-    grads = mid(0, 1, weight)
+    grads = mid(0, 2, weight)
     part = add_states(d_states, grads[3])
     parts_of_grad = across(part)
-    grad_x, grad_b, dc, sums = mid(1, G - 1, part, grads)
-    start = add_states(parts_of_start, sums, copies=G)
+    start = add_states(parts_of_start, part, copies=G)
+    *grads, start = mid(2, 1, start, grads, handed=True)
     start = lax.all_to_all(start, "resp", 0, 0, axis_index_groups=inside)
+    grad_x, grad_b, dc, sums = mid(3, 1, weight, grads)
     p_grad, p_heads = prompt_grad(
         place, v, halo, dt_mine, masks, wb_mine, hp, weight, p_step, beyond, parts_of_grad, sums
     )

time: 268 us -> 263 us (0.981)
  waiting for transfers between devices: 51.3 us -> 41.6 us
  local copies, waits for them, and re-layouts: 17.1 us -> 20.1 us
    ppermute x2, waiting for transfers between devices: 0.01 us -> 30.6 us  [across(): return [part] + [lax.ppermute(part, 'resp', route) for route in routes]]
    all_to_all x1, waiting for transfers between devices: 23.1 us -> 3.06 us  [shards(): start = lax.all_to_all(start, 'resp', 0, 0, axis_index_groups=inside)]
    all_to_all x1, waiting for transfers between devices: 19.6 us -> 3.22 us  [shards(): d_states = lax.all_to_all(d_states, 'resp', 0, 0, axis_index_groups=inside)]
    all_to_all x1, waiting for transfers between devices: 8.56 us -> 4.69 us  [to_all(): return lax.all_to_all(copies, axes, 0, 0, axis_index_groups=groups)]
    pallas_call x2 -> x3, Pallas kernels: 65.9 us -> 66.3 us  [response_mid(): pl.pallas_call(functools.partial(resp_mid_kernel, first, handed), grid=(c...]
  transfers between devices with their start and end apart: 8 -> 8, of which waited for: 3 -> 4; matrix products, arithmetic and copies ran while one was open for 8% -> 10% of each run, Pallas kernels for 46% -> 47%
where the time goes in v3:
time: 263 us; the launch traced here: 261 us
  Pallas kernels  136 us (52%)
  waiting for transfers between devices  41.6 us (16%)
  blocking collectives  28.7 us (11%)
  starting transfers between devices  22.3 us (8%)
  local copies, waits for them, and re-layouts  20.1 us (8%)
  other arithmetic  9.68 us (4%)
  between operations  3.16 us (1%)
    pallas_call x3, Pallas kernels, response_mid(): pl.pallas_call(functools.partial(resp_mid_kernel, first, handed), grid=(c...  66.3 us
    ppermute x2, waiting for transfers between devices, across(): return [part] + [lax.ppermute(part, 'resp', route) for route in routes]  30.6 us
    pallas_call x1, Pallas kernels, prompt_grad(): pl.pallas_call(functools.partial(prompt_grad_kernel, len(states)), in_spe...  23.8 us
    all_to_all x1, blocking collectives, sum_over_all(): mine = jnp.sum(lax.all_to_all(slices, axes, 0, 0), axis=0)  15.7 us
    pallas_call x1, Pallas kernels, prompt_state(): pl.pallas_call(prompt_state_kernel, in_specs=[SMEM] + [pl.BlockSpec()] *...  14.6 us
    all_to_all x1, blocking collectives, to_all(): return lax.all_to_all(copies, axes, 0, 0, axis_index_groups=groups)  13 us
    pallas_call x1, Pallas kernels, response_end(): pl.pallas_call(resp_end_kernel, grid=(G,), in_specs=[SMEM, SMEM, pl.Block...  11.3 us
    pallas_call x2, Pallas kernels, add_states(): pl.pallas_call(functools.partial(add_kernel, len(terms)), grid=(4,), in_s...  8.35 us
  transfers between devices with their start and end apart: 8, of which 4 were waited for; matrix products, arithmetic and copies ran while one was open for 10% of the time, Pallas kernels for 47%

profile of v3, /device:TPU:0, one launch (start us, length us, event | category | flops | bytes accessed | tf_op | source)
XLA Modules:
  0.0 261.5 jit_solution(14384068861639032610)
XLA Ops:
  1.4 1.0 slice.32
  2.7 0.9 maximum_maximum_fusion
  3.6 1.0 broadcast_in_dim.43
  4.6 7.3 %all-to-all-start = ((bf16[8,384,128]{2,1,0:T(8,128)(2,1)}), bf16[8,384,128]{2,1,0:T(8,128)(2,1)}, u32[]{:S(2)}, u32[]{:S(2)}) async-start(bf16[8,384,128]{2,1,0:T(8,128)(2,1)} %broadcast_in_dim.43), calls=%async_computation | async-start | bytes 1572864 | tf_op jit(solution)/shard_map/all_to_all | solution.py:784
  11.9 1.5 slice.43
  13.4 1.7 copy.45
  15.2 1.3 copy-done
  16.5 1.3 fusion.5
  17.8 2.0 collective-permute-start
  19.8 1.5 collective-permute-start.1
  21.3 1.5 collective-permute-start.2
  24.1 0.7 fusion.7
  24.8 0.6 pad.30.hp
  25.4 2.0 resp_steps.1
  27.6 4.7 %all-to-all-done = bf16[8,384,128]{2,1,0:T(8,128)(2,1)} async-done(((bf16[8,384,128]{2,1,0:T(8,128)(2,1)}), bf16[8,384,128]{2,1,0:T(8,128)(2,1)}, u32[]{:S(2)}, u32[]{:S(2)}) %all-to-all-start) | async-done | bytes 786464 | tf_op jit(solution)/shard_map/all_to_all | solution.py:784
  32.3 0.9 constant_dynamic-slice_fusion.5
  33.2 0.8 pad_convert_fusion.1.tail_c.tail_x.tail_b
  34.0 1.4 convert_reduce_fusion.4
  36.1 7.9 %resp_state.1 = (bf16[4,256,2048]{2,1,0:T(8,128)(2,1)}, bf16[256,8192]{1,0:T(8,128)(2,1)}, bf16[256,1024]{1,0:T(8,128)(2,1)}) custom-call(f32[1,1]{1,0:T(1,128)} %bitcast.8.adv.scale, bf16[256,10240]{1,0:T(8,128)(2,1)} %bitcast.56, f32[8,10240]{1,0:T(8,128)} %pad_convert_fusion.1.tail_c.tail_x.tail_b, f32[8,10240]{1,0:T(8,128)} %copy-done.2, ...), custom_call_target="tpu_custom_call" | custom-call | flops 1073741824 | bytes 14680064 | tf_op jit(solution)/shard_map/resp_state/pallas_call | solution.py:529
  44.0 5.2 %all-to-all-start.1 = ((bf16[4,256,2048]{2,1,0:T(8,128)(2,1)}), bf16[4,256,2048]{2,1,0:T(8,128)(2,1)}, u32[]{:S(2)}, u32[]{:S(2)}) async-start(bf16[4,256,2048]{2,1,0:T(8,128)(2,1)} %get-tuple-element.39), calls=%async_computation.1 | async-start | bytes 8388608 | tf_op jit(solution)/shard_map/all_to_all | solution.py:867
  49.2 0.9 constant_dynamic-slice_fusion.2
  50.1 0.6 pad_maximum_fusion.2.wb
  50.7 0.6 add_bitcast_fusion.place
  51.4 1.0 copy.37
  52.5 0.7 broadcast_in_dim_reshape.3.skip
  53.5 0.8 fusion.6.masks
  54.3 1.6 pad_maximum_fusion
  55.9 2.0 bitcast_dynamic-update-slice_fusion.2
  57.9 1.9 bitcast_dynamic-update-slice_fusion.1
  59.8 1.9 bitcast_dynamic-update-slice_fusion
  61.8 1.7 slice.45
  63.5 0.6 pad_maximum_fusion.1.halo
  64.2 14.6 %prompt_state.1 = (bf16[256,2048]{1,0:T(8,128)(2,1)}, f32[512,128]{1,0:T(8,128)}, f32[512,128]{1,0:T(8,128)}, f32[8,128]{1,0:T(8,128)}) custom-call(s32[1,2]{1,0:T(1,128)} %add_bitcast_fusion.place, bf16[512,2304]{1,0:T(8,128)(2,1)} %bitcast.26.v, f32[8,2304]{1,0:T(8,128)} %pad_maximum_fusion.1.halo, bf16[1024,128]{1,0:T(8,128)(2,1)} %bitcast.78, ...), custom_call_target="tpu_custom_call" | custom-call | flops 536870912 | bytes 4194304 | tf_op jit(solution)/shard_map/prompt_state/pallas_call | solution.py:716
  78.7 33.6 %resp_mid.3 = (f32[8,8192]{1,0:T(8,128)}, f32[8,1024]{1,0:T(8,128)}, f32[256,1024]{1,0:T(8,128)}, f32[520,128]{1,0:T(8,128)}) custom-call(s32[1,1]{1,0:T(1,128)S(6)} %copy.57.len_ref, bf16[256,10240]{1,0:T(8,128)(2,1)} %bitcast.57, bf16[256,10240]{1,0:T(8,128)(2,1)} %bitcast.58, f32[8,10240]{1,0:T(8,128)} %pad_convert_fusion.1.tail_c.tail_x.tail_b, ...), custom_call_target="tpu_custom_call" | custom-call | flops 8589934592 | bytes 4096 | tf_op jit(solution)/shard_map/resp_mid/pallas_call | solution.py:566
  112.3 3.2 %all-to-all-done.1.refs_0_.refs_1_.refs_2_.refs_3_ = bf16[4,256,2048]{2,1,0:T(8,128)(2,1)} async-done(((bf16[4,256,2048]{2,1,0:T(8,128)(2,1)}), bf16[4,256,2048]{2,1,0:T(8,128)(2,1)}, u32[]{:S(2)}, u32[]{:S(2)}) %all-to-all-start.1) | async-done | bytes 4194336 | tf_op jit(solution)/shard_map/all_to_all | solution.py:867
  115.6 4.2 %add_states.2.refs_2_.refs_0_ = bf16[256,2048]{1,0:T(8,128)(2,1)} custom-call(bf16[4,256,2048]{2,1,0:T(8,128)(2,1)} %all-to-all-done.1.refs_0_.refs_1_.refs_2_.refs_3_, bf16[4,256,2048]{2,1,0:T(8,128)(2,1)} %all-to-all-done.1.refs_0_.refs_1_.refs_2_.refs_3_, bf16[4,256,2048]{2,1,0:T(8,128)(2,1)} %all-to-all-done.1.refs_0_.refs_1_.refs_2_.refs_3_, ...), custom_call_target="tpu_custom_call" | custom-call | flops 4194304 | bytes 6291456 | tf_op jit(solution)/shard_map/add_states/pallas_call | solution.py:698
  119.7 0.7 constant_dynamic-slice_fusion.dt_mine
  120.4 30.6 %collective-permute-done.3.refs_1_ = bf16[256,2048]{1,0:T(8,128)(2,1)} collective-permute-done((bf16[256,2048]{1,0:T(8,128)(2,1)}, bf16[256,2048]{1,0:T(8,128)(2,1)}, u32[]{:S(2)}, u32[]{:S(2)}) %collective-permute-start.3) | collective-permute-done | bytes 1048608 | tf_op jit(solution)/shard_map/ppermute | solution.py:880
  151.0 4.2 %add_states.3.earlier_out = bf16[4,256,2048]{2,1,0:T(8,128)(2,1)} custom-call(bf16[256,2048]{1,0:T(8,128)(2,1)} %get-tuple-element.38.refs_0_, bf16[256,2048]{1,0:T(8,128)(2,1)} %collective-permute-done.3.refs_1_, bf16[256,2048]{1,0:T(8,128)(2,1)} %add_states.2.refs_2_.refs_0_), custom_call_target="tpu_custom_call" | custom-call | flops 4194304 | bytes 6291456 | tf_op jit(solution)/shard_map/add_states/pallas_call | solution.py:698
  155.2 16.3 %resp_mid.4 = (f32[8,8192]{1,0:T(8,128)}, f32[8,1024]{1,0:T(8,128)}, f32[256,1024]{1,0:T(8,128)}, f32[520,128]{1,0:T(8,128)}, bf16[4,256,2048]{2,1,0:T(8,128)(2,1)}) custom-call(s32[1,1]{1,0:T(1,128)S(6)} %copy.57.len_ref, bf16[256,10240]{1,0:T(8,128)(2,1)} %bitcast.59, ...), custom_call_target="tpu_custom_call", output_to_operand_aliasing={{0}: (15, {}), {1}: (16, {}), {2}: (17, {}), {4}: (14, {})} | custom-call | flops 1048576 | bytes 4096 | tf_op jit(solution)/shard_map/resp_mid/pallas_call | solution.py:566
  171.5 4.9 %all-to-all-start.2 = ((bf16[4,256,2048]{2,1,0:T(8,128)(2,1)}), bf16[4,256,2048]{2,1,0:T(8,128)(2,1)}, u32[]{:S(2)}, u32[]{:S(2)}) async-start(bf16[4,256,2048]{2,1,0:T(8,128)(2,1)} %get-tuple-element.45), calls=%async_computation.2 | async-start | bytes 8388608 | tf_op jit(solution)/shard_map/all_to_all | solution.py:889
  176.3 16.4 %resp_mid.5 = (f32[8,8192]{1,0:T(8,128)}, f32[8,1024]{1,0:T(8,128)}, f32[256,1024]{1,0:T(8,128)}, f32[520,128]{1,0:T(8,128)}) custom-call(s32[1,1]{1,0:T(1,128)S(6)} %copy.57.len_ref, bf16[256,10240]{1,0:T(8,128)(2,1)} %bitcast.61, bf16[256,10240]{1,0:T(8,128)(2,1)} %bitcast.62, ...), custom_call_target="tpu_custom_call", output_to_operand_aliasing={{0}: (15, {}), {1}: (16, {}), {2}: (17, {})} | custom-call | flops 1048576 | bytes 4096 | tf_op jit(solution)/shard_map/resp_mid/pallas_call | solution.py:566
  192.7 23.8 %prompt_grad.1 = (f32[8,2304]{1,0:T(8,128)}, f32[8,128]{1,0:T(8,128)}) custom-call(s32[1,2]{1,0:T(1,128)} %add_bitcast_fusion.place, bf16[512,2304]{1,0:T(8,128)(2,1)} %bitcast.26.v, f32[8,2304]{1,0:T(8,128)} %pad_maximum_fusion.1.halo, bf16[512,128]{1,0:T(8,128)(2,1)} %constant_dynamic-slice_fusion.dt_mine, f32[512,8]{1,0:T(8,128)} %fusion.6.masks, ...), custom_call_target="tpu_custom_call" | custom-call | flops 68719476736 | bytes 8388608 | tf_op jit(solution)/shard_map/prompt_grad/pallas_call | solution.py:744
  216.5 3.1 %all-to-all-done.2.start = bf16[4,256,2048]{2,1,0:T(8,128)(2,1)} async-done(((bf16[4,256,2048]{2,1,0:T(8,128)(2,1)}), bf16[4,256,2048]{2,1,0:T(8,128)(2,1)}, u32[]{:S(2)}, u32[]{:S(2)}) %all-to-all-start.2) | async-done | bytes 4194336 | tf_op jit(solution)/shard_map/all_to_all | solution.py:889
  219.6 11.3 %resp_end.1 = f32[64,8,128]{2,1,0:T(8,128)} custom-call(s32[1,2]{1,0:T(1,128)} %add_bitcast_fusion.place, f32[1,1]{1,0:T(1,128)} %bitcast.8.adv.scale, bf16[256,10240]{1,0:T(8,128)(2,1)} %bitcast.63, f32[8,10240]{1,0:T(8,128)} %pad_convert_fusion.1.tail_c.tail_x.tail_b, f32[8,10240]{1,0:T(8,128)} %copy-done.2, bf16[256,1024]{1,0:T(8,128)(2,1)} %get-tuple-element.33.c_act, ...), custom_call_target="tpu_custom_call" | custom-call | flops 2147483648 | bytes 12582912 | tf_op jit(solution)/shard_map/resp_end/pallas_call | solution.py:642
  230.9 15.7 %all_to_all.25 = f32[32,2,8,128]{3,2,1,0:T(8,128)S(1)} all-to-all(f32[32,2,8,128]{3,2,1,0:T(8,128)} %bitcast.80), channel_id=1, replica_groups=mesh['group'=4,'resp'=8] {'group','resp'}, dimensions={0} | all-to-all | bytes 524288 | tf_op jit(solution)/shard_map/all_to_all | solution.py:789
  246.6 13.0 %all_to_all.26 = f32[32,2,8,128]{3,2,1,0:T(8,128)} all-to-all(f32[32,2,8,128]{3,2,1,0:T(8,128)S(1)} %broadcast_in_dim.49), channel_id=1, replica_groups=mesh['group'=4,'resp'=8] {'group','resp'}, dimensions={0} | all-to-all | bytes 524288 | tf_op jit(solution)/shard_map/all_to_all | solution.py:784
  259.7 1.8 unpack.1
  (53 shorter events, 1.8 us)
Async XLA Ops:
  0.6 11.3 %copy-start.3 = (bf16[1,128,10240]{2,1,0:T(8,128)(2,1)S(1)}, bf16[1,128,10240]{2,1,0:T(8,128)(2,1)}, u32[]{:S(2)}) copy-start(bf16[1,128,10240]{2,1,0:T(8,128)(2,1)} %param.11) | copy-start | bytes 7864324
  4.6 27.7 %all-to-all-start = ((bf16[8,384,128]{2,1,0:T(8,128)(2,1)}), bf16[8,384,128]{2,1,0:T(8,128)(2,1)}, u32[]{:S(2)}, u32[]{:S(2)}) async-start(bf16[8,384,128]{2,1,0:T(8,128)(2,1)} %broadcast_in_dim.43), calls=%async_computation | async-start | bytes 1572864 | tf_op jit(solution)/shard_map/all_to_all | solution.py:784
  15.2 1.3 copy-start
  15.2 8.2 %copy-start.9 = (s32[1,4]{1,0:T(1,128)S(1)}, s32[1,4]{1,0:T(1,128)}, u32[]{:S(2)}) copy-start(s32[1,4]{1,0:T(1,128)} %param.13) | copy-start | bytes 52
  15.2 9.7 %copy-start.8 = (f32[3,128]{1,0:T(4,128)S(1)}, f32[3,128]{1,0:T(4,128)}, u32[]{:S(2)}) copy-start(f32[3,128]{1,0:T(4,128)} %param.21) | copy-start | bytes 4612
  15.2 12.3 %copy-start.6 = (f32[4,10240]{1,0:T(4,128)S(1)}, f32[4,10240]{1,0:T(4,128)}, u32[]{:S(2)}) copy-start(f32[4,10240]{1,0:T(4,128)} %param.19) | copy-start | bytes 491524
  15.2 12.3 %copy-start.7 = (f32[10240]{0:T(1024)S(1)}, f32[10240]{0:T(1024)}, u32[]{:S(2)}) copy-start(f32[10240]{0:T(1024)} %param.20) | copy-start | bytes 122884
  17.8 38.1 %collective-permute-start = (bf16[128,2304]{1,0:T(8,128)(2,1)}, bf16[128,2304]{1,0:T(8,128)(2,1)}, u32[]{:S(2)}, u32[]{:S(2)}) collective-permute-start(bf16[128,2304]{1,0:T(8,128)(2,1)} %get-tuple-element.66), channel_id=1, source_target_pairs={{0,1},{1,2},{2,3},{3,0},{4,5},{5,6},{6,7},{7,4},{8,9},{9,10},{10,1... | collective-permute-start | bytes 1769480 | tf_op jit(solution)/shard_map/ppermute | solution.py:834
  19.8 38.1 %collective-permute-start.1 = (bf16[128,2304]{1,0:T(8,128)(2,1)}, bf16[128,2304]{1,0:T(8,128)(2,1)}, u32[]{:S(2)}, u32[]{:S(2)}) collective-permute-start(bf16[128,2304]{1,0:T(8,128)(2,1)} %get-tuple-element.67), channel_id=1, source_target_pairs={{0,2},{1,3},{2,0},{3,1},{4,6},{5,7},{6,4},{7,5},{8,10},{9,11},{10,... | collective-permute-start | bytes 1769480 | tf_op jit(solution)/shard_map/ppermute | solution.py:834
  21.3 38.5 %collective-permute-start.2 = (bf16[128,2304]{1,0:T(8,128)(2,1)}, bf16[128,2304]{1,0:T(8,128)(2,1)}, u32[]{:S(2)}, u32[]{:S(2)}) collective-permute-start(bf16[128,2304]{1,0:T(8,128)(2,1)} %get-tuple-element.65), channel_id=1, source_target_pairs={{0,3},{1,0},{2,1},{3,2},{4,7},{5,4},{6,5},{7,6},{8,11},{9,8},{10,9... | collective-permute-start | bytes 1769480 | tf_op jit(solution)/shard_map/ppermute | solution.py:834
  27.6 8.5 %copy-start.2 = (f32[8,10240]{1,0:T(8,128)}, f32[8,10240]{1,0:T(8,128)S(1)}, u32[]{:S(2)}) copy-start(f32[8,10240]{1,0:T(8,128)S(1)} %select_maximum_fusion.wb_c.wb_x.wb_b) | copy-start | bytes 983044
  44.0 7.3 %copy-start.5 = (f32[256,128]{1,0:T(8,128)S(1)}, f32[256,128]{1,0:T(8,128)}, u32[]{:S(2)}) copy-start(f32[256,128]{1,0:T(8,128)} %get-tuple-element.36.cum) | copy-start | bytes 393220
  44.0 10.3 %copy-start.1 = (bf16[16,4,8,2048]{3,2,0,1:T(8,128)(2,1)S(1)}, bf16[16,4,8,2048]{3,2,0,1:T(8,128)(2,1)}, u32[]{:S(2)}) copy-start(bf16[16,4,8,2048]{3,2,0,1:T(8,128)(2,1)} %copy-done) | copy-start | bytes 6291460
  44.0 71.5 %all-to-all-start.1 = ((bf16[4,256,2048]{2,1,0:T(8,128)(2,1)}), bf16[4,256,2048]{2,1,0:T(8,128)(2,1)}, u32[]{:S(2)}, u32[]{:S(2)}) async-start(bf16[4,256,2048]{2,1,0:T(8,128)(2,1)} %get-tuple-element.39), calls=%async_computation.1 | async-start | bytes 8388608 | tf_op jit(solution)/shard_map/all_to_all | solution.py:867
  78.7 72.3 %collective-permute-start.3 = (bf16[256,2048]{1,0:T(8,128)(2,1)}, bf16[256,2048]{1,0:T(8,128)(2,1)}, u32[]{:S(2)}, u32[]{:S(2)}) collective-permute-start(bf16[256,2048]{1,0:T(8,128)(2,1)} %get-tuple-element.38.refs_0_), channel_id=1, source_target_pairs={{0,4},{1,5},{2,6},{3,7},{4,0},{5,1},{6,2},{7,3},{8,12},{9,13},{10,... | collective-permute-start | bytes 3145736 | tf_op jit(solution)/shard_map/ppermute | solution.py:880
  115.5 4.2 %copy-start.4 = (bf16[8,128,128]{2,1,0:T(8,128)(2,1)S(1)}, bf16[8,128,128]{2,1,0:T(8,128)(2,1)}, u32[]{:S(2)}) copy-start(bf16[8,128,128]{2,1,0:T(8,128)(2,1)} %slice.45) | copy-start | bytes 786436
  119.7 73.0 %collective-permute-start.4 = (bf16[256,2048]{1,0:T(8,128)(2,1)}, bf16[256,2048]{1,0:T(8,128)(2,1)}, u32[]{:S(2)}, u32[]{:S(2)}) collective-permute-start(bf16[256,2048]{1,0:T(8,128)(2,1)} %add_states.2.refs_2_.refs_0_), channel_id=1, source_target_pairs={{0,4},{1,5},{2,6},{3,7},{4,0},{5,1},{6,2},{7,3},{8,12},{9,13},{10,... | collective-permute-start | bytes 3145736 | tf_op jit(solution)/shard_map/ppermute | solution.py:880
  171.5 48.1 %all-to-all-start.2 = ((bf16[4,256,2048]{2,1,0:T(8,128)(2,1)}), bf16[4,256,2048]{2,1,0:T(8,128)(2,1)}, u32[]{:S(2)}, u32[]{:S(2)}) async-start(bf16[4,256,2048]{2,1,0:T(8,128)(2,1)} %get-tuple-element.45), calls=%async_computation.2 | async-start | bytes 8388608 | tf_op jit(solution)/shard_map/all_to_all | solution.py:889

commit v4 on v3

--- a/solution.py
+++ b/solution.py
@@ -884,10 +884,10 @@
     grads = mid(0, 2, weight)
     part = add_states(d_states, grads[3])
     parts_of_grad = across(part)
-    start = add_states(parts_of_start, part, copies=G)
-    *grads, start = mid(2, 1, start, grads, handed=True)
+    grads = mid(2, 1, part, grads)
+    start = add_states(parts_of_start, grads[3], copies=G)
+    grad_x, grad_b, dc, sums = mid(3, 1, start, grads)
     start = lax.all_to_all(start, "resp", 0, 0, axis_index_groups=inside)
-    grad_x, grad_b, dc, sums = mid(3, 1, weight, grads)
     p_grad, p_heads = prompt_grad(
         place, v, halo, dt_mine, masks, wb_mine, hp, weight, p_step, beyond, parts_of_grad, sums
     )

time: 263 us -> 259 us (0.985)
  local copies, waits for them, and re-layouts: 20.1 us -> 17.2 us
    ppermute x2, waiting for transfers between devices: 30.6 us -> 13.8 us  [across(): return [part] + [lax.ppermute(part, 'resp', route) for route in routes]]
    all_to_all x1, waiting for transfers between devices: 3.06 us -> 15.8 us  [shards(): start = lax.all_to_all(start, 'resp', 0, 0, axis_index_groups=inside)]
    all_to_all x1, waiting for transfers between devices: 4.69 us -> 8.53 us  [to_all(): return lax.all_to_all(copies, axes, 0, 0, axis_index_groups=groups)]
  transfers between devices with their start and end apart: 8 -> 8, of which waited for: 4 -> 4; matrix products, arithmetic and copies ran while one was open for 10% -> 9% of each run, Pallas kernels for 47% -> 48%
where the time goes in v4:
time: 259 us; the launch traced here: 258 us
  Pallas kernels  136 us (53%)
  waiting for transfers between devices  41.6 us (16%)
  blocking collectives  28.6 us (11%)
  starting transfers between devices  21.4 us (8%)
  local copies, waits for them, and re-layouts  17.2 us (7%)
  other arithmetic  9.49 us (4%)
  between operations  3.04 us (1%)
    pallas_call x3, Pallas kernels, response_mid(): pl.pallas_call(functools.partial(resp_mid_kernel, first, handed), grid=(c...  66.5 us
    pallas_call x1, Pallas kernels, prompt_grad(): pl.pallas_call(functools.partial(prompt_grad_kernel, len(states)), in_spe...  23.8 us
    all_to_all x1, waiting for transfers between devices, shards(): start = lax.all_to_all(start, 'resp', 0, 0, axis_index_groups=inside)  15.8 us
    all_to_all x1, blocking collectives, sum_over_all(): mine = jnp.sum(lax.all_to_all(slices, axes, 0, 0), axis=0)  15.5 us
    pallas_call x1, Pallas kernels, prompt_state(): pl.pallas_call(prompt_state_kernel, in_specs=[SMEM] + [pl.BlockSpec()] *...  14.6 us
    ppermute x2, waiting for transfers between devices, across(): return [part] + [lax.ppermute(part, 'resp', route) for route in routes]  13.8 us
    all_to_all x1, blocking collectives, to_all(): return lax.all_to_all(copies, axes, 0, 0, axis_index_groups=groups)  13 us
    pallas_call x1, Pallas kernels, response_end(): pl.pallas_call(resp_end_kernel, grid=(G,), in_specs=[SMEM, SMEM, pl.Block...  11.3 us
  transfers between devices with their start and end apart: 8, of which 4 were waited for; matrix products, arithmetic and copies ran while one was open for 9% of the time, Pallas kernels for 48%

profile of v4, /device:TPU:0, one launch (start us, length us, event | category | flops | bytes accessed | tf_op | source)
XLA Modules:
  0.0 257.6 jit_solution(5138645507101766559)
XLA Ops:
  1.5 1.0 slice.32
  2.7 0.9 maximum_maximum_fusion
  3.6 1.0 broadcast_in_dim.43
  4.6 7.3 %all-to-all-start = ((bf16[8,384,128]{2,1,0:T(8,128)(2,1)}), bf16[8,384,128]{2,1,0:T(8,128)(2,1)}, u32[]{:S(2)}, u32[]{:S(2)}) async-start(bf16[8,384,128]{2,1,0:T(8,128)(2,1)} %broadcast_in_dim.43), calls=%async_computation | async-start | bytes 1572864 | tf_op jit(solution)/shard_map/all_to_all | solution.py:784
  11.9 0.1 slice.43
  12.3 1.3 copy-done
  13.6 1.2 fusion.5
  14.8 2.9 %collective-permute-start.2 = (bf16[128,2304]{1,0:T(8,128)(2,1)}, bf16[128,2304]{1,0:T(8,128)(2,1)}, u32[]{:S(2)}, u32[]{:S(2)}) collective-permute-start(bf16[128,2304]{1,0:T(8,128)(2,1)} %get-tuple-element.63), channel_id=1, source_target_pairs={{0,3},{1,0},{2,1},{3,2},{4,7},{5,4},{6,5},{7,6},{8,11},{9,8},{10,9... | collective-permute-start | bytes 1769480 | tf_op jit(solution)/shard_map/ppermute | solution.py:834
  17.8 1.1 collective-permute-start.1
  19.7 0.6 slice.39
  20.3 0.7 fusion.7
  21.0 0.6 pad.30.hp
  21.6 2.0 resp_steps.1
  23.7 8.5 %all-to-all-done = bf16[8,384,128]{2,1,0:T(8,128)(2,1)} async-done(((bf16[8,384,128]{2,1,0:T(8,128)(2,1)}), bf16[8,384,128]{2,1,0:T(8,128)(2,1)}, u32[]{:S(2)}, u32[]{:S(2)}) %all-to-all-start) | async-done | bytes 786464 | tf_op jit(solution)/shard_map/all_to_all | solution.py:784
  32.3 0.9 constant_dynamic-slice_fusion.5
  33.2 0.8 pad_convert_fusion.1.tail_c.tail_x.tail_b
  34.0 1.3 convert_reduce_fusion.4
  35.9 8.0 %resp_state.1 = (bf16[4,256,2048]{2,1,0:T(8,128)(2,1)}, bf16[256,8192]{1,0:T(8,128)(2,1)}, bf16[256,1024]{1,0:T(8,128)(2,1)}) custom-call(f32[1,1]{1,0:T(1,128)} %bitcast.8.adv.scale, bf16[256,10240]{1,0:T(8,128)(2,1)} %bitcast.56, f32[8,10240]{1,0:T(8,128)} %pad_convert_fusion.1.tail_c.tail_x.tail_b, f32[8,10240]{1,0:T(8,128)} %copy-done.2, ...), custom_call_target="tpu_custom_call" | custom-call | flops 1073741824 | bytes 14680064 | tf_op jit(solution)/shard_map/resp_state/pallas_call | solution.py:529
  43.8 5.3 %all-to-all-start.1 = ((bf16[4,256,2048]{2,1,0:T(8,128)(2,1)}), bf16[4,256,2048]{2,1,0:T(8,128)(2,1)}, u32[]{:S(2)}, u32[]{:S(2)}) async-start(bf16[4,256,2048]{2,1,0:T(8,128)(2,1)} %get-tuple-element.38), calls=%async_computation.1 | async-start | bytes 8388608 | tf_op jit(solution)/shard_map/all_to_all | solution.py:867
  49.1 0.9 constant_dynamic-slice_fusion.2
  50.0 0.6 pad_maximum_fusion.2.wb
  50.6 0.6 add_bitcast_fusion.place
  51.3 0.7 broadcast_in_dim_reshape.3.skip
  52.0 0.3 copy.37
  52.4 1.0 copy.39
  53.4 0.7 fusion.6.masks
  54.2 1.6 pad_maximum_fusion
  55.7 1.9 bitcast_dynamic-update-slice_fusion.2
  57.7 1.9 bitcast_dynamic-update-slice_fusion.1
  59.6 1.9 bitcast_dynamic-update-slice_fusion
  61.6 1.7 slice.45
  63.4 0.6 pad_maximum_fusion.1.halo
  64.0 14.6 %prompt_state.1 = (bf16[256,2048]{1,0:T(8,128)(2,1)}, f32[512,128]{1,0:T(8,128)}, f32[512,128]{1,0:T(8,128)}, f32[8,128]{1,0:T(8,128)}) custom-call(s32[1,2]{1,0:T(1,128)} %add_bitcast_fusion.place, bf16[512,2304]{1,0:T(8,128)(2,1)} %bitcast.22.v, f32[8,2304]{1,0:T(8,128)} %pad_maximum_fusion.1.halo, bf16[1024,128]{1,0:T(8,128)(2,1)} %bitcast.78, ...), custom_call_target="tpu_custom_call" | custom-call | flops 536870912 | bytes 4194304 | tf_op jit(solution)/shard_map/prompt_state/pallas_call | solution.py:716
  78.6 33.6 %resp_mid.3 = (f32[8,8192]{1,0:T(8,128)}, f32[8,1024]{1,0:T(8,128)}, f32[256,1024]{1,0:T(8,128)}, f32[520,128]{1,0:T(8,128)}) custom-call(s32[1,1]{1,0:T(1,128)S(6)} %copy.55.len_ref, bf16[256,10240]{1,0:T(8,128)(2,1)} %bitcast.57, bf16[256,10240]{1,0:T(8,128)(2,1)} %bitcast.58, f32[8,10240]{1,0:T(8,128)} %pad_convert_fusion.1.tail_c.tail_x.tail_b, ...), custom_call_target="tpu_custom_call" | custom-call | flops 8589934592 | bytes 4096 | tf_op jit(solution)/shard_map/resp_mid/pallas_call | solution.py:566
  112.2 3.4 %all-to-all-done.1.refs_0_.refs_1_.refs_2_.refs_3_ = bf16[4,256,2048]{2,1,0:T(8,128)(2,1)} async-done(((bf16[4,256,2048]{2,1,0:T(8,128)(2,1)}), bf16[4,256,2048]{2,1,0:T(8,128)(2,1)}, u32[]{:S(2)}, u32[]{:S(2)}) %all-to-all-start.1) | async-done | bytes 4194336 | tf_op jit(solution)/shard_map/all_to_all | solution.py:867
  115.6 4.2 %add_states.2.earlier_out.refs_0_ = bf16[256,2048]{1,0:T(8,128)(2,1)} custom-call(bf16[4,256,2048]{2,1,0:T(8,128)(2,1)} %all-to-all-done.1.refs_0_.refs_1_.refs_2_.refs_3_, bf16[4,256,2048]{2,1,0:T(8,128)(2,1)} %all-to-all-done.1.refs_0_.refs_1_.refs_2_.refs_3_, bf16[4,256,2048]{2,1,0:T(8,128)(2,1)} %all-to-all-done.1.refs_0_.refs_1_.refs_2_.refs_3_, ...), custom_call_target="tpu_custom_call" | custom-call | flops 4194304 | bytes 6291456 | tf_op jit(solution)/shard_map/add_states/pallas_call | solution.py:698
  119.8 0.7 constant_dynamic-slice_fusion.dt_mine
  120.5 16.5 %resp_mid.4 = (f32[8,8192]{1,0:T(8,128)}, f32[8,1024]{1,0:T(8,128)}, f32[256,1024]{1,0:T(8,128)}, f32[520,128]{1,0:T(8,128)}) custom-call(s32[1,1]{1,0:T(1,128)S(6)} %copy.55.len_ref, bf16[256,10240]{1,0:T(8,128)(2,1)} %bitcast.59, bf16[256,10240]{1,0:T(8,128)(2,1)} %bitcast.60, ...), custom_call_target="tpu_custom_call", output_to_operand_aliasing={{0}: (15, {}), {1}: (16, {}), {2}: (17, {})} | custom-call | flops 1048576 | bytes 4096 | tf_op jit(solution)/shard_map/resp_mid/pallas_call | solution.py:566
  137.0 13.8 %collective-permute-done.3.refs_1_ = bf16[256,2048]{1,0:T(8,128)(2,1)} collective-permute-done((bf16[256,2048]{1,0:T(8,128)(2,1)}, bf16[256,2048]{1,0:T(8,128)(2,1)}, u32[]{:S(2)}, u32[]{:S(2)}) %collective-permute-start.3) | collective-permute-done | bytes 1048608 | tf_op jit(solution)/shard_map/ppermute | solution.py:880
  150.8 4.2 %add_states.3.earlier_out = bf16[4,256,2048]{2,1,0:T(8,128)(2,1)} custom-call(bf16[256,2048]{1,0:T(8,128)(2,1)} %get-tuple-element.34.refs_0_, bf16[256,2048]{1,0:T(8,128)(2,1)} %collective-permute-done.3.refs_1_, f32[520,128]{1,0:T(8,128)} %get-tuple-element.44.refs_2_.refs_3_), custom_call_target="tpu_custom_call" | custom-call | flops 4194304 | bytes 6291456 | tf_op jit(solution)/shard_map/add_states/pallas_call | solution.py:698
  155.0 4.9 %all-to-all-start.2 = ((bf16[4,256,2048]{2,1,0:T(8,128)(2,1)}), bf16[4,256,2048]{2,1,0:T(8,128)(2,1)}, u32[]{:S(2)}, u32[]{:S(2)}) async-start(bf16[4,256,2048]{2,1,0:T(8,128)(2,1)} %add_states.3.earlier_out), calls=%async_computation.2 | async-start | bytes 8388608 | tf_op jit(solution)/shard_map/all_to_all | solution.py:890
  159.9 16.4 %resp_mid.5 = (f32[8,8192]{1,0:T(8,128)}, f32[8,1024]{1,0:T(8,128)}, f32[256,1024]{1,0:T(8,128)}, f32[520,128]{1,0:T(8,128)}) custom-call(s32[1,1]{1,0:T(1,128)S(6)} %copy.55.len_ref, bf16[256,10240]{1,0:T(8,128)(2,1)} %bitcast.61, bf16[256,10240]{1,0:T(8,128)(2,1)} %bitcast.62, ...), custom_call_target="tpu_custom_call", output_to_operand_aliasing={{0}: (15, {}), {1}: (16, {}), {2}: (17, {})} | custom-call | flops 1048576 | bytes 4096 | tf_op jit(solution)/shard_map/resp_mid/pallas_call | solution.py:566
  176.3 23.8 %prompt_grad.1 = (f32[8,2304]{1,0:T(8,128)}, f32[8,128]{1,0:T(8,128)}) custom-call(s32[1,2]{1,0:T(1,128)} %add_bitcast_fusion.place, bf16[512,2304]{1,0:T(8,128)(2,1)} %bitcast.22.v, f32[8,2304]{1,0:T(8,128)} %pad_maximum_fusion.1.halo, bf16[512,128]{1,0:T(8,128)(2,1)} %constant_dynamic-slice_fusion.dt_mine, f32[512,8]{1,0:T(8,128)} %fusion.6.masks, ...), custom_call_target="tpu_custom_call" | custom-call | flops 68719476736 | bytes 8388608 | tf_op jit(solution)/shard_map/prompt_grad/pallas_call | solution.py:744
  200.1 15.8 %all-to-all-done.2.start = bf16[4,256,2048]{2,1,0:T(8,128)(2,1)} async-done(((bf16[4,256,2048]{2,1,0:T(8,128)(2,1)}), bf16[4,256,2048]{2,1,0:T(8,128)(2,1)}, u32[]{:S(2)}, u32[]{:S(2)}) %all-to-all-start.2) | async-done | bytes 4194336 | tf_op jit(solution)/shard_map/all_to_all | solution.py:890
  215.9 11.3 %resp_end.1 = f32[64,8,128]{2,1,0:T(8,128)} custom-call(s32[1,2]{1,0:T(1,128)} %add_bitcast_fusion.place, f32[1,1]{1,0:T(1,128)} %bitcast.8.adv.scale, bf16[256,10240]{1,0:T(8,128)(2,1)} %bitcast.63, f32[8,10240]{1,0:T(8,128)} %pad_convert_fusion.1.tail_c.tail_x.tail_b, f32[8,10240]{1,0:T(8,128)} %copy-done.2, bf16[256,1024]{1,0:T(8,128)(2,1)} %get-tuple-element.32.c_act, ...), custom_call_target="tpu_custom_call" | custom-call | flops 2147483648 | bytes 12582912 | tf_op jit(solution)/shard_map/resp_end/pallas_call | solution.py:642
  227.2 15.5 %all_to_all.25 = f32[32,2,8,128]{3,2,1,0:T(8,128)S(1)} all-to-all(f32[32,2,8,128]{3,2,1,0:T(8,128)} %bitcast.80), channel_id=1, replica_groups=mesh['group'=4,'resp'=8] {'group','resp'}, dimensions={0} | all-to-all | bytes 524288 | tf_op jit(solution)/shard_map/all_to_all | solution.py:789
  242.8 13.0 %all_to_all.26 = f32[32,2,8,128]{3,2,1,0:T(8,128)} all-to-all(f32[32,2,8,128]{3,2,1,0:T(8,128)S(1)} %broadcast_in_dim.49), channel_id=1, replica_groups=mesh['group'=4,'resp'=8] {'group','resp'}, dimensions={0} | all-to-all | bytes 524288 | tf_op jit(solution)/shard_map/all_to_all | solution.py:784
  255.8 1.8 unpack.1
  (53 shorter events, 1.1 us)
Async XLA Ops:
  0.6 11.3 %copy-start.3 = (bf16[1,128,10240]{2,1,0:T(8,128)(2,1)S(1)}, bf16[1,128,10240]{2,1,0:T(8,128)(2,1)}, u32[]{:S(2)}) copy-start(bf16[1,128,10240]{2,1,0:T(8,128)(2,1)} %param.11) | copy-start | bytes 7864324
  4.6 27.7 %all-to-all-start = ((bf16[8,384,128]{2,1,0:T(8,128)(2,1)}), bf16[8,384,128]{2,1,0:T(8,128)(2,1)}, u32[]{:S(2)}, u32[]{:S(2)}) async-start(bf16[8,384,128]{2,1,0:T(8,128)(2,1)} %broadcast_in_dim.43), calls=%async_computation | async-start | bytes 1572864 | tf_op jit(solution)/shard_map/all_to_all | solution.py:784
  12.2 1.4 copy-start
  12.3 7.3 %copy-start.9 = (s32[1,4]{1,0:T(1,128)S(1)}, s32[1,4]{1,0:T(1,128)}, u32[]{:S(2)}) copy-start(s32[1,4]{1,0:T(1,128)} %param.13) | copy-start | bytes 52
  12.3 8.7 %copy-start.8 = (f32[3,128]{1,0:T(4,128)S(1)}, f32[3,128]{1,0:T(4,128)}, u32[]{:S(2)}) copy-start(f32[3,128]{1,0:T(4,128)} %param.21) | copy-start | bytes 4612
  12.3 11.3 %copy-start.6 = (f32[4,10240]{1,0:T(4,128)S(1)}, f32[4,10240]{1,0:T(4,128)}, u32[]{:S(2)}) copy-start(f32[4,10240]{1,0:T(4,128)} %param.19) | copy-start | bytes 491524
  12.3 11.3 %copy-start.7 = (f32[10240]{0:T(1024)S(1)}, f32[10240]{0:T(1024)}, u32[]{:S(2)}) copy-start(f32[10240]{0:T(1024)} %param.20) | copy-start | bytes 122884
  14.8 44.8 %collective-permute-start.2 = (bf16[128,2304]{1,0:T(8,128)(2,1)}, bf16[128,2304]{1,0:T(8,128)(2,1)}, u32[]{:S(2)}, u32[]{:S(2)}) collective-permute-start(bf16[128,2304]{1,0:T(8,128)(2,1)} %get-tuple-element.63), channel_id=1, source_target_pairs={{0,3},{1,0},{2,1},{3,2},{4,7},{5,4},{6,5},{7,6},{8,11},{9,8},{10,9... | collective-permute-start | bytes 1769480 | tf_op jit(solution)/shard_map/ppermute | solution.py:834
  17.8 38.0 %collective-permute-start = (bf16[128,2304]{1,0:T(8,128)(2,1)}, bf16[128,2304]{1,0:T(8,128)(2,1)}, u32[]{:S(2)}, u32[]{:S(2)}) collective-permute-start(bf16[128,2304]{1,0:T(8,128)(2,1)} %get-tuple-element.64), channel_id=1, source_target_pairs={{0,1},{1,2},{2,3},{3,0},{4,5},{5,6},{6,7},{7,4},{8,9},{9,10},{10,1... | collective-permute-start | bytes 1769480 | tf_op jit(solution)/shard_map/ppermute | solution.py:834
  17.8 39.9 %collective-permute-start.1 = (bf16[128,2304]{1,0:T(8,128)(2,1)}, bf16[128,2304]{1,0:T(8,128)(2,1)}, u32[]{:S(2)}, u32[]{:S(2)}) collective-permute-start(bf16[128,2304]{1,0:T(8,128)(2,1)} %get-tuple-element.65), channel_id=1, source_target_pairs={{0,2},{1,3},{2,0},{3,1},{4,6},{5,7},{6,4},{7,5},{8,10},{9,11},{10,... | collective-permute-start | bytes 1769480 | tf_op jit(solution)/shard_map/ppermute | solution.py:834
  23.7 12.1 %copy-start.2 = (f32[8,10240]{1,0:T(8,128)}, f32[8,10240]{1,0:T(8,128)S(1)}, u32[]{:S(2)}) copy-start(f32[8,10240]{1,0:T(8,128)S(1)} %select_maximum_fusion.wb_c.wb_x.wb_b) | copy-start | bytes 983044
  43.8 8.5 %copy-start.5 = (f32[256,128]{1,0:T(8,128)S(1)}, f32[256,128]{1,0:T(8,128)}, u32[]{:S(2)}) copy-start(f32[256,128]{1,0:T(8,128)} %get-tuple-element.36.cum) | copy-start | bytes 393220
  43.8 10.3 %copy-start.1 = (bf16[16,4,8,2048]{3,2,0,1:T(8,128)(2,1)S(1)}, bf16[16,4,8,2048]{3,2,0,1:T(8,128)(2,1)}, u32[]{:S(2)}) copy-start(bf16[16,4,8,2048]{3,2,0,1:T(8,128)(2,1)} %copy-done) | copy-start | bytes 6291460
  43.8 71.7 %all-to-all-start.1 = ((bf16[4,256,2048]{2,1,0:T(8,128)(2,1)}), bf16[4,256,2048]{2,1,0:T(8,128)(2,1)}, u32[]{:S(2)}, u32[]{:S(2)}) async-start(bf16[4,256,2048]{2,1,0:T(8,128)(2,1)} %get-tuple-element.38), calls=%async_computation.1 | async-start | bytes 8388608 | tf_op jit(solution)/shard_map/all_to_all | solution.py:867
  78.6 72.3 %collective-permute-start.3 = (bf16[256,2048]{1,0:T(8,128)(2,1)}, bf16[256,2048]{1,0:T(8,128)(2,1)}, u32[]{:S(2)}, u32[]{:S(2)}) collective-permute-start(bf16[256,2048]{1,0:T(8,128)(2,1)} %get-tuple-element.34.refs_0_), channel_id=1, source_target_pairs={{0,4},{1,5},{2,6},{3,7},{4,0},{5,1},{6,2},{7,3},{8,12},{9,13},{10,... | collective-permute-start | bytes 3145736 | tf_op jit(solution)/shard_map/ppermute | solution.py:880
  115.6 4.2 %copy-start.4 = (bf16[8,128,128]{2,1,0:T(8,128)(2,1)S(1)}, bf16[8,128,128]{2,1,0:T(8,128)(2,1)}, u32[]{:S(2)}) copy-start(bf16[8,128,128]{2,1,0:T(8,128)(2,1)} %slice.45) | copy-start | bytes 786436
  119.8 56.5 %collective-permute-start.4 = (bf16[256,2048]{1,0:T(8,128)(2,1)}, bf16[256,2048]{1,0:T(8,128)(2,1)}, u32[]{:S(2)}, u32[]{:S(2)}) collective-permute-start(bf16[256,2048]{1,0:T(8,128)(2,1)} %add_states.2.earlier_out.refs_0_), channel_id=1, source_target_pairs={{0,4},{1,5},{2,6},{3,7},{4,0},{5,1},{6,2},{7,3},{8,12},{9,13},{10,... | collective-permute-start | bytes 3145736 | tf_op jit(solution)/shard_map/ppermute | solution.py:880
  155.0 60.9 %all-to-all-start.2 = ((bf16[4,256,2048]{2,1,0:T(8,128)(2,1)}), bf16[4,256,2048]{2,1,0:T(8,128)(2,1)}, u32[]{:S(2)}, u32[]{:S(2)}) async-start(bf16[4,256,2048]{2,1,0:T(8,128)(2,1)} %add_states.3.earlier_out), calls=%async_computation.2 | async-start | bytes 8388608 | tf_op jit(solution)/shard_map/all_to_all | solution.py:890

commit v5 on v4

--- a/solution.py
+++ b/solution.py
@@ -476,6 +476,13 @@
     grad_h[...] = jnp.zeros_like(grad_h)
     grad_h[0:1] = d_rate + behind * beyond[0:1]
     grad_h[1:2] = d_bias + behind * beyond[1:2]
+
+
+def join_kernel(mine, *refs):
+    block = refs[0].shape[0]
+    for k in range(G):
+        at = lax.rem(mine[0, 0] + (G - k), G)
+        refs[G][pl.ds(pl.multiple_of(at * block, block), block), :] = refs[k][...]
 
 
 def add_kernel(terms, *refs):
@@ -623,7 +630,7 @@
         ],
         compiler_params=params("arbitrary"),
         cost_estimate=pl.CostEstimate(
-            flops=2**20 if so_far else 2**33, bytes_accessed=2**12, transcendentals=0
+            flops=2**20 if so_far else 2**37, bytes_accessed=2**12, transcendentals=0
         ),
         name="resp_mid",
     )(
@@ -682,6 +689,17 @@
     )(packed)
 
 
+def join(mine, pieces):
+    block, width = pieces[0].shape
+    return pl.pallas_call(
+        join_kernel,
+        in_specs=[SMEM] + [pl.BlockSpec()] * G,
+        out_shape=sds((G * block, width), bf16),
+        compiler_params=params(),
+        name="join",
+    )(mine, *pieces)
+
+
 def add_states(terms, earlier_out, copies=0):
     rows, width = terms[0].shape
     part = rows // 4
@@ -827,13 +845,12 @@
     x_parts = rows_in[:, :XC].reshape(block, G, GX).transpose(1, 0, 2)
     b_parts = rows_in[:, XC : XC + G * N].reshape(block, G, N).transpose(1, 0, 2)
     parts = jnp.concatenate([x_parts, b_parts], axis=2)
-    v = parts
+    pieces = [lax.dynamic_index_in_dim(parts, mine, 0, False)]
     for k in range(1, G):
         route = [(c * G + q, c * G + (q + k) % G) for c in range(clusters) for q in range(G)]
         sent = lax.dynamic_index_in_dim(parts, (mine + k) % G, 0, False)
-        came = lax.ppermute(sent, "resp", route)
-        v = lax.dynamic_update_index_in_dim(v, came, (mine - k) % G, 0)
-    v = v.reshape(G * block, GX + N)
+        pieces.append(lax.ppermute(sent, "resp", route))
+    v = join(mine.reshape(1, 1), pieces)
 
     def own_channels(a):
         return jnp.concatenate(

time: 259 us -> 296 us (1.14)
  waiting for transfers between devices: 41.6 us -> 83 us
  local copies, waits for them, and re-layouts: 17.2 us -> 10.1 us
  Pallas kernels: 136 us -> 139 us
    all_to_all x1, waiting for transfers between devices: 3.39 us -> 34.6 us  [shards(): d_states = lax.all_to_all(d_states, 'resp', 0, 0, axis_index_groups=inside)]
    ppermute x3, waiting for transfers between devices: 0.01 us -> 24.5 us  [shards(): pieces.append(lax.ppermute(sent, 'resp', route))]
    ppermute x2, waiting for transfers between devices: 13.8 us -> 2.69 us  [across(): return [part] + [lax.ppermute(part, 'resp', route) for route in routes]]
    all_to_all x1, waiting for transfers between devices: 8.53 us -> 0.01 us  [to_all(): return lax.all_to_all(copies, axes, 0, 0, axis_index_groups=groups)]
    dynamic_update_slice x3 -> x0, local copies, waits for them, and re-layouts: 5.8 us -> none  [shards(): v = lax.dynamic_update_index_in_dim(v, came, (mine - k) % G, 0)]
    all_to_all x1, waiting for transfers between devices: 15.8 us -> 21.1 us  [shards(): start = lax.all_to_all(start, 'resp', 0, 0, axis_index_groups=inside)]
    pallas_call x0 -> x1, Pallas kernels: none -> 3.14 us  [join(): pl.pallas_call(join_kernel, in_specs=[SMEM] + [pl.BlockSpec()] * G, out_s...]
  transfers between devices with their start and end apart: 8 -> 8, of which waited for: 4 -> 5; matrix products, arithmetic and copies ran while one was open for 9% -> 4% of each run, Pallas kernels for 48% -> 38%
where the time goes in v5:
time: 296 us; the launch traced here: 295 us
  Pallas kernels  139 us (47%)
  waiting for transfers between devices  83 us (28%)
  blocking collectives  27.2 us (9%)
  starting transfers between devices  23.6 us (8%)
  local copies, waits for them, and re-layouts  10.1 us (3%)
  other arithmetic  8.2 us (3%)
  between operations  3.07 us (1%)
    pallas_call x3, Pallas kernels, response_mid(): pl.pallas_call(functools.partial(resp_mid_kernel, first, handed), grid=(c...  66.6 us
    all_to_all x1, waiting for transfers between devices, shards(): d_states = lax.all_to_all(d_states, 'resp', 0, 0, axis_index_groups=inside)  34.6 us
    ppermute x3, waiting for transfers between devices, shards(): pieces.append(lax.ppermute(sent, 'resp', route))  24.5 us
    pallas_call x1, Pallas kernels, prompt_grad(): pl.pallas_call(functools.partial(prompt_grad_kernel, len(states)), in_spe...  23.8 us
    all_to_all x1, waiting for transfers between devices, shards(): start = lax.all_to_all(start, 'resp', 0, 0, axis_index_groups=inside)  21.1 us
    pallas_call x1, Pallas kernels, prompt_state(): pl.pallas_call(prompt_state_kernel, in_specs=[SMEM] + [pl.BlockSpec()] *...  14.6 us
    all_to_all x1, blocking collectives, sum_over_all(): mine = jnp.sum(lax.all_to_all(slices, axes, 0, 0), axis=0)  14.2 us
    all_to_all x1, blocking collectives, to_all(): return lax.all_to_all(copies, axes, 0, 0, axis_index_groups=groups)  13 us
  transfers between devices with their start and end apart: 8, of which 5 were waited for; matrix products, arithmetic and copies ran while one was open for 4% of the time, Pallas kernels for 38%

profile of v5, /device:TPU:0, one launch (start us, length us, event | category | flops | bytes accessed | tf_op | source)
XLA Modules:
  0.0 294.7 jit_solution(12752831604477167599)
XLA Ops:
  1.5 1.0 slice.32
  2.7 0.9 maximum_maximum_fusion
  3.6 1.0 broadcast_in_dim.14
  4.6 7.3 %all-to-all-start = ((bf16[8,384,128]{2,1,0:T(8,128)(2,1)}), bf16[8,384,128]{2,1,0:T(8,128)(2,1)}, u32[]{:S(2)}, u32[]{:S(2)}) async-start(bf16[8,384,128]{2,1,0:T(8,128)(2,1)} %broadcast_in_dim.14), calls=%async_computation | async-start | bytes 1572864 | tf_op jit(solution)/shard_map/all_to_all | solution.py:802
  11.9 0.1 slice.43
  12.1 0.1 copy.44
  12.3 1.5 fusion.1
  13.9 2.9 collective-permute-start.2
  16.8 1.1 collective-permute-start.1
  17.9 0.1 convert_reduce_fusion.3
  18.0 0.6 slice.39
  18.7 0.7 fusion.9
  19.5 0.3 copy.37
  19.8 0.7 fusion.8.masks
  20.6 0.6 add_bitcast_fusion.place
  21.8 0.6 pad.30.hp
  22.5 0.7 broadcast_in_dim_reshape.3.skip
  23.2 2.0 resp_steps.1
  25.2 1.0 copy.38
  26.2 1.0 copy.39
  27.2 0.6 pad_maximum_fusion.1.wb
  27.8 20.5 %collective-permute-done.2.refs_3_ = bf16[128,2304]{1,0:T(8,128)(2,1)S(1)} collective-permute-done((bf16[128,2304]{1,0:T(8,128)(2,1)}, bf16[128,2304]{1,0:T(8,128)(2,1)S(1)}, u32[]{:S(2)}, u32[]{:S(2)}) %collective-permute-start.2) | collective-permute-done | bytes 589856 | tf_op jit(solution)/shard_map/ppermute | solution.py:852
  48.3 4.0 %collective-permute-done.1.refs_2_ = bf16[128,2304]{1,0:T(8,128)(2,1)} collective-permute-done((bf16[128,2304]{1,0:T(8,128)(2,1)}, bf16[128,2304]{1,0:T(8,128)(2,1)}, u32[]{:S(2)}, u32[]{:S(2)}) %collective-permute-start.1) | collective-permute-done | bytes 589856 | tf_op jit(solution)/shard_map/ppermute | solution.py:852
  52.4 3.1 %join.1.v = bf16[512,2304]{1,0:T(8,128)(2,1)} custom-call(s32[1,1]{1,0:T(1,128)} %bitcast.13.mine, bf16[128,2304]{1,0:T(8,128)(2,1)} %get-tuple-element.64.refs_0_, bf16[128,2304]{1,0:T(8,128)(2,1)} %collective-permute-done.refs_1_, bf16[128,2304]{1,0:T(8,128)(2,1)} %collective-permute-done.1.refs_2_, bf16[128,2304]{1,0:T(8,128)(2,1)} %copy-done.3), custom_call_target="tpu_custom_call" | custom-call | tf_op jit(solution)/shard_map/join/pallas_call | solution.py:694
  55.5 0.9 constant_dynamic-slice_fusion.5
  56.5 0.8 pad_convert_fusion.1.tail_c.tail_x.tail_b
  57.3 0.6 pad_maximum_fusion.halo
  58.0 1.7 slice.45
  59.6 14.6 %prompt_state.1 = (bf16[256,2048]{1,0:T(8,128)(2,1)}, f32[512,128]{1,0:T(8,128)}, f32[512,128]{1,0:T(8,128)}, f32[8,128]{1,0:T(8,128)}) custom-call(s32[1,2]{1,0:T(1,128)} %add_bitcast_fusion.place, bf16[512,2304]{1,0:T(8,128)(2,1)} %join.1.v, f32[8,2304]{1,0:T(8,128)} %pad_maximum_fusion.halo, bf16[1024,128]{1,0:T(8,128)(2,1)} %bitcast.71, ...), custom_call_target="tpu_custom_call" | custom-call | flops 536870912 | bytes 4194304 | tf_op jit(solution)/shard_map/prompt_state/pallas_call | solution.py:734
  74.2 2.4 collective-permute-start.3
  76.6 1.3 convert_reduce_fusion.4
  78.6 7.9 %resp_state.1 = (bf16[4,256,2048]{2,1,0:T(8,128)(2,1)}, bf16[256,8192]{1,0:T(8,128)(2,1)}, bf16[256,1024]{1,0:T(8,128)(2,1)}) custom-call(f32[1,1]{1,0:T(1,128)} %bitcast.8.adv.scale, bf16[256,10240]{1,0:T(8,128)(2,1)} %bitcast.52, f32[8,10240]{1,0:T(8,128)} %pad_convert_fusion.1.tail_c.tail_x.tail_b, f32[8,10240]{1,0:T(8,128)} %copy-done, ...), custom_call_target="tpu_custom_call" | custom-call | flops 1073741824 | bytes 14680064 | tf_op jit(solution)/shard_map/resp_state/pallas_call | solution.py:536
  86.5 5.0 %all-to-all-start.1 = ((bf16[4,256,2048]{2,1,0:T(8,128)(2,1)}), bf16[4,256,2048]{2,1,0:T(8,128)(2,1)}, u32[]{:S(2)}, u32[]{:S(2)}) async-start(bf16[4,256,2048]{2,1,0:T(8,128)(2,1)} %get-tuple-element.38), calls=%async_computation.1 | async-start | bytes 8388608 | tf_op jit(solution)/shard_map/all_to_all | solution.py:884
  91.6 33.7 %resp_mid.3 = (f32[8,8192]{1,0:T(8,128)}, f32[8,1024]{1,0:T(8,128)}, f32[256,1024]{1,0:T(8,128)}, f32[520,128]{1,0:T(8,128)}) custom-call(s32[1,1]{1,0:T(1,128)S(6)} %copy.52.len_ref, bf16[256,10240]{1,0:T(8,128)(2,1)} %bitcast.53, bf16[256,10240]{1,0:T(8,128)(2,1)} %bitcast.54, f32[8,10240]{1,0:T(8,128)} %pad_convert_fusion.1.tail_c.tail_x.tail_b, ...), custom_call_target="tpu_custom_call" | custom-call | flops 137438953472 | bytes 4096 | tf_op jit(solution)/shard_map/resp_mid/pallas_call | solution.py:573
  125.2 34.6 %all-to-all-done.1.refs_0_.refs_1_.refs_2_.refs_3_ = bf16[4,256,2048]{2,1,0:T(8,128)(2,1)} async-done(((bf16[4,256,2048]{2,1,0:T(8,128)(2,1)}), bf16[4,256,2048]{2,1,0:T(8,128)(2,1)}, u32[]{:S(2)}, u32[]{:S(2)}) %all-to-all-start.1) | async-done | bytes 4194336 | tf_op jit(solution)/shard_map/all_to_all | solution.py:884
  159.9 4.2 %add_states.2.earlier_out.refs_0_ = bf16[256,2048]{1,0:T(8,128)(2,1)} custom-call(bf16[4,256,2048]{2,1,0:T(8,128)(2,1)} %all-to-all-done.1.refs_0_.refs_1_.refs_2_.refs_3_, bf16[4,256,2048]{2,1,0:T(8,128)(2,1)} %all-to-all-done.1.refs_0_.refs_1_.refs_2_.refs_3_, bf16[4,256,2048]{2,1,0:T(8,128)(2,1)} %all-to-all-done.1.refs_0_.refs_1_.refs_2_.refs_3_, ...), custom_call_target="tpu_custom_call" | custom-call | flops 4194304 | bytes 6291456 | tf_op jit(solution)/shard_map/add_states/pallas_call | solution.py:716
  164.0 0.7 constant_dynamic-slice_fusion.dt_mine
  164.7 16.5 %resp_mid.4 = (f32[8,8192]{1,0:T(8,128)}, f32[8,1024]{1,0:T(8,128)}, f32[256,1024]{1,0:T(8,128)}, f32[520,128]{1,0:T(8,128)}) custom-call(s32[1,1]{1,0:T(1,128)S(6)} %copy.52.len_ref, bf16[256,10240]{1,0:T(8,128)(2,1)} %bitcast.55, bf16[256,10240]{1,0:T(8,128)(2,1)} %bitcast.56, ...), custom_call_target="tpu_custom_call", output_to_operand_aliasing={{0}: (15, {}), {1}: (16, {}), {2}: (17, {})} | custom-call | flops 1048576 | bytes 4096 | tf_op jit(solution)/shard_map/resp_mid/pallas_call | solution.py:573
  181.2 4.2 %add_states.3.earlier_out = bf16[4,256,2048]{2,1,0:T(8,128)(2,1)} custom-call(bf16[256,2048]{1,0:T(8,128)(2,1)} %get-tuple-element.34.refs_0_, bf16[256,2048]{1,0:T(8,128)(2,1)} %collective-permute-done.3.refs_1_, f32[520,128]{1,0:T(8,128)} %get-tuple-element.44.refs_2_.refs_3_), custom_call_target="tpu_custom_call" | custom-call | flops 4194304 | bytes 6291456 | tf_op jit(solution)/shard_map/add_states/pallas_call | solution.py:716
  185.4 4.8 %all-to-all-start.2 = ((bf16[4,256,2048]{2,1,0:T(8,128)(2,1)}), bf16[4,256,2048]{2,1,0:T(8,128)(2,1)}, u32[]{:S(2)}, u32[]{:S(2)}) async-start(bf16[4,256,2048]{2,1,0:T(8,128)(2,1)} %add_states.3.earlier_out), calls=%async_computation.2 | async-start | bytes 8388608 | tf_op jit(solution)/shard_map/all_to_all | solution.py:907
  190.3 16.4 %resp_mid.5 = (f32[8,8192]{1,0:T(8,128)}, f32[8,1024]{1,0:T(8,128)}, f32[256,1024]{1,0:T(8,128)}, f32[520,128]{1,0:T(8,128)}) custom-call(s32[1,1]{1,0:T(1,128)S(6)} %copy.52.len_ref, bf16[256,10240]{1,0:T(8,128)(2,1)} %bitcast.57, bf16[256,10240]{1,0:T(8,128)(2,1)} %bitcast.58, ...), custom_call_target="tpu_custom_call", output_to_operand_aliasing={{0}: (15, {}), {1}: (16, {}), {2}: (17, {})} | custom-call | flops 1048576 | bytes 4096 | tf_op jit(solution)/shard_map/resp_mid/pallas_call | solution.py:573
  206.7 2.7 collective-permute-done.4.refs_1_
  209.4 23.8 %prompt_grad.1 = (f32[8,2304]{1,0:T(8,128)}, f32[8,128]{1,0:T(8,128)}) custom-call(s32[1,2]{1,0:T(1,128)} %add_bitcast_fusion.place, bf16[512,2304]{1,0:T(8,128)(2,1)} %join.1.v, f32[8,2304]{1,0:T(8,128)} %pad_maximum_fusion.halo, bf16[512,128]{1,0:T(8,128)(2,1)} %constant_dynamic-slice_fusion.dt_mine, f32[512,8]{1,0:T(8,128)} %fusion.8.masks, ...), custom_call_target="tpu_custom_call" | custom-call | flops 68719476736 | bytes 8388608 | tf_op jit(solution)/shard_map/prompt_grad/pallas_call | solution.py:762
  233.2 21.1 %all-to-all-done.2.start = bf16[4,256,2048]{2,1,0:T(8,128)(2,1)} async-done(((bf16[4,256,2048]{2,1,0:T(8,128)(2,1)}), bf16[4,256,2048]{2,1,0:T(8,128)(2,1)}, u32[]{:S(2)}, u32[]{:S(2)}) %all-to-all-start.2) | async-done | bytes 4194336 | tf_op jit(solution)/shard_map/all_to_all | solution.py:907
  254.3 11.3 %resp_end.1 = f32[64,8,128]{2,1,0:T(8,128)} custom-call(s32[1,2]{1,0:T(1,128)} %add_bitcast_fusion.place, f32[1,1]{1,0:T(1,128)} %bitcast.8.adv.scale, bf16[256,10240]{1,0:T(8,128)(2,1)} %bitcast.59, f32[8,10240]{1,0:T(8,128)} %pad_convert_fusion.1.tail_c.tail_x.tail_b, f32[8,10240]{1,0:T(8,128)} %copy-done, bf16[256,1024]{1,0:T(8,128)(2,1)} %get-tuple-element.32.c_act, ...), custom_call_target="tpu_custom_call" | custom-call | flops 2147483648 | bytes 12582912 | tf_op jit(solution)/shard_map/resp_end/pallas_call | solution.py:649
  265.6 14.2 %all_to_all.25 = f32[32,2,8,128]{3,2,1,0:T(8,128)S(1)} all-to-all(f32[32,2,8,128]{3,2,1,0:T(8,128)} %bitcast.73), channel_id=1, replica_groups=mesh['group'=4,'resp'=8] {'group','resp'}, dimensions={0} | all-to-all | bytes 524288 | tf_op jit(solution)/shard_map/all_to_all | solution.py:807
  279.8 13.0 %all_to_all.26 = f32[32,2,8,128]{3,2,1,0:T(8,128)} all-to-all(f32[32,2,8,128]{3,2,1,0:T(8,128)S(1)} %broadcast_in_dim.17), channel_id=1, replica_groups=mesh['group'=4,'resp'=8] {'group','resp'}, dimensions={0} | all-to-all | bytes 524288 | tf_op jit(solution)/shard_map/all_to_all | solution.py:802
  292.9 1.8 unpack.1
  (46 shorter events, 0.8 us)
Async XLA Ops:
  0.6 11.3 %copy-start.1 = (bf16[1,128,10240]{2,1,0:T(8,128)(2,1)S(1)}, bf16[1,128,10240]{2,1,0:T(8,128)(2,1)}, u32[]{:S(2)}) copy-start(bf16[1,128,10240]{2,1,0:T(8,128)(2,1)} %param.11) | copy-start | bytes 7864324
  4.6 50.9 %all-to-all-start = ((bf16[8,384,128]{2,1,0:T(8,128)(2,1)}), bf16[8,384,128]{2,1,0:T(8,128)(2,1)}, u32[]{:S(2)}, u32[]{:S(2)}) async-start(bf16[8,384,128]{2,1,0:T(8,128)(2,1)} %broadcast_in_dim.14), calls=%async_computation | async-start | bytes 1572864 | tf_op jit(solution)/shard_map/all_to_all | solution.py:802
  12.3 5.6 %copy-start.7 = (s32[1,4]{1,0:T(1,128)S(1)}, s32[1,4]{1,0:T(1,128)}, u32[]{:S(2)}) copy-start(s32[1,4]{1,0:T(1,128)} %param.13) | copy-start | bytes 52
  12.3 6.3 %copy-start.4 = (f32[4,10240]{1,0:T(4,128)S(1)}, f32[4,10240]{1,0:T(4,128)}, u32[]{:S(2)}) copy-start(f32[4,10240]{1,0:T(4,128)} %param.19) | copy-start | bytes 491524
  12.3 6.3 %copy-start.5 = (f32[10240]{0:T(1024)S(1)}, f32[10240]{0:T(1024)}, u32[]{:S(2)}) copy-start(f32[10240]{0:T(1024)} %param.20) | copy-start | bytes 122884
  12.3 8.2 %copy-start.6 = (f32[3,128]{1,0:T(4,128)S(1)}, f32[3,128]{1,0:T(4,128)}, u32[]{:S(2)}) copy-start(f32[3,128]{1,0:T(4,128)} %param.21) | copy-start | bytes 4612
  13.9 34.5 %collective-permute-start.2 = (bf16[128,2304]{1,0:T(8,128)(2,1)}, bf16[128,2304]{1,0:T(8,128)(2,1)S(1)}, u32[]{:S(2)}, u32[]{:S(2)}) collective-permute-start(bf16[128,2304]{1,0:T(8,128)(2,1)} %get-tuple-element.63), channel_id=1, source_target_pairs={{0,3},{1,0},{2,1},{3,2},{4,7},{5,4},{6,5},{7,6},{8,11},{9,8},{10,9... | collective-permute-start | bytes 1769480 | tf_op jit(solution)/shard_map/ppermute | solution.py:852
  16.8 31.6 %collective-permute-start = (bf16[128,2304]{1,0:T(8,128)(2,1)}, bf16[128,2304]{1,0:T(8,128)(2,1)}, u32[]{:S(2)}, u32[]{:S(2)}) collective-permute-start(bf16[128,2304]{1,0:T(8,128)(2,1)} %get-tuple-element.65), channel_id=1, source_target_pairs={{0,1},{1,2},{2,3},{3,0},{4,5},{5,6},{6,7},{7,4},{8,9},{9,10},{10,1... | collective-permute-start | bytes 1769480 | tf_op jit(solution)/shard_map/ppermute | solution.py:852
  16.8 35.6 %collective-permute-start.1 = (bf16[128,2304]{1,0:T(8,128)(2,1)}, bf16[128,2304]{1,0:T(8,128)(2,1)}, u32[]{:S(2)}, u32[]{:S(2)}) collective-permute-start(bf16[128,2304]{1,0:T(8,128)(2,1)} %get-tuple-element.66), channel_id=1, source_target_pairs={{0,2},{1,3},{2,0},{3,1},{4,6},{5,7},{6,4},{7,5},{8,10},{9,11},{10,... | collective-permute-start | bytes 1769480 | tf_op jit(solution)/shard_map/ppermute | solution.py:852
  18.7 36.8 %copy-start = (f32[8,10240]{1,0:T(8,128)}, f32[8,10240]{1,0:T(8,128)S(1)}, u32[]{:S(2)}) copy-start(f32[8,10240]{1,0:T(8,128)S(1)} %select_maximum_fusion.wb_c.wb_x.wb_b) | copy-start | bytes 983044
  48.3 4.0 %copy-start.3 = (bf16[128,2304]{1,0:T(8,128)(2,1)}, bf16[128,2304]{1,0:T(8,128)(2,1)S(1)}, u32[]{:S(2)}) copy-start(bf16[128,2304]{1,0:T(8,128)(2,1)S(1)} %collective-permute-done.2.refs_3_) | copy-start | bytes 1769476
  74.2 107.0 %collective-permute-start.3 = (bf16[256,2048]{1,0:T(8,128)(2,1)}, bf16[256,2048]{1,0:T(8,128)(2,1)}, u32[]{:S(2)}, u32[]{:S(2)}) collective-permute-start(bf16[256,2048]{1,0:T(8,128)(2,1)} %get-tuple-element.34.refs_0_), channel_id=1, source_target_pairs={{0,4},{1,5},{2,6},{3,7},{4,0},{5,1},{6,2},{7,3},{8,12},{9,13},{10,... | collective-permute-start | bytes 3145736 | tf_op jit(solution)/shard_map/ppermute | solution.py:897
  86.5 73.3 %all-to-all-start.1 = ((bf16[4,256,2048]{2,1,0:T(8,128)(2,1)}), bf16[4,256,2048]{2,1,0:T(8,128)(2,1)}, u32[]{:S(2)}, u32[]{:S(2)}) async-start(bf16[4,256,2048]{2,1,0:T(8,128)(2,1)} %get-tuple-element.38), calls=%async_computation.1 | async-start | bytes 8388608 | tf_op jit(solution)/shard_map/all_to_all | solution.py:884
  159.8 4.2 %copy-start.2 = (bf16[8,128,128]{2,1,0:T(8,128)(2,1)S(1)}, bf16[8,128,128]{2,1,0:T(8,128)(2,1)}, u32[]{:S(2)}) copy-start(bf16[8,128,128]{2,1,0:T(8,128)(2,1)} %slice.45) | copy-start | bytes 786436
  164.0 45.4 %collective-permute-start.4 = (bf16[256,2048]{1,0:T(8,128)(2,1)}, bf16[256,2048]{1,0:T(8,128)(2,1)}, u32[]{:S(2)}, u32[]{:S(2)}) collective-permute-start(bf16[256,2048]{1,0:T(8,128)(2,1)} %add_states.2.earlier_out.refs_0_), channel_id=1, source_target_pairs={{0,4},{1,5},{2,6},{3,7},{4,0},{5,1},{6,2},{7,3},{8,12},{9,13},{10,... | collective-permute-start | bytes 3145736 | tf_op jit(solution)/shard_map/ppermute | solution.py:897
  185.4 68.9 %all-to-all-start.2 = ((bf16[4,256,2048]{2,1,0:T(8,128)(2,1)}), bf16[4,256,2048]{2,1,0:T(8,128)(2,1)}, u32[]{:S(2)}, u32[]{:S(2)}) async-start(bf16[4,256,2048]{2,1,0:T(8,128)(2,1)} %add_states.3.earlier_out), calls=%async_computation.2 | async-start | bytes 8388608 | tf_op jit(solution)/shard_map/all_to_all | solution.py:907

commit v6 on v4

--- a/solution.py
+++ b/solution.py
@@ -698,7 +698,7 @@
     return pl.pallas_call(
         functools.partial(add_kernel, len(terms)),
         grid=(4,),
-        in_specs=blocks + [pl.BlockSpec(memory_space=pl.ANY)],
+        in_specs=blocks + [pl.BlockSpec(memory_space=pl.ANY)] * len(earlier_out),
         out_specs=many if copies else one,
         out_shape=sds((copies, rows, width) if copies else (rows, width), bf16),
         compiler_params=params("arbitrary"),
@@ -706,7 +706,7 @@
             flops=8 * rows * width, bytes_accessed=12 * rows * width, transcendentals=0
         ),
         name="add_states",
-    )(*terms, earlier_out)
+    )(*terms, *earlier_out)
 
 
 def prompt_state(place, v, halo, dt_all, masks, wb, hp):
@@ -882,10 +882,10 @@
     part, weight, p_step, beyond = prompt_state(place, v, halo, dt_all, masks, wb_mine, hp)
     parts_of_start = across(part)
     grads = mid(0, 2, weight)
-    part = add_states(d_states, grads[3])
+    part = add_states(d_states, (grads[3], *parts_of_start[1:]))
     parts_of_grad = across(part)
-    grads = mid(2, 1, part, grads)
-    start = add_states(parts_of_start, grads[3], copies=G)
+    start = add_states(parts_of_start, (part,), copies=G)
+    grads = mid(2, 1, start, grads)
     grad_x, grad_b, dc, sums = mid(3, 1, start, grads)
     start = lax.all_to_all(start, "resp", 0, 0, axis_index_groups=inside)
     p_grad, p_heads = prompt_grad(

time: 259 us -> 249 us (0.961)
  waiting for transfers between devices: 41.6 us -> 32.1 us
    all_to_all x1, waiting for transfers between devices: 15.8 us -> 8.53 us  [shards(): start = lax.all_to_all(start, 'resp', 0, 0, axis_index_groups=inside)]
    all_to_all x1, waiting for transfers between devices: 3.39 us -> 0.01 us  [shards(): d_states = lax.all_to_all(d_states, 'resp', 0, 0, axis_index_groups=inside)]
where the time goes in v6:
time: 249 us; the launch traced here: 248 us
  Pallas kernels  136 us (55%)
  waiting for transfers between devices  32.1 us (13%)
  blocking collectives  27.3 us (11%)
  starting transfers between devices  22.4 us (9%)
  local copies, waits for them, and re-layouts  17.2 us (7%)
  other arithmetic  9.58 us (4%)
  between operations  3.11 us (1%)
    pallas_call x3, Pallas kernels, response_mid(): pl.pallas_call(functools.partial(resp_mid_kernel, first, handed), grid=(c...  66.3 us
    pallas_call x1, Pallas kernels, prompt_grad(): pl.pallas_call(functools.partial(prompt_grad_kernel, len(states)), in_spe...  24 us
    ppermute x2, waiting for transfers between devices, across(): return [part] + [lax.ppermute(part, 'resp', route) for route in routes]  15 us
    pallas_call x1, Pallas kernels, prompt_state(): pl.pallas_call(prompt_state_kernel, in_specs=[SMEM] + [pl.BlockSpec()] *...  14.6 us
    all_to_all x1, blocking collectives, sum_over_all(): mine = jnp.sum(lax.all_to_all(slices, axes, 0, 0), axis=0)  14.3 us
    all_to_all x1, blocking collectives, to_all(): return lax.all_to_all(copies, axes, 0, 0, axis_index_groups=groups)  13 us
    pallas_call x1, Pallas kernels, response_end(): pl.pallas_call(resp_end_kernel, grid=(G,), in_specs=[SMEM, SMEM, pl.Block...  11.1 us
    all_to_all x1, waiting for transfers between devices, to_all(): return lax.all_to_all(copies, axes, 0, 0, axis_index_groups=groups)  8.55 us
  transfers between devices with their start and end apart: 8, of which 4 were waited for; matrix products, arithmetic and copies ran while one was open for 9% of the time, Pallas kernels for 48%

profile of v6, /device:TPU:0, one launch (start us, length us, event | category | flops | bytes accessed | tf_op | source)
XLA Modules:
  0.0 247.7 jit_solution(18394869757863640693)
XLA Ops:
  1.5 1.0 slice.32
  2.7 0.9 maximum_maximum_fusion
  3.6 1.0 broadcast_in_dim.43
  4.6 7.3 %all-to-all-start = ((bf16[8,384,128]{2,1,0:T(8,128)(2,1)}), bf16[8,384,128]{2,1,0:T(8,128)(2,1)}, u32[]{:S(2)}, u32[]{:S(2)}) async-start(bf16[8,384,128]{2,1,0:T(8,128)(2,1)} %broadcast_in_dim.43), calls=%async_computation | async-start | bytes 1572864 | tf_op jit(solution)/shard_map/all_to_all | solution.py:784
  12.3 1.3 copy-done
  13.6 1.2 fusion.5
  14.8 2.9 %collective-permute-start.2 = (bf16[128,2304]{1,0:T(8,128)(2,1)}, bf16[128,2304]{1,0:T(8,128)(2,1)}, u32[]{:S(2)}, u32[]{:S(2)}) collective-permute-start(bf16[128,2304]{1,0:T(8,128)(2,1)} %get-tuple-element.63), channel_id=1, source_target_pairs={{0,3},{1,0},{2,1},{3,2},{4,7},{5,4},{6,5},{7,6},{8,11},{9,8},{10,9... | collective-permute-start | bytes 1769480 | tf_op jit(solution)/shard_map/ppermute | solution.py:834
  17.7 1.1 collective-permute-start.1
  19.6 0.6 slice.39
  20.2 0.7 fusion.7
  21.0 0.6 pad.30.hp
  21.6 2.0 resp_steps.1
  23.7 8.5 %all-to-all-done = bf16[8,384,128]{2,1,0:T(8,128)(2,1)} async-done(((bf16[8,384,128]{2,1,0:T(8,128)(2,1)}), bf16[8,384,128]{2,1,0:T(8,128)(2,1)}, u32[]{:S(2)}, u32[]{:S(2)}) %all-to-all-start) | async-done | bytes 786464 | tf_op jit(solution)/shard_map/all_to_all | solution.py:784
  32.3 0.9 constant_dynamic-slice_fusion.5
  33.2 0.8 pad_convert_fusion.1.tail_c.tail_x.tail_b
  33.9 1.4 convert_reduce_fusion.4
  35.9 7.9 %resp_state.1 = (bf16[4,256,2048]{2,1,0:T(8,128)(2,1)}, bf16[256,8192]{1,0:T(8,128)(2,1)}, bf16[256,1024]{1,0:T(8,128)(2,1)}) custom-call(f32[1,1]{1,0:T(1,128)} %bitcast.8.adv.scale, bf16[256,10240]{1,0:T(8,128)(2,1)} %bitcast.56, f32[8,10240]{1,0:T(8,128)} %pad_convert_fusion.1.tail_c.tail_x.tail_b, f32[8,10240]{1,0:T(8,128)} %copy-done.2, ...), custom_call_target="tpu_custom_call" | custom-call | flops 1073741824 | bytes 14680064 | tf_op jit(solution)/shard_map/resp_state/pallas_call | solution.py:529
  43.8 5.2 %all-to-all-start.1 = ((bf16[4,256,2048]{2,1,0:T(8,128)(2,1)}), bf16[4,256,2048]{2,1,0:T(8,128)(2,1)}, u32[]{:S(2)}, u32[]{:S(2)}) async-start(bf16[4,256,2048]{2,1,0:T(8,128)(2,1)} %get-tuple-element.35), calls=%async_computation.1 | async-start | bytes 8388608 | tf_op jit(solution)/shard_map/all_to_all | solution.py:867
  49.1 0.8 constant_dynamic-slice_fusion.2
  49.9 0.6 pad_maximum_fusion.2.wb
  50.5 0.6 add_bitcast_fusion.place
  51.1 0.3 copy.37
  51.5 0.8 fusion.6.masks
  52.2 1.6 pad_maximum_fusion
  53.8 2.0 bitcast_dynamic-update-slice_fusion.2
  55.8 1.9 bitcast_dynamic-update-slice_fusion.1
  57.7 1.9 bitcast_dynamic-update-slice_fusion
  59.7 1.7 slice.45
  61.5 0.6 pad_maximum_fusion.1.halo
  62.1 14.6 %prompt_state.1 = (bf16[256,2048]{1,0:T(8,128)(2,1)}, f32[512,128]{1,0:T(8,128)}, f32[512,128]{1,0:T(8,128)}, f32[8,128]{1,0:T(8,128)}) custom-call(s32[1,2]{1,0:T(1,128)} %add_bitcast_fusion.place, bf16[512,2304]{1,0:T(8,128)(2,1)} %bitcast.22.v, f32[8,2304]{1,0:T(8,128)} %pad_maximum_fusion.1.halo, bf16[1024,128]{1,0:T(8,128)(2,1)} %bitcast.78, ...), custom_call_target="tpu_custom_call" | custom-call | flops 536870912 | bytes 4194304 | tf_op jit(solution)/shard_map/prompt_state/pallas_call | solution.py:716
  76.7 0.3 collective-permute-start.3
  77.1 0.7 broadcast_in_dim_reshape.3.skip
  77.9 1.0 copy.39
  79.0 33.6 %resp_mid.3 = (f32[8,8192]{1,0:T(8,128)}, f32[8,1024]{1,0:T(8,128)}, f32[256,1024]{1,0:T(8,128)}, f32[520,128]{1,0:T(8,128)}) custom-call(s32[1,1]{1,0:T(1,128)S(6)} %copy.55.len_ref, bf16[256,10240]{1,0:T(8,128)(2,1)} %bitcast.57, bf16[256,10240]{1,0:T(8,128)(2,1)} %bitcast.58, f32[8,10240]{1,0:T(8,128)} %pad_convert_fusion.1.tail_c.tail_x.tail_b, ...), custom_call_target="tpu_custom_call" | custom-call | flops 8589934592 | bytes 4096 | tf_op jit(solution)/shard_map/resp_mid/pallas_call | solution.py:566
  112.6 11.6 %collective-permute-done.3.refs_5_.refs_1_ = bf16[256,2048]{1,0:T(8,128)(2,1)} collective-permute-done((bf16[256,2048]{1,0:T(8,128)(2,1)}, bf16[256,2048]{1,0:T(8,128)(2,1)}, u32[]{:S(2)}, u32[]{:S(2)}) %collective-permute-start.3) | collective-permute-done | bytes 1048608 | tf_op jit(solution)/shard_map/ppermute | solution.py:880
  124.1 4.2 %add_states.2.refs_2_.refs_0_ = bf16[256,2048]{1,0:T(8,128)(2,1)} custom-call(bf16[4,256,2048]{2,1,0:T(8,128)(2,1)} %all-to-all-done.1.refs_0_.refs_1_.refs_2_.refs_3_, bf16[4,256,2048]{2,1,0:T(8,128)(2,1)} %all-to-all-done.1.refs_0_.refs_1_.refs_2_.refs_3_, bf16[4,256,2048]{2,1,0:T(8,128)(2,1)} %all-to-all-done.1.refs_0_.refs_1_.refs_2_.refs_3_, ...), custom_call_target="tpu_custom_call" | custom-call | flops 4194304 | bytes 6291456 | tf_op jit(solution)/shard_map/add_states/pallas_call | solution.py:698
  128.3 0.7 constant_dynamic-slice_fusion.dt_mine
  129.0 4.2 %add_states.3.earlier_out = bf16[4,256,2048]{2,1,0:T(8,128)(2,1)} custom-call(bf16[256,2048]{1,0:T(8,128)(2,1)} %get-tuple-element.34.refs_0_, bf16[256,2048]{1,0:T(8,128)(2,1)} %collective-permute-done.3.refs_5_.refs_1_, bf16[256,2048]{1,0:T(8,128)(2,1)} %add_states.2.refs_2_.refs_0_), custom_call_target="tpu_custom_call" | custom-call | flops 4194304 | bytes 6291456 | tf_op jit(solution)/shard_map/add_states/pallas_call | solution.py:698
  133.2 5.6 %all-to-all-start.2 = ((bf16[4,256,2048]{2,1,0:T(8,128)(2,1)}), bf16[4,256,2048]{2,1,0:T(8,128)(2,1)}, u32[]{:S(2)}, u32[]{:S(2)}) async-start(bf16[4,256,2048]{2,1,0:T(8,128)(2,1)} %add_states.3.earlier_out), calls=%async_computation.2 | async-start | bytes 8388608 | tf_op jit(solution)/shard_map/all_to_all | solution.py:890
  138.8 16.3 %resp_mid.4 = (f32[8,8192]{1,0:T(8,128)}, f32[8,1024]{1,0:T(8,128)}, f32[256,1024]{1,0:T(8,128)}, f32[520,128]{1,0:T(8,128)}) custom-call(s32[1,1]{1,0:T(1,128)S(6)} %copy.55.len_ref, bf16[256,10240]{1,0:T(8,128)(2,1)} %bitcast.59, bf16[256,10240]{1,0:T(8,128)(2,1)} %bitcast.60, ...), custom_call_target="tpu_custom_call", output_to_operand_aliasing={{0}: (15, {}), {1}: (16, {}), {2}: (17, {})} | custom-call | flops 1048576 | bytes 4096 | tf_op jit(solution)/shard_map/resp_mid/pallas_call | solution.py:566
  155.1 16.4 %resp_mid.5 = (f32[8,8192]{1,0:T(8,128)}, f32[8,1024]{1,0:T(8,128)}, f32[256,1024]{1,0:T(8,128)}, f32[520,128]{1,0:T(8,128)}) custom-call(s32[1,1]{1,0:T(1,128)S(6)} %copy.55.len_ref, bf16[256,10240]{1,0:T(8,128)(2,1)} %bitcast.61, bf16[256,10240]{1,0:T(8,128)(2,1)} %bitcast.62, ...), custom_call_target="tpu_custom_call", output_to_operand_aliasing={{0}: (15, {}), {1}: (16, {}), {2}: (17, {})} | custom-call | flops 1048576 | bytes 4096 | tf_op jit(solution)/shard_map/resp_mid/pallas_call | solution.py:566
  171.5 3.4 %collective-permute-done.4.refs_1_ = bf16[256,2048]{1,0:T(8,128)(2,1)} collective-permute-done((bf16[256,2048]{1,0:T(8,128)(2,1)}, bf16[256,2048]{1,0:T(8,128)(2,1)}, u32[]{:S(2)}, u32[]{:S(2)}) %collective-permute-start.4) | collective-permute-done | bytes 1048608 | tf_op jit(solution)/shard_map/ppermute | solution.py:880
  174.9 24.0 %prompt_grad.1 = (f32[8,2304]{1,0:T(8,128)}, f32[8,128]{1,0:T(8,128)}) custom-call(s32[1,2]{1,0:T(1,128)} %add_bitcast_fusion.place, bf16[512,2304]{1,0:T(8,128)(2,1)} %bitcast.22.v, f32[8,2304]{1,0:T(8,128)} %pad_maximum_fusion.1.halo, bf16[512,128]{1,0:T(8,128)(2,1)} %constant_dynamic-slice_fusion.dt_mine, f32[512,8]{1,0:T(8,128)} %fusion.6.masks, ...), custom_call_target="tpu_custom_call" | custom-call | flops 68719476736 | bytes 8388608 | tf_op jit(solution)/shard_map/prompt_grad/pallas_call | solution.py:744
  199.0 8.5 %all-to-all-done.2.start = bf16[4,256,2048]{2,1,0:T(8,128)(2,1)} async-done(((bf16[4,256,2048]{2,1,0:T(8,128)(2,1)}), bf16[4,256,2048]{2,1,0:T(8,128)(2,1)}, u32[]{:S(2)}, u32[]{:S(2)}) %all-to-all-start.2) | async-done | bytes 4194336 | tf_op jit(solution)/shard_map/all_to_all | solution.py:890
  207.5 11.1 %resp_end.1 = f32[64,8,128]{2,1,0:T(8,128)} custom-call(s32[1,2]{1,0:T(1,128)} %add_bitcast_fusion.place, f32[1,1]{1,0:T(1,128)} %bitcast.8.adv.scale, bf16[256,10240]{1,0:T(8,128)(2,1)} %bitcast.63, f32[8,10240]{1,0:T(8,128)} %pad_convert_fusion.1.tail_c.tail_x.tail_b, f32[8,10240]{1,0:T(8,128)} %copy-done.2, bf16[256,1024]{1,0:T(8,128)(2,1)} %get-tuple-element.32.c_act, ...), custom_call_target="tpu_custom_call" | custom-call | flops 2147483648 | bytes 12582912 | tf_op jit(solution)/shard_map/resp_end/pallas_call | solution.py:642
  218.5 14.3 %all_to_all.25 = f32[32,2,8,128]{3,2,1,0:T(8,128)S(1)} all-to-all(f32[32,2,8,128]{3,2,1,0:T(8,128)} %bitcast.80), channel_id=1, replica_groups=mesh['group'=4,'resp'=8] {'group','resp'}, dimensions={0} | all-to-all | bytes 524288 | tf_op jit(solution)/shard_map/all_to_all | solution.py:789
  232.9 13.0 %all_to_all.26 = f32[32,2,8,128]{3,2,1,0:T(8,128)} all-to-all(f32[32,2,8,128]{3,2,1,0:T(8,128)S(1)} %broadcast_in_dim.49), channel_id=1, replica_groups=mesh['group'=4,'resp'=8] {'group','resp'}, dimensions={0} | all-to-all | bytes 524288 | tf_op jit(solution)/shard_map/all_to_all | solution.py:784
  245.9 1.8 unpack.1
  (53 shorter events, 1.2 us)
Async XLA Ops:
  0.6 11.2 %copy-start.3 = (bf16[1,128,10240]{2,1,0:T(8,128)(2,1)S(1)}, bf16[1,128,10240]{2,1,0:T(8,128)(2,1)}, u32[]{:S(2)}) copy-start(bf16[1,128,10240]{2,1,0:T(8,128)(2,1)} %param.11) | copy-start | bytes 7864324
  4.6 27.7 %all-to-all-start = ((bf16[8,384,128]{2,1,0:T(8,128)(2,1)}), bf16[8,384,128]{2,1,0:T(8,128)(2,1)}, u32[]{:S(2)}, u32[]{:S(2)}) async-start(bf16[8,384,128]{2,1,0:T(8,128)(2,1)} %broadcast_in_dim.43), calls=%async_computation | async-start | bytes 1572864 | tf_op jit(solution)/shard_map/all_to_all | solution.py:784
  12.2 1.3 copy-start
  12.2 7.3 %copy-start.9 = (s32[1,4]{1,0:T(1,128)S(1)}, s32[1,4]{1,0:T(1,128)}, u32[]{:S(2)}) copy-start(s32[1,4]{1,0:T(1,128)} %param.13) | copy-start | bytes 52
  12.2 8.7 %copy-start.8 = (f32[3,128]{1,0:T(4,128)S(1)}, f32[3,128]{1,0:T(4,128)}, u32[]{:S(2)}) copy-start(f32[3,128]{1,0:T(4,128)} %param.21) | copy-start | bytes 4612
  12.3 11.3 %copy-start.6 = (f32[4,10240]{1,0:T(4,128)S(1)}, f32[4,10240]{1,0:T(4,128)}, u32[]{:S(2)}) copy-start(f32[4,10240]{1,0:T(4,128)} %param.19) | copy-start | bytes 491524
  12.3 11.3 %copy-start.7 = (f32[10240]{0:T(1024)S(1)}, f32[10240]{0:T(1024)}, u32[]{:S(2)}) copy-start(f32[10240]{0:T(1024)} %param.20) | copy-start | bytes 122884
  14.8 42.9 %collective-permute-start.2 = (bf16[128,2304]{1,0:T(8,128)(2,1)}, bf16[128,2304]{1,0:T(8,128)(2,1)}, u32[]{:S(2)}, u32[]{:S(2)}) collective-permute-start(bf16[128,2304]{1,0:T(8,128)(2,1)} %get-tuple-element.63), channel_id=1, source_target_pairs={{0,3},{1,0},{2,1},{3,2},{4,7},{5,4},{6,5},{7,6},{8,11},{9,8},{10,9... | collective-permute-start | bytes 1769480 | tf_op jit(solution)/shard_map/ppermute | solution.py:834
  17.7 36.1 %collective-permute-start = (bf16[128,2304]{1,0:T(8,128)(2,1)}, bf16[128,2304]{1,0:T(8,128)(2,1)}, u32[]{:S(2)}, u32[]{:S(2)}) collective-permute-start(bf16[128,2304]{1,0:T(8,128)(2,1)} %get-tuple-element.64), channel_id=1, source_target_pairs={{0,1},{1,2},{2,3},{3,0},{4,5},{5,6},{6,7},{7,4},{8,9},{9,10},{10,1... | collective-permute-start | bytes 1769480 | tf_op jit(solution)/shard_map/ppermute | solution.py:834
  17.7 38.1 %collective-permute-start.1 = (bf16[128,2304]{1,0:T(8,128)(2,1)}, bf16[128,2304]{1,0:T(8,128)(2,1)}, u32[]{:S(2)}, u32[]{:S(2)}) collective-permute-start(bf16[128,2304]{1,0:T(8,128)(2,1)} %get-tuple-element.65), channel_id=1, source_target_pairs={{0,2},{1,3},{2,0},{3,1},{4,6},{5,7},{6,4},{7,5},{8,10},{9,11},{10,... | collective-permute-start | bytes 1769480 | tf_op jit(solution)/shard_map/ppermute | solution.py:834
  23.7 12.3 %copy-start.2 = (f32[8,10240]{1,0:T(8,128)}, f32[8,10240]{1,0:T(8,128)S(1)}, u32[]{:S(2)}) copy-start(f32[8,10240]{1,0:T(8,128)S(1)} %select_maximum_fusion.wb_c.wb_x.wb_b) | copy-start | bytes 983044
  43.8 8.4 %copy-start.1 = (bf16[16,4,8,2048]{3,2,0,1:T(8,128)(2,1)S(1)}, bf16[16,4,8,2048]{3,2,0,1:T(8,128)(2,1)}, u32[]{:S(2)}) copy-start(bf16[16,4,8,2048]{3,2,0,1:T(8,128)(2,1)} %copy-done) | copy-start | bytes 6291460
  43.8 80.3 %all-to-all-start.1 = ((bf16[4,256,2048]{2,1,0:T(8,128)(2,1)}), bf16[4,256,2048]{2,1,0:T(8,128)(2,1)}, u32[]{:S(2)}, u32[]{:S(2)}) async-start(bf16[4,256,2048]{2,1,0:T(8,128)(2,1)} %get-tuple-element.35), calls=%async_computation.1 | async-start | bytes 8388608 | tf_op jit(solution)/shard_map/all_to_all | solution.py:867
  59.7 18.2 %copy-start.5 = (f32[256,128]{1,0:T(8,128)S(1)}, f32[256,128]{1,0:T(8,128)}, u32[]{:S(2)}) copy-start(f32[256,128]{1,0:T(8,128)} %get-tuple-element.37.cum) | copy-start | bytes 393220
  76.7 47.4 %collective-permute-start.3 = (bf16[256,2048]{1,0:T(8,128)(2,1)}, bf16[256,2048]{1,0:T(8,128)(2,1)}, u32[]{:S(2)}, u32[]{:S(2)}) collective-permute-start(bf16[256,2048]{1,0:T(8,128)(2,1)} %get-tuple-element.34.refs_0_), channel_id=1, source_target_pairs={{0,4},{1,5},{2,6},{3,7},{4,0},{5,1},{6,2},{7,3},{8,12},{9,13},{10,... | collective-permute-start | bytes 3145736 | tf_op jit(solution)/shard_map/ppermute | solution.py:880
  124.1 4.2 %copy-start.4 = (bf16[8,128,128]{2,1,0:T(8,128)(2,1)S(1)}, bf16[8,128,128]{2,1,0:T(8,128)(2,1)}, u32[]{:S(2)}) copy-start(bf16[8,128,128]{2,1,0:T(8,128)(2,1)} %slice.45) | copy-start | bytes 786436
  128.3 46.6 %collective-permute-start.4 = (bf16[256,2048]{1,0:T(8,128)(2,1)}, bf16[256,2048]{1,0:T(8,128)(2,1)}, u32[]{:S(2)}, u32[]{:S(2)}) collective-permute-start(bf16[256,2048]{1,0:T(8,128)(2,1)} %add_states.2.refs_2_.refs_0_), channel_id=1, source_target_pairs={{0,4},{1,5},{2,6},{3,7},{4,0},{5,1},{6,2},{7,3},{8,12},{9,13},{10,... | collective-permute-start | bytes 3145736 | tf_op jit(solution)/shard_map/ppermute | solution.py:880
  133.2 74.3 %all-to-all-start.2 = ((bf16[4,256,2048]{2,1,0:T(8,128)(2,1)}), bf16[4,256,2048]{2,1,0:T(8,128)(2,1)}, u32[]{:S(2)}, u32[]{:S(2)}) async-start(bf16[4,256,2048]{2,1,0:T(8,128)(2,1)} %add_states.3.earlier_out), calls=%async_computation.2 | async-start | bytes 8388608 | tf_op jit(solution)/shard_map/all_to_all | solution.py:890
